TPU v7x, 128 devices: a whole 4x4x4 slice. The times are simulated.
128 devices in a mesh: space: 32 (over z, x, core), segment: 4 (over y).
Axes of the slice: x: 4, y: 4, z: 4, core: 2. Of those that a mesh axis runs over, the one named last changes fastest.
Arguments:
- features: bfloat16 [4, 32768, 128], P('segment', 'space'), may hold values from -6 to 6
- weights: bfloat16 [4, 27, 128, 128], P('segment'), may hold values from -0.109375 to 0.109375
- cotangent: bfloat16 [4, 32768, 128], P('segment', 'space'), may hold values from -6 to 6
- local_map: int32 [32768, 27], P('space'), may hold values from 0 to 1024, as said below
- send_map: int32 [36864, 27], P('space'), may hold values from 0 to 1024, as said below
- recv_map: int32 [36864], P('space'), may hold values from 0 to 1024, as said below
Outputs:
- mixed: bfloat16 [4, 32768, 128], P('segment', 'space')
- input_grad: bfloat16 [4, 32768, 128], P('segment', 'space')
- weight_grad: float32 [4, 27, 128, 128], P('segment')
Inputs may be any that keep to these rules, and one draw needn't show every extreme that they name: Each tile is a block of 8 x 8 x 32 cells of a grid of 4 x 8 tiles, of which exactly 1024 cells are occupied. local_map[p, v, k] is the row of the occupied cell at offset (k // 9 - 1, (k // 3) % 3 - 1, k % 3 - 1) from voxel v inside the same tile, else 1024; offset 13 is the voxel itself, and local_map[p, v, k] = u < 1024 exactly when local_map[p, u, 26 - k] = v. For tile p and direction d, the slots list the cells of the neighbouring tile p + delta(d) that touch tile p (a face of 256 cells, or a vertical edge of 32 cells for a diagonal direction); send_map[p, d, c, k] is the row in tile p of the occupied cell at offset k from slot c's cell, else 1024. A direction without a neighbouring tile has only 1024. recv_map[q, d, c] is the row in tile q of the cell of slot c of the list that tile q - delta(d) holds for direction d, or 1024 where that cell is empty or that tile does not exist.
All inputs are finite; a program needn't handle non-finite values.
Results may differ from a plain program's by a relative error of at most 0.0051.
Values may be sent and summed in bfloat16 or wider, within the bound.
No kernel may reach another device: no remote copies, remote signals or barrier semaphores. Data moves between devices by JAX's collectives and lax.ppermute only.
A program may use at most 64 MiB of HBM per device.

v0:
```python
import functools

import jax
import jax.numpy as jnp
from jax import lax
from jax.experimental import pallas as pl
from jax.experimental.pallas import tpu as pltpu
from jax.sharding import PartitionSpec as P

TZ = 32
TILES_X = 4
CAP = 256
ROWS = 1024
C = 128
HALO = 1152

DIRECTIONS = ((-1, -1), (-1, 0), (-1, 1), (0, -1), (0, 1), (1, -1), (1, 0), (1, 1))
BF = jnp.bfloat16
F32 = jnp.float32


def spans():
    result = []
    start = 0
    for step_x, step_y in DIRECTIONS:
        length = TZ if step_x != 0 and step_y != 0 else CAP
        result.append((start, length))
        start = start + length
    return result


SPANS = spans()
FACES = [n for n, (a, b) in enumerate(DIRECTIONS) if a == 0 or b == 0]
CORNERS = [n for n, (a, b) in enumerate(DIRECTIONS) if a != 0 and b != 0]


def toward(step_x, step_y):
    picked = []
    for offset in range(27):
        along_x = offset // 9 - 1
        along_y = offset // 3 % 3 - 1
        if (step_x == 0 or along_x == -step_x) and (step_y == 0 or along_y == -step_y):
            picked.append(offset)
    return picked


def dot(a, b, dims=((1,), (0,))):
    return lax.dot_general(a, b, (dims, ((), ())), preferred_element_type=F32)


def hot(row, rows):
    pos = lax.broadcasted_iota(jnp.int32, (256, 128), 0).astype(jnp.int16)
    count = row.shape[1]
    blocks = []
    for base in range(0, rows, 256):
        rel = (row - base).astype(jnp.int16)
        parts = [
            jnp.where(rel[:, t : t + 128] == pos, BF(1), BF(0)) for t in range(0, count, 128)
        ]
        blocks.append(jnp.concatenate(parts, 1))
    return jnp.concatenate(blocks, 0)


def spread(column, count):
    kept = jnp.where(column == ROWS, -1, column)
    return jnp.broadcast_to(kept, (column.shape[0], count)).astype(jnp.int16)


def places_from_one(rows):
    return (lax.broadcasted_iota(jnp.int32, (rows, 128), 0) + 1).astype(BF)


def positions(column, row):
    rows, count = column.shape
    numbers = places_from_one(rows)
    numbers = jnp.concatenate([numbers] * (count // 128), 1)
    found = jnp.where(column == row.astype(jnp.int16), numbers, BF(0))
    while rows > 16:
        rows //= 2
        found = jnp.maximum(found[:rows], found[rows:])
    return jnp.max(found.astype(F32), axis=0, keepdims=True)


def match(row, rows):
    numbers = places_from_one(rows)
    row = row.astype(BF)
    parts = [jnp.where(row[:, t : t + 128] == numbers, BF(1), BF(0)) for t in range(0, row.shape[1], 128)]
    return jnp.concatenate(parts, 1)


def face_rows(block):
    block = block.astype(F32)
    return [jnp.concatenate([block[k : k + 1], block[16 + k : 17 + k]], 1) for k in range(9)]


def column_of(row):
    return jnp.broadcast_to(row.astype(F32), (8, row.shape[1])).T[:, :1].astype(jnp.int32)


def inside(place, axis, dims):
    return (lax.broadcasted_iota(jnp.int32, dims, axis) // TZ) == place


def number_of(step_x, step_y):
    return DIRECTIONS.index((step_x, step_y))


def pack_sides(lists, orient, sides, xa_ref, xb_ref, ya_ref, yb_ref):
    x_odd, y_odd = sides[0] == 1, sides[1] == 1

    def x_side(side):
        picked = [(orient * side, 0), (orient * side, -orient), (orient * side, orient)]
        return jnp.concatenate([lists[number_of(*d)] for d in picked], 0)

    plus, minus = x_side(1), x_side(-1)
    xa_ref[...] = jnp.where(x_odd, minus, plus)
    xb_ref[...] = jnp.where(x_odd, plus, minus)
    plus, minus = lists[number_of(0, orient)], lists[number_of(0, -orient)]
    ya_ref[...] = jnp.where(y_odd, minus, plus)
    yb_ref[...] = jnp.where(y_odd, plus, minus)


def unpack_sides(orient, sides, face, edge, xa, xb, ya, yb):
    x_odd, y_odd = sides[0] == 1, sides[1] == 1

    def of_side(side, odd, a, b):
        return jnp.where(odd, b, a) if side == 1 else jnp.where(odd, a, b)

    lists = []
    for step_x, step_y in DIRECTIONS:
        if step_y == 0:
            lists.append(of_side(-orient * step_x, x_odd, xa[:face], xb[:face]))
        elif step_x == 0:
            lists.append(of_side(-orient * step_y, y_odd, ya[:face], yb[:face]))
        else:
            first = of_side(-orient * step_y, y_odd, ya[face : face + edge], yb[face : face + edge])
            second = of_side(-orient * step_y, y_odd, ya[face + edge :], yb[face + edge :])
            lists.append(of_side(-orient * step_x, x_odd, first, second))
    return lists


def start_kernel(side_ref, x_ref, rr_ref, sm_ref, xa_ref, xb_ref, ya_ref, yb_ref, face_p_ref, edge_p_ref):
    lists = [None] * 8
    row = rr_ref[...]
    column = column_of(row)
    listed = dot(x_ref[...].astype(F32).T.astype(BF), hot(row, ROWS)).T.astype(BF)
    for place, number in enumerate(FACES):
        start, length = SPANS[number]
        other, _ = SPANS[7 - number]
        wide = spread(column[other : other + length], length)
        found = [
            positions(wide, sm_ref[offset : offset + 1, start : start + length])
            for offset in toward(*DIRECTIONS[number])
        ]
        found = jnp.concatenate(found + [jnp.zeros((7, length), F32)], 0)
        found = jnp.concatenate([found[:, :128], found[:, 128:]], 0).astype(BF)
        face_p_ref[place] = found
        lists[number] = jnp.concatenate([listed[other : other + length], found], 0)
    wide = spread(
        jnp.concatenate([column[SPANS[7 - n][0] : SPANS[7 - n][0] + TZ] for n in CORNERS], 0), 4 * TZ
    )
    found = []
    for step in range(3):
        pieces = []
        for number in CORNERS:
            start, length = SPANS[number]
            offset = toward(*DIRECTIONS[number])[step]
            pieces.append(sm_ref[offset : offset + 1, start : start + length])
        found.append(positions(wide, jnp.concatenate(pieces, 1)))
    found = jnp.concatenate(found + [jnp.zeros((13, 4 * TZ), F32)], 0).astype(BF)
    edge_p_ref[...] = found
    for number in CORNERS:
        other, length = SPANS[7 - number]
        lists[number] = jnp.concatenate([listed[other : other + length], found], 0)
    pack_sides(lists, 1, (side_ref[0], side_ref[1]), xa_ref, xb_ref, ya_ref, yb_ref)


def forward_kernel(x_ref, lm_ref, w_ref, *refs, width, first):
    g_ref, sum_ref = refs[-2:]
    source = x_ref[...].astype(F32).T.astype(BF)
    offsets = range(first, first + 13)
    weight = jnp.concatenate([w_ref[k] for k in offsets], 0)
    for begin in range(0, ROWS, width):
        cols = slice(begin, begin + width)
        gathered = [dot(source, hot(lm_ref[k : k + 1, cols], ROWS)).astype(BF) for k in offsets]
        gathered = jnp.concatenate(gathered, 0)
        g_ref[:, cols] = gathered
        part = dot(weight, gathered, ((0,), (0,)))
        if first == 0:
            sum_ref[:, cols] = part + dot(w_ref[13], source[:, cols], ((0,), (0,)))
        else:
            sum_ref[cols, :] = (part + refs[0][:, cols]).T


def high_low(values):
    high = values.astype(BF)
    return jnp.concatenate([high, (values - high.astype(F32)).astype(BF)], 1)


def activate_kernel(
    side_ref, pre_ref, ixa_ref, ixb_ref, iya_ref, iyb_ref, rr_ref, cot_ref, pair_ref, w_ref,
    act_ref, grad_ref, xa_ref, xb_ref, ya_ref, yb_ref, dw_ref,
):
    sides = (side_ref[0], side_ref[1])
    arrived = unpack_sides(
        1, sides, CAP + 32, TZ + 16, ixa_ref[...], ixb_ref[...], iya_ref[...], iyb_ref[...]
    )
    sums = [None] * 8
    sources = []
    for number in FACES:
        picked = toward(*DIRECTIONS[number])
        source = arrived[number][:CAP].astype(F32).T.astype(BF)
        sources.append(source)
        gathered = [dot(source, match(row, CAP)).astype(BF) for row in face_rows(arrived[number][CAP:])]
        weight = jnp.concatenate([w_ref[offset] for offset in picked], 0)
        sums[number] = dot(weight, jnp.concatenate(gathered, 0), ((0,), (0,))).T
    edge_source = jnp.concatenate([arrived[n][:TZ] for n in CORNERS], 0).astype(F32).T.astype(BF)
    edge_found = jnp.zeros((16, 4 * TZ), F32)
    for place, number in enumerate(CORNERS):
        rows = arrived[number][TZ:].astype(F32)
        edge_found = jnp.where(inside(place, 1, rows.shape), rows, edge_found)
    gathered = [dot(edge_source, match(edge_found[k : k + 1], 4 * TZ)).astype(BF) for k in range(3)]
    masked = []
    weights = []
    for place, number in enumerate(CORNERS):
        for step in range(3):
            masked.append(jnp.where(inside(place, 1, (C, 4 * TZ)), gathered[step], BF(0)))
            weights.append(w_ref[toward(*DIRECTIONS[number])[step]])
    total = dot(jnp.concatenate(weights, 0), jnp.concatenate(masked, 0), ((0,), (0,))).T
    for place, number in enumerate(CORNERS):
        sums[number] = total[place * TZ : (place + 1) * TZ]

    selector = hot(rr_ref[...], ROWS)
    both = dot(selector, high_low(jnp.concatenate(sums, 0)))
    pre = pre_ref[...] + both[:, :C] + both[:, C:]
    gate = 1.0 / (1.0 + jnp.exp(-pre))
    act_ref[...] = (pre * gate).astype(BF)
    upstream = cot_ref[...].astype(F32) + pair_ref[...].astype(F32)
    grad = upstream * gate * (1.0 + pre * (1.0 - gate))
    grad_ref[...] = grad.astype(BF)
    listed = dot(grad.T.astype(BF), selector).T.astype(BF)
    lists = [listed[start : start + length] for start, length in SPANS]
    pack_sides(lists, -1, sides, xa_ref, xb_ref, ya_ref, yb_ref)

    dw_ref[...] = jnp.zeros_like(dw_ref)
    for source, number in zip(sources, FACES):
        pieces = [
            dot(match(row, CAP), lists[number]).astype(BF) for row in face_rows(arrived[number][CAP:])
        ]
        part = dot(source, jnp.concatenate(pieces, 1))
        for index, offset in enumerate(toward(*DIRECTIONS[number])):
            dw_ref[offset] += part[:, index * C : (index + 1) * C]
    back = jnp.concatenate([lists[n] for n in CORNERS], 0)
    spots = [dot(match(edge_found[k : k + 1], 4 * TZ), back).astype(BF) for k in range(3)]
    pieces = [
        jnp.where(inside(place, 0, (4 * TZ, C)), spots[step], BF(0)) for place in range(4) for step in range(3)
    ]
    part = dot(edge_source, jnp.concatenate(pieces, 1))
    for place, number in enumerate(CORNERS):
        for step in range(3):
            index = 3 * place + step
            dw_ref[toward(*DIRECTIONS[number])[step]] += part[:, index * C : (index + 1) * C]


def weight_first_kernel(g_ref, grad_ref, x_ref, halo_ref, dw_ref):
    grad = grad_ref[...]
    dw_ref[: 13 * C, :] = dot(g_ref[...], grad) + halo_ref[:13].reshape(13 * C, C)
    dw_ref[13 * C :, :] = dot(x_ref[...], grad, ((0,), (0,))) + halo_ref[13]


def weight_second_kernel(side_ref, g_ref, grad_ref, first_ref, halo_ref, kept_ref, sent_ref, total):
    total[: 14 * C, :] = first_ref[...]
    total[14 * C :, :] = dot(g_ref[...], grad_ref[...]) + halo_ref[14:].reshape(13 * C, C)
    half = kept_ref.shape[0]
    kept_ref[...] = total[pl.ds(pl.multiple_of(side_ref[2] * half, 8), half), :]
    sent_ref[...] = total[pl.ds(pl.multiple_of((1 - side_ref[2]) * half, 8), half), :].astype(BF)


def return_kernel(side_ref, ixa_ref, ixb_ref, iya_ref, iyb_ref, face_p_ref, edge_p_ref, w_ref, placed_ref):
    sides = (side_ref[0], side_ref[1])
    returned = unpack_sides(-1, sides, CAP, TZ, ixa_ref[...], ixb_ref[...], iya_ref[...], iyb_ref[...])
    for place, number in enumerate(FACES):
        other, length = SPANS[7 - number]
        pieces = [dot(match(row, CAP), returned[number]).astype(BF) for row in face_rows(face_p_ref[place])]
        weight = jnp.concatenate([w_ref[offset] for offset in toward(*DIRECTIONS[number])], 1)
        placed_ref[other : other + length, :] = dot(jnp.concatenate(pieces, 1), weight, ((1,), (1,)))
    back = jnp.concatenate([returned[n] for n in CORNERS], 0)
    found = edge_p_ref[...].astype(F32)
    spots = [dot(match(found[k : k + 1], 4 * TZ), back).astype(BF) for k in range(3)]
    pieces = []
    weights = []
    for place, number in enumerate(CORNERS):
        for step in range(3):
            pieces.append(jnp.where(inside(place, 0, (4 * TZ, C)), spots[step], BF(0)))
            weights.append(w_ref[toward(*DIRECTIONS[number])[step]])
    result = dot(jnp.concatenate(pieces, 1), jnp.concatenate(weights, 1), ((1,), (1,)))
    for place, number in enumerate(CORNERS):
        other, length = SPANS[7 - number]
        placed_ref[other : other + length, :] = result[place * TZ : (place + 1) * TZ, :]


def backward_kernel(grad_ref, lm_ref, w_ref, out_ref, *, begin):
    size = out_ref.shape[0]
    source = grad_ref[...].astype(F32).T.astype(BF)
    gathered = []
    for k in range(27):
        if k == 13:
            gathered.append(source[:, begin : begin + size])
        else:
            gathered.append(dot(source, hot(lm_ref[26 - k : 27 - k, begin : begin + size], ROWS)).astype(BF))
    weight = jnp.concatenate([w_ref[k] for k in range(27)], 1)
    out_ref[...] = dot(weight, jnp.concatenate(gathered, 0)).T


def final_kernel(*refs):
    placed_ref, rr_ref, act_ref, pair_ref, mixed_ref, out_ref = refs[-6:]
    both = dot(hot(rr_ref[...], ROWS), high_low(placed_ref[...]))
    both = both[:, :C] + both[:, C:]
    size = ROWS // len(refs[:-6])
    for index, ref in enumerate(refs[:-6]):
        rows = slice(index * size, (index + 1) * size)
        out_ref[rows, :] = (ref[...] + both[rows]).astype(BF)
    mixed_ref[...] = (act_ref[...].astype(F32) + pair_ref[...].astype(F32)).astype(BF)


def assemble_kernel(bits_ref, own_ref, one_ref, two_ref, four_ref, out_ref):
    place = bits_ref[0] * 4 + bits_ref[1] * 2 + bits_ref[2]
    blocks = [own_ref[...], one_ref[...]] + [two_ref[i] for i in range(2)] + [four_ref[i] for i in range(4)]
    for distance, block in enumerate(blocks):
        out_ref[place ^ distance] = block.astype(F32)


PARAMS = pltpu.CompilerParams(vmem_limit_bytes=30 * 2**20)


def shape(dims, dtype):
    return jax.ShapeDtypeStruct(dims, dtype)


def whole(dims):
    return pl.BlockSpec(dims, lambda *ids: (0,) * len(dims))


def pairing(axis, which):
    pairs = []
    for tile in range(lax.axis_size("space")):
        at_x, at_y = tile % TILES_X, tile // TILES_X
        tiles_y = lax.axis_size("space") // TILES_X
        if axis == "x":
            move = 1 if (at_x + which) % 2 == 0 else -1
            at_x = (at_x + move) % TILES_X
        else:
            move = 1 if (at_y + which) % 2 == 0 else -1
            at_y = (at_y + move) % tiles_y
        pairs.append((tile, at_y * TILES_X + at_x))
    return pairs


def exchange_x(xa, xb):
    return [lax.ppermute(v, "space", pairing("x", n)) for n, v in enumerate((xa, xb))]


def second_phase(ya, yb, xa, xb, sides, face, edge):
    sent = []
    for which, own in enumerate((ya, yb)):
        down = sides[1] != which
        corners = [jnp.where(down, v[face : face + edge], v[face + edge :]) for v in (xa, xb)]
        sent.append(jnp.concatenate([own] + corners, 0))
    return sent


def exchange_y(sent):
    return [lax.ppermute(v, "space", pairing("y", n)) for n, v in enumerate(sent)]


def swapped(array):
    return lax.ppermute(array, "segment", [(i, i ^ 1) for i in range(lax.axis_size("segment"))])


def xor_send(value, bits):
    return lax.ppermute(value, "space", [(i, i ^ bits) for i in range(lax.axis_size("space"))])


def pick(array, index):
    return lax.dynamic_index_in_dim(array, index, 0, False)


def cost(flops, data):
    return pl.CostEstimate(flops=int(flops), bytes_accessed=int(data), transcendentals=0)


def tie(value, other):
    return lax.optimization_barrier((value, other))[0]


def on_device(features, weights, cotangent, local_map, send_map, recv_map):
    x = features[0]
    w = weights[0]
    cot = cotangent[0]
    lm = local_map.T
    sm = send_map.T
    rr = recv_map.reshape(1, HALO)
    me = lax.axis_index("space")
    sides = jnp.stack([me % 2, me // TILES_X % 2, me % 2]).astype(jnp.int32)
    smem = pl.BlockSpec(memory_space=pltpu.SMEM)
    vmem = pl.BlockSpec(memory_space=pltpu.VMEM)
    def lists_shape(face, edge):
        return [shape((face + 2 * edge, C), BF)] * 2 + [shape((face, C), BF)] * 2

    xa, xb, ya, yb, face_p, edge_p = pl.pallas_call(
        start_kernel,
        in_specs=[smem] + [vmem] * 3,
        out_shape=lists_shape(CAP + 32, TZ + 16) + [shape((4, 32, C), BF), shape((16, C), BF)],
        compiler_params=PARAMS,
        cost_estimate=cost(2e9, 4e6),
        name="start",
    )(sides, x, rr, sm)
    cot_pair = swapped(cot)
    in_x = exchange_x(xa, xb)

    def forward(first, dims, x, *before):
        return pl.pallas_call(
            functools.partial(forward_kernel, width=512, first=first),
            out_shape=[shape((13 * C, ROWS), BF), shape(dims, F32)],
            compiler_params=PARAMS,
            cost_estimate=cost(7e9, 5e6),
            name="forward",
        )(x, lm, w, *before)

    g0, pre = forward(0, (C, ROWS), x)
    in_x = [tie(v, pre) for v in in_x]
    sent = second_phase(ya, yb, *in_x, sides, CAP + 32, TZ + 16)
    in_y = exchange_y(sent)
    g1, pre = forward(14, (ROWS, C), tie(x, sent[0]), pre)
    in_y = [tie(v, pre) for v in in_y]
    act, grad, xa, xb, ya, yb, dw_halo = pl.pallas_call(
        activate_kernel,
        in_specs=[smem] + [vmem] * 9,
        out_shape=[shape((ROWS, C), BF)] * 2 + lists_shape(CAP, TZ) + [shape((27, C, C), F32)],
        compiler_params=PARAMS,
        cost_estimate=cost(4e9, 3e6),
        name="activate",
    )(sides, pre, *in_x, *in_y, rr, cot, cot_pair, w)
    half = 27 * C // 2
    in_x = exchange_x(xa, xb)
    first = pl.pallas_call(
        weight_first_kernel,
        out_shape=shape((14 * C, C), F32),
        compiler_params=PARAMS,
        cost_estimate=cost(4e9, 5e6),
        name="weight_first",
    )(g0, grad, x, dw_halo)
    sent = second_phase(*[tie(v, first) for v in (ya, yb, *in_x)], sides, CAP, TZ)
    in_y = exchange_y(sent)
    kept, sent = pl.pallas_call(
        weight_second_kernel,
        in_specs=[smem] + [vmem] * 4,
        out_shape=[shape((half, C), F32), shape((half, C), BF)],
        scratch_shapes=[pltpu.VMEM((27 * C, C), F32)],
        compiler_params=PARAMS,
        cost_estimate=cost(4e9, 5e6),
        name="weight_second",
    )(sides, g1, tie(grad, tuple(sent)), first, dw_halo)

    size = ROWS // 4

    def backward(index, grad):
        return pl.pallas_call(
            functools.partial(backward_kernel, begin=index * size),
            out_shape=shape((size, C), F32),
            compiler_params=PARAMS,
            cost_estimate=cost(3e9, 2e6),
            name="backward",
        )(grad, lm, w)

    bits = [me % 2, (me // 2 + me // 4) % 2, (me // 8 + me // 16) % 2]

    def halve(blocks, stage):
        return pick(blocks, bits[stage]), pick(blocks, 1 - bits[stage]).astype(BF)

    def plus(one, two):
        return one.astype(F32) + two.astype(F32)

    locals_ = []
    got = xor_send(sent, 1)
    kept, sent = halve(plus(kept, got).reshape(2, 2, -1, C), 1)
    got = xor_send(sent, 2)
    locals_.append(backward(0, tie(grad, sent)))
    placed = pl.pallas_call(
        return_kernel,
        in_specs=[smem] + [vmem] * 7,
        out_shape=shape((HALO, C), F32),
        compiler_params=PARAMS,
        cost_estimate=cost(3e9, 4e6),
        name="returning",
    )(sides, *in_x, *in_y, face_p, edge_p, tie(w, locals_[0]))
    kept, sent = halve(plus(kept, tie(got, placed)), 2)
    got = xor_send(sent, 8)
    locals_.append(backward(1, tie(grad, sent)))
    own = plus(kept, tie(got, locals_[1])).astype(BF)
    got = xor_send(own, 6)
    act_pair = swapped(tie(act, own))
    locals_.append(backward(2, tie(grad, own)))
    own = plus(own, tie(got, locals_[2])).astype(BF)
    got = xor_send(own, 24)
    locals_.append(backward(3, tie(grad, own)))
    own = plus(own, tie(got, locals_[3])).astype(BF)
    one = xor_send(own, 8)
    mixed, input_grad = pl.pallas_call(
        final_kernel,
        out_shape=[shape((ROWS, C), BF), shape((ROWS, C), BF)],
        compiler_params=PARAMS,
        cost_estimate=cost(1e9, 3e6),
        name="final",
    )(*locals_, tie(placed, own), rr, act, act_pair)
    one = tie(one, input_grad)
    two = xor_send(jnp.stack([own, one]), 2)
    four = xor_send(jnp.concatenate([jnp.stack([own, one]), two], 0), 1)
    weight_grad = pl.pallas_call(
        assemble_kernel,
        in_specs=[smem] + [vmem] * 4,
        out_shape=shape((8,) + own.shape, F32),
        compiler_params=PARAMS,
        cost_estimate=cost(1e6, 3e6),
        name="assemble",
    )(jnp.stack(bits).astype(jnp.int32), own, one, two, four)
    return (mixed[None], input_grad[None], weight_grad.reshape(w.shape)[None])


def solution(mesh):
    in_specs = (
        P("segment", "space", None),
        P("segment", None, None, None),
        P("segment", "space", None),
        P("space", None),
        P("space", None),
        P("space"),
    )
    out_specs = (
        P("segment", "space", None),
        P("segment", "space", None),
        P("segment", None, None, None),
    )
    return jax.shard_map(
        on_device, mesh=mesh, in_specs=in_specs, out_specs=out_specs, check_vma=False
    )
```

profile of v0, /device:TPU:1, one launch (start us, length us, event | category | flops | bytes accessed | tf_op | source)
XLA Modules:
  0.0 89.5 jit_solution(537158241529326728)
XLA Ops:
  0.6 2.2 %collective-permute-start.4 = (bf16[1024,128]{1,0:T(8,128)(2,1)}, bf16[1024,128]{1,0:T(8,128)(2,1)S(1)}, u32[]{:S(2)}, u32[]{:S(2)}) collective-permute-start(bf16[1024,128]{1,0:T(8,128)(2,1)} %bitcast.37), channel_id=1, source_target_pairs={{0,1},{1,0},{2,3},{3,2},{4,5},{5,4},{6,7},{7,6},{8,9},{9,8},{10,11... | collective-permute-start | bytes 786440 | tf_op jit(solution)/shard_map/ppermute | solution.py:377
  2.8 0.7 reshape.14.rr_ref.refs_5_
  3.5 0.1 pad_add_fusion.side_ref
  3.6 0.9 %copy-done.2 = bf16[1,1024,128]{2,1,0:T(8,128)(2,1)S(1)} copy-done((bf16[1,1024,128]{2,1,0:T(8,128)(2,1)S(1)}, bf16[1,1024,128]{2,1,0:T(8,128)(2,1)}, u32[]{:S(2)}) %copy-start.2) | copy-done | bytes 262168
  4.6 0.9 %copy-done.4 = s32[1152,27]{0,1:T(8,128)S(1)} copy-done((s32[1152,27]{0,1:T(8,128)S(1)}, s32[1152,27]{0,1:T(8,128)}, u32[]{:S(2)}) %copy-start.4) | copy-done | bytes 124440
  5.5 2.3 %start.1 = (bf16[384,128]{1,0:T(8,128)(2,1)S(1)}, bf16[384,128]{1,0:T(8,128)(2,1)S(1)}, bf16[288,128]{1,0:T(8,128)(2,1)S(1)}, bf16[288,128]{1,0:T(8,128)(2,1)S(1...) custom-call(s32[3]{0:T(128)S(1)} %pad_add_fusion.side_ref, bf16[1024,128]{1,0:T(8,128)(2,1)S(1)} %bitcast.39, ...), custom_call_target="tpu_custom_call" | custom-call | flops 2000000000 | bytes 4000000 | tf_op jit(solution)/shard_map/start/pallas_call | solution.py:410
  7.8 1.0 %collective-permute-start = (bf16[384,128]{1,0:T(8,128)(2,1)S(1)}, bf16[384,128]{1,0:T(8,128)(2,1)S(1)}, u32[]{:S(2)}, u32[]{:S(2)}) collective-permute-start(bf16[384,128]{1,0:T(8,128)(2,1)S(1)} %get-tuple-element.47), channel_id=1, source_target_pairs={{0,4},{4,0},{8,12},{12,8},{16,20},{20,16},{24,28},{28,24},{32,36},... | collective-permute-start | bytes 294920 | tf_op jit(solution)/shard_map/ppermute | solution.py:360
  8.8 1.2 %collective-permute-start.1 = (bf16[384,128]{1,0:T(8,128)(2,1)S(1)}, bf16[384,128]{1,0:T(8,128)(2,1)S(1)}, u32[]{:S(2)}, u32[]{:S(2)}) collective-permute-start(bf16[384,128]{1,0:T(8,128)(2,1)S(1)} %get-tuple-element.50), channel_id=1, source_target_pairs={{0,12},{4,8},{8,4},{12,0},{16,28},{20,24},{24,20},{28,16},{32,44},... | collective-permute-start | bytes 294920 | tf_op jit(solution)/shard_map/ppermute | solution.py:360
  10.0 0.0 copy-done
  10.0 0.0 copy-done.5
  10.0 4.3 %forward.2 = (bf16[1664,1024]{1,0:T(8,128)(2,1)S(1)}, f32[128,1024]{1,0:T(8,128)S(1)}) custom-call(bf16[1024,128]{1,0:T(8,128)(2,1)S(1)} %bitcast.40, s32[27,1024]{1,0:T(8,128)S(1)} %bitcast.44, bf16[27,128,128]{2,1,0:T(8,128)(2,1)S(1)} %bitcast.29), custom_call_target="tpu_custom_call" | custom-call | flops 7000000000 | bytes 5000000 | tf_op jit(solution)/shard_map/forward/pallas_call | solution.py:422
  14.3 0.0 copy-start.6
  14.4 1.7 %copy-done.6 = bf16[1664,1024]{1,0:T(8,128)(2,1)} copy-done((bf16[1664,1024]{1,0:T(8,128)(2,1)}, bf16[1664,1024]{1,0:T(8,128)(2,1)S(1)}, u32[]{:S(2)}) %copy-start.6) | copy-done | bytes 3407896
  16.1 0.0 collective-permute-done.1.ixb_ref
  16.1 0.0 collective-permute-done.ixa_ref
  16.1 2.5 %collective-permute-start.2 = (bf16[384,128]{1,0:T(8,128)(2,1)S(1)}, bf16[384,128]{1,0:T(8,128)(2,1)S(1)}, u32[]{:S(2)}, u32[]{:S(2)}) collective-permute-start(bf16[384,128]{1,0:T(8,128)(2,1)S(1)} %pad_maximum_fusion.2), channel_id=1, source_target_pairs={{0,16},{4,20},{8,24},{12,28},{16,0},{20,4},{24,8},{28,12},{32,48},... | collective-permute-start | bytes 294920 | tf_op jit(solution)/shard_map/ppermute | solution.py:373
  18.6 4.3 %collective-permute-start.3 = (bf16[384,128]{1,0:T(8,128)(2,1)S(1)}, bf16[384,128]{1,0:T(8,128)(2,1)S(1)}, u32[]{:S(2)}, u32[]{:S(2)}) collective-permute-start(bf16[384,128]{1,0:T(8,128)(2,1)S(1)} %pad_maximum_fusion.3), channel_id=1, source_target_pairs={{0,112},{4,116},{8,120},{12,124},{16,32},{20,36},{24,40},{28,44},{... | collective-permute-start | bytes 294920 | tf_op jit(solution)/shard_map/ppermute | solution.py:373
  22.9 0.0 copy-done.3
  22.9 4.4 %forward.3 = (bf16[1664,1024]{1,0:T(8,128)(2,1)S(1)}, f32[1024,128]{1,0:T(8,128)S(1)}) custom-call(bf16[1024,128]{1,0:T(8,128)(2,1)S(1)} %bitcast.41, s32[27,1024]{1,0:T(8,128)S(1)} %bitcast.45, bf16[27,128,128]{2,1,0:T(8,128)(2,1)S(1)} %bitcast.30, f32[128,1024]{1,0:T(8,128)S(1)} %get-tuple-element.48.refs_0_), custom_call_target="tpu_custom_call" | custom-call | flops 7000000000 | bytes 5000000 | tf_op jit(solution)/shard_map/forward/pallas_call | solution.py:422
  27.3 0.0 collective-permute-done.3.iyb_ref
  27.3 0.0 collective-permute-done.2.iya_ref
  27.3 0.0 collective-permute-done.4.pair_ref
  27.3 0.0 copy-done.1
  27.3 6.8 %activate.1 = (bf16[1024,128]{1,0:T(8,128)(2,1)S(1)}, bf16[1024,128]{1,0:T(8,128)(2,1)S(1)}, bf16[320,128]{1,0:T(8,128)(2,1)S(1)}, bf16[320,128]{1,0:T(8,128)(2,...) custom-call(s32[3]{0:T(128)S(1)} %pad_add_fusion.side_ref, ...), custom_call_target="tpu_custom_call" | custom-call | flops 4000000000 | bytes 3000000 | tf_op jit(solution)/shard_map/activate/pallas_call | solution.py:436
  34.1 1.2 %collective-permute-start.5 = (bf16[320,128]{1,0:T(8,128)(2,1)S(1)}, bf16[320,128]{1,0:T(8,128)(2,1)S(1)}, u32[]{:S(2)}, u32[]{:S(2)}) collective-permute-start(bf16[320,128]{1,0:T(8,128)(2,1)S(1)} %get-tuple-element.63), channel_id=1, source_target_pairs={{0,4},{4,0},{8,12},{12,8},{16,20},{20,16},{24,28},{28,24},{32,36},... | collective-permute-start | bytes 245768 | tf_op jit(solution)/shard_map/ppermute | solution.py:360
  35.3 0.0 copy-done.7
  35.3 1.1 %weight_first.1.first_ref = f32[1792,128]{1,0:T(8,128)S(1)} custom-call(bf16[1664,1024]{1,0:T(8,128)(2,1)S(1)} %copy-done.7, bf16[1024,128]{1,0:T(8,128)(2,1)S(1)} %get-tuple-element.81.grad_ref, bf16[1024,128]{1,0:T(8,128)(2,1)S(1)} %bitcast.42, f32[27,128,128]{2,1,0:T(8,128)S(1)} %get-tuple-element.61.halo_ref), custom_call_target="tpu_custom_call" | custom-call | flops 4000000000 | bytes 5000000 | tf_op jit(solution)/shard_map/weight_first/pallas_call | solution.py:446
  36.5 0.2 collective-permute-start.6
  36.7 0.0 collective-permute-done.5.ixa_ref
  36.7 3.9 %collective-permute-done.6.ixb_ref = bf16[320,128]{1,0:T(8,128)(2,1)S(1)} collective-permute-done((bf16[320,128]{1,0:T(8,128)(2,1)S(1)}, bf16[320,128]{1,0:T(8,128)(2,1)S(1)}, u32[]{:S(2)}, u32[]{:S(2)}) %collective-permute-start.6) | collective-permute-done | bytes 81952 | tf_op jit(solution)/shard_map/ppermute | solution.py:360
  40.6 0.6 pad_maximum_fusion.5
  41.3 0.6 pad_maximum_fusion.4
  41.9 1.7 %weight_second.1 = (f32[1728,128]{1,0:T(8,128)S(1)}, bf16[1728,128]{1,0:T(8,128)(2,1)S(1)}) custom-call(s32[3]{0:T(128)S(1)} %pad_add_fusion.side_ref, bf16[1664,1024]{1,0:T(8,128)(2,1)S(1)} %get-tuple-element.58.g_ref, bf16[1024,128]{1,0:T(8,128)(2,1)S(1)} %get-tuple-element.81.grad_ref, f32[1792,128]{1,0:T(8,128)S(1)} %weight_first.1.first_ref, ...), custom_call_target="tpu_custom_call" | custom-call | flops 4000000000 | bytes 5000000 | tf_op jit(solution)/shard_map/weight_second/pallas_call | solution.py:455
  43.7 0.4 collective-permute-start.7
  44.1 0.4 collective-permute-start.9
  44.5 4.3 %collective-permute-start.10 = (bf16[320,128]{1,0:T(8,128)(2,1)}, bf16[320,128]{1,0:T(8,128)(2,1)S(1)}, u32[]{:S(2)}, u32[]{:S(2)}) collective-permute-start(bf16[320,128]{1,0:T(8,128)(2,1)} %pad_maximum_fusion.5), channel_id=1, source_target_pairs={{0,112},{4,116},{8,120},{12,124},{16,32},{20,36},{24,40},{28,44},{... | collective-permute-start | bytes 245768 | tf_op jit(solution)/shard_map/ppermute | solution.py:373
  48.8 0.0 collective-permute-done.7
  48.8 0.1 convert_add_fusion
  48.9 0.2 collective-permute-start.8
  49.1 2.4 %backward.4.refs_0_ = f32[256,128]{1,0:T(8,128)S(1)} custom-call(bf16[1024,128]{1,0:T(8,128)(2,1)S(1)} %get-tuple-element.81.grad_ref, s32[27,1024]{1,0:T(8,128)S(1)} %bitcast.46, bf16[27,128,128]{2,1,0:T(8,128)(2,1)S(1)} %bitcast.32), custom_call_target="tpu_custom_call" | custom-call | flops 3000000000 | bytes 2000000 | tf_op jit(solution)/shard_map/backward/pallas_call | solution.py:468
  51.6 0.0 collective-permute-done.9.iya_ref
  51.6 1.4 %collective-permute-done.10.iyb_ref = bf16[320,128]{1,0:T(8,128)(2,1)S(1)} collective-permute-done((bf16[320,128]{1,0:T(8,128)(2,1)}, bf16[320,128]{1,0:T(8,128)(2,1)S(1)}, u32[]{:S(2)}, u32[]{:S(2)}) %collective-permute-start.10) | collective-permute-done | bytes 81952 | tf_op jit(solution)/shard_map/ppermute | solution.py:373
  53.0 3.0 %returning.1.refs_4_ = f32[1152,128]{1,0:T(8,128)S(1)} custom-call(s32[3]{0:T(128)S(1)} %pad_add_fusion.side_ref, bf16[320,128]{1,0:T(8,128)(2,1)S(1)} %collective-permute-done.5.ixa_ref, bf16[320,128]{1,0:T(8,128)(2,1)S(1)} %collective-permute-done.6.ixb_ref, bf16[320,128]{1,0:T(8,128)(2,1)S(1)} %collective-permute-done.9.iya_ref, ...), custom_call_target="tpu_custom_call" | custom-call | flops 3000000000 | bytes 4000000 | tf_op jit(solution)/shard_map/returning/pallas_call | solution.py:489
  55.9 0.2 collective-permute-done.8
  56.3 0.1 collective-permute-start.11
  56.3 2.4 %backward.5.refs_1_ = f32[256,128]{1,0:T(8,128)S(1)} custom-call(bf16[1024,128]{1,0:T(8,128)(2,1)S(1)} %get-tuple-element.81.grad_ref, s32[27,1024]{1,0:T(8,128)S(1)} %bitcast.47, bf16[27,128,128]{2,1,0:T(8,128)(2,1)S(1)} %bitcast.34), custom_call_target="tpu_custom_call" | custom-call | flops 3000000000 | bytes 2000000 | tf_op jit(solution)/shard_map/backward/pallas_call | solution.py:468
  58.8 1.1 %collective-permute-done.11 = bf16[432,128]{1,0:T(8,128)(2,1)S(1)} collective-permute-done((bf16[432,128]{1,0:T(8,128)(2,1)S(1)}, bf16[432,128]{1,0:T(8,128)(2,1)S(1)}, u32[]{:S(2)}, u32[]{:S(2)}) %collective-permute-start.11) | collective-permute-done | bytes 110624 | tf_op jit(solution)/shard_map/ppermute | solution.py:381
  60.0 0.1 collective-permute-start.12
  60.1 2.4 %backward.6.refs_2_ = f32[256,128]{1,0:T(8,128)S(1)} custom-call(bf16[1024,128]{1,0:T(8,128)(2,1)S(1)} %get-tuple-element.81.grad_ref, s32[27,1024]{1,0:T(8,128)S(1)} %bitcast.48, bf16[27,128,128]{2,1,0:T(8,128)(2,1)S(1)} %bitcast.35), custom_call_target="tpu_custom_call" | custom-call | flops 3000000000 | bytes 2000000 | tf_op jit(solution)/shard_map/backward/pallas_call | solution.py:468
  62.5 0.2 collective-permute-start.14
  62.8 2.1 %collective-permute-done.12 = bf16[432,128]{1,0:T(8,128)(2,1)S(1)} collective-permute-done((bf16[432,128]{1,0:T(8,128)(2,1)S(1)}, bf16[432,128]{1,0:T(8,128)(2,1)S(1)}, u32[]{:S(2)}, u32[]{:S(2)}) %collective-permute-start.12) | collective-permute-done | bytes 110624 | tf_op jit(solution)/shard_map/ppermute | solution.py:381
  64.9 1.2 %collective-permute-start.13 = (bf16[432,128]{1,0:T(8,128)(2,1)S(1)}, bf16[432,128]{1,0:T(8,128)(2,1)S(1)}, u32[]{:S(2)}, u32[]{:S(2)}) collective-permute-start(bf16[432,128]{1,0:T(8,128)(2,1)S(1)} %add_convert_fusion.1), channel_id=1, source_target_pairs={{0,96},{4,100},{8,104},{12,108},{16,112},{20,116},{24,120},{28,124... | collective-permute-start | bytes 331784 | tf_op jit(solution)/shard_map/ppermute | solution.py:381
  66.0 2.4 %backward.7.refs_3_ = f32[256,128]{1,0:T(8,128)S(1)} custom-call(bf16[1024,128]{1,0:T(8,128)(2,1)S(1)} %get-tuple-element.81.grad_ref, s32[27,1024]{1,0:T(8,128)S(1)} %bitcast.49, bf16[27,128,128]{2,1,0:T(8,128)(2,1)S(1)} %bitcast.36), custom_call_target="tpu_custom_call" | custom-call | flops 3000000000 | bytes 2000000 | tf_op jit(solution)/shard_map/backward/pallas_call | solution.py:468
  68.5 1.5 %collective-permute-done.13 = bf16[432,128]{1,0:T(8,128)(2,1)S(1)} collective-permute-done((bf16[432,128]{1,0:T(8,128)(2,1)S(1)}, bf16[432,128]{1,0:T(8,128)(2,1)S(1)}, u32[]{:S(2)}, u32[]{:S(2)}) %collective-permute-start.13) | collective-permute-done | bytes 110624 | tf_op jit(solution)/shard_map/ppermute | solution.py:381
  70.1 0.1 collective-permute-start.15
  70.2 0.0 collective-permute-done.14.refs_7_
  70.2 1.7 %final.1 = (bf16[1024,128]{1,0:T(8,128)(2,1)}, bf16[1024,128]{1,0:T(8,128)(2,1)}) custom-call(f32[256,128]{1,0:T(8,128)S(1)} %backward.4.refs_0_, f32[256,128]{1,0:T(8,128)S(1)} %backward.5.refs_1_, f32[256,128]{1,0:T(8,128)S(1)} %backward.6.refs_2_, f32[256,128]{1,0:T(8,128)S(1)} %backward.7.refs_3_, f32[1152,128]{1,0:T(8,128)S(1)} %returning.1.refs_4_, ...), custom_call_target="tpu_custom_call" | custom-call | flops 1000000000 | bytes 3000000 | tf_op jit(solution)/shard_map/final/pallas_call | solution.py:509
  71.9 2.2 %collective-permute-done.15.one_ref = bf16[432,128]{1,0:T(8,128)(2,1)S(1)} collective-permute-done((bf16[432,128]{1,0:T(8,128)(2,1)S(1)}, bf16[432,128]{1,0:T(8,128)(2,1)S(1)}, u32[]{:S(2)}, u32[]{:S(2)}) %collective-permute-start.15) | collective-permute-done | bytes 110624 | tf_op jit(solution)/shard_map/ppermute | solution.py:381
  74.1 0.1 collective-permute-start.16
  74.2 5.1 %collective-permute-done.16.two_ref = bf16[2,432,128]{2,1,0:T(8,128)(2,1)S(1)} collective-permute-done((bf16[2,432,128]{2,1,0:T(8,128)(2,1)S(1)}, bf16[2,432,128]{2,1,0:T(8,128)(2,1)S(1)}, u32[]{:S(2)}, u32[]{:S(2)}) %collective-permute-start.16) | collective-permute-done | bytes 221216 | tf_op jit(solution)/shard_map/ppermute | solution.py:381
  79.3 6.9 %collective-permute-start.17 = (bf16[4,432,128]{2,1,0:T(8,128)(2,1)S(1)}, bf16[4,432,128]{2,1,0:T(8,128)(2,1)S(1)}, u32[]{:S(2)}, u32[]{:S(2)}) collective-permute-start(bf16[4,432,128]{2,1,0:T(8,128)(2,1)S(1)} %pad_maximum_fusion), channel_id=1, source_target_pairs={{0,4},{4,0},{8,12},{12,8},{16,20},{20,16},{24,28},{28,24},{32,36},... | collective-permute-start | bytes 1327112 | tf_op jit(solution)/shard_map/ppermute | solution.py:381
  86.2 0.1 pad_add_fusion.1.bits_ref
  86.3 1.3 %collective-permute-done.17.four_ref = bf16[4,432,128]{2,1,0:T(8,128)(2,1)S(1)} collective-permute-done((bf16[4,432,128]{2,1,0:T(8,128)(2,1)S(1)}, bf16[4,432,128]{2,1,0:T(8,128)(2,1)S(1)}, u32[]{:S(2)}, u32[]{:S(2)}) %collective-permute-start.17) | collective-permute-done | bytes 442400 | tf_op jit(solution)/shard_map/ppermute | solution.py:381
  87.6 1.9 %assemble.1 = f32[8,432,128]{2,1,0:T(8,128)} custom-call(s32[3]{0:T(128)S(1)} %pad_add_fusion.1.bits_ref, bf16[432,128]{1,0:T(8,128)(2,1)S(1)} %add_convert_fusion.own_ref, bf16[432,128]{1,0:T(8,128)(2,1)S(1)} %collective-permute-done.15.one_ref, bf16[2,432,128]{2,1,0:T(8,128)(2,1)S(1)} %collective-permute-done.16.two_ref, ...), custom_call_target="tpu_custom_call" | custom-call | flops 1000000 | bytes 3000000 | tf_op jit(solution)/shard_map/assemble/pallas_call | solution.py:519
  (20 shorter events, 0.3 us)
Async XLA Ops:
  0.6 26.7 %collective-permute-start.4 = (bf16[1024,128]{1,0:T(8,128)(2,1)}, bf16[1024,128]{1,0:T(8,128)(2,1)S(1)}, u32[]{:S(2)}, u32[]{:S(2)}) collective-permute-start(bf16[1024,128]{1,0:T(8,128)(2,1)} %bitcast.37), channel_id=1, source_target_pairs={{0,1},{1,0},{2,3},{3,2},{4,5},{5,4},{6,7},{7,6},{8,9},{9,8},{10,11... | collective-permute-start | bytes 786440 | tf_op jit(solution)/shard_map/ppermute | solution.py:377
  3.6 1.0 %copy-start.2 = (bf16[1,1024,128]{2,1,0:T(8,128)(2,1)S(1)}, bf16[1,1024,128]{2,1,0:T(8,128)(2,1)}, u32[]{:S(2)}) copy-start(bf16[1,1024,128]{2,1,0:T(8,128)(2,1)} %param.6) | copy-start | bytes 786436
  4.6 0.9 %copy-start.4 = (s32[1152,27]{0,1:T(8,128)S(1)}, s32[1152,27]{0,1:T(8,128)}, u32[]{:S(2)}) copy-start(s32[1152,27]{0,1:T(8,128)} %param.10) | copy-start | bytes 373252
  5.5 4.5 %copy-start = (bf16[1,27,128,128]{3,2,1,0:T(8,128)(2,1)S(1)}, bf16[1,27,128,128]{3,2,1,0:T(8,128)(2,1)}, u32[]{:S(2)}) copy-start(bf16[1,27,128,128]{3,2,1,0:T(8,128)(2,1)} %param.7) | copy-start | bytes 2654212
  5.5 4.5 %copy-start.5 = (s32[1024,27]{0,1:T(8,128)S(1)}, s32[1024,27]{0,1:T(8,128)}, u32[]{:S(2)}) copy-start(s32[1024,27]{0,1:T(8,128)} %param.9) | copy-start | bytes 331780
  7.8 8.3 %collective-permute-start = (bf16[384,128]{1,0:T(8,128)(2,1)S(1)}, bf16[384,128]{1,0:T(8,128)(2,1)S(1)}, u32[]{:S(2)}, u32[]{:S(2)}) collective-permute-start(bf16[384,128]{1,0:T(8,128)(2,1)S(1)} %get-tuple-element.47), channel_id=1, source_target_pairs={{0,4},{4,0},{8,12},{12,8},{16,20},{20,16},{24,28},{28,24},{32,36},... | collective-permute-start | bytes 294920 | tf_op jit(solution)/shard_map/ppermute | solution.py:360
  8.8 7.2 %collective-permute-start.1 = (bf16[384,128]{1,0:T(8,128)(2,1)S(1)}, bf16[384,128]{1,0:T(8,128)(2,1)S(1)}, u32[]{:S(2)}, u32[]{:S(2)}) collective-permute-start(bf16[384,128]{1,0:T(8,128)(2,1)S(1)} %get-tuple-element.50), channel_id=1, source_target_pairs={{0,12},{4,8},{8,4},{12,0},{16,28},{20,24},{24,20},{28,16},{32,44},... | collective-permute-start | bytes 294920 | tf_op jit(solution)/shard_map/ppermute | solution.py:360
  10.0 12.9 %copy-start.3 = (bf16[1,1024,128]{2,1,0:T(8,128)(2,1)S(1)}, bf16[1,1024,128]{2,1,0:T(8,128)(2,1)}, u32[]{:S(2)}) copy-start(bf16[1,1024,128]{2,1,0:T(8,128)(2,1)} %param.6) | copy-start | bytes 786436
  14.3 1.7 %copy-start.6 = (bf16[1664,1024]{1,0:T(8,128)(2,1)}, bf16[1664,1024]{1,0:T(8,128)(2,1)S(1)}, u32[]{:S(2)}) copy-start(bf16[1664,1024]{1,0:T(8,128)(2,1)S(1)} %get-tuple-element.60.g_ref) | copy-start | bytes 10223620
  16.1 11.2 %collective-permute-start.2 = (bf16[384,128]{1,0:T(8,128)(2,1)S(1)}, bf16[384,128]{1,0:T(8,128)(2,1)S(1)}, u32[]{:S(2)}, u32[]{:S(2)}) collective-permute-start(bf16[384,128]{1,0:T(8,128)(2,1)S(1)} %pad_maximum_fusion.2), channel_id=1, source_target_pairs={{0,16},{4,20},{8,24},{12,28},{16,0},{20,4},{24,8},{28,12},{32,48},... | collective-permute-start | bytes 294920 | tf_op jit(solution)/shard_map/ppermute | solution.py:373
  18.6 8.7 %copy-start.1 = (bf16[1,1024,128]{2,1,0:T(8,128)(2,1)S(1)}, bf16[1,1024,128]{2,1,0:T(8,128)(2,1)}, u32[]{:S(2)}) copy-start(bf16[1,1024,128]{2,1,0:T(8,128)(2,1)} %param.8) | copy-start | bytes 786436
  18.6 8.7 %collective-permute-start.3 = (bf16[384,128]{1,0:T(8,128)(2,1)S(1)}, bf16[384,128]{1,0:T(8,128)(2,1)S(1)}, u32[]{:S(2)}, u32[]{:S(2)}) collective-permute-start(bf16[384,128]{1,0:T(8,128)(2,1)S(1)} %pad_maximum_fusion.3), channel_id=1, source_target_pairs={{0,112},{4,116},{8,120},{12,124},{16,32},{20,36},{24,40},{28,44},{... | collective-permute-start | bytes 294920 | tf_op jit(solution)/shard_map/ppermute | solution.py:373
  27.3 8.0 %copy-start.7 = (bf16[1664,1024]{1,0:T(8,128)(2,1)S(1)}, bf16[1664,1024]{1,0:T(8,128)(2,1)}, u32[]{:S(2)}) copy-start(bf16[1664,1024]{1,0:T(8,128)(2,1)} %copy-done.6) | copy-start | bytes 10223620
  34.1 2.6 %collective-permute-start.5 = (bf16[320,128]{1,0:T(8,128)(2,1)S(1)}, bf16[320,128]{1,0:T(8,128)(2,1)S(1)}, u32[]{:S(2)}, u32[]{:S(2)}) collective-permute-start(bf16[320,128]{1,0:T(8,128)(2,1)S(1)} %get-tuple-element.63), channel_id=1, source_target_pairs={{0,4},{4,0},{8,12},{12,8},{16,20},{20,16},{24,28},{28,24},{32,36},... | collective-permute-start | bytes 245768 | tf_op jit(solution)/shard_map/ppermute | solution.py:360
  36.5 4.2 %collective-permute-start.6 = (bf16[320,128]{1,0:T(8,128)(2,1)S(1)}, bf16[320,128]{1,0:T(8,128)(2,1)S(1)}, u32[]{:S(2)}, u32[]{:S(2)}) collective-permute-start(bf16[320,128]{1,0:T(8,128)(2,1)S(1)} %get-tuple-element.65), channel_id=1, source_target_pairs={{0,12},{4,8},{8,4},{12,0},{16,28},{20,24},{24,20},{28,16},{32,44},... | collective-permute-start | bytes 245768 | tf_op jit(solution)/shard_map/ppermute | solution.py:360
  43.7 5.1 %collective-permute-start.7 = (bf16[1728,128]{1,0:T(8,128)(2,1)S(1)}, bf16[1728,128]{1,0:T(8,128)(2,1)S(1)}, u32[]{:S(2)}, u32[]{:S(2)}) collective-permute-start(bf16[1728,128]{1,0:T(8,128)(2,1)S(1)} %get-tuple-element.71), channel_id=1, source_target_pairs={{0,4},{4,0},{8,12},{12,8},{16,20},{20,16},{24,28},{28,24},{32,36},... | collective-permute-start | bytes 1327112 | tf_op jit(solution)/shard_map/ppermute | solution.py:381
  44.1 7.5 %collective-permute-start.9 = (bf16[320,128]{1,0:T(8,128)(2,1)}, bf16[320,128]{1,0:T(8,128)(2,1)S(1)}, u32[]{:S(2)}, u32[]{:S(2)}) collective-permute-start(bf16[320,128]{1,0:T(8,128)(2,1)} %pad_maximum_fusion.4), channel_id=1, source_target_pairs={{0,16},{4,20},{8,24},{12,28},{16,0},{20,4},{24,8},{28,12},{32,48},... | collective-permute-start | bytes 245768 | tf_op jit(solution)/shard_map/ppermute | solution.py:373
  44.5 8.5 %collective-permute-start.10 = (bf16[320,128]{1,0:T(8,128)(2,1)}, bf16[320,128]{1,0:T(8,128)(2,1)S(1)}, u32[]{:S(2)}, u32[]{:S(2)}) collective-permute-start(bf16[320,128]{1,0:T(8,128)(2,1)} %pad_maximum_fusion.5), channel_id=1, source_target_pairs={{0,112},{4,116},{8,120},{12,124},{16,32},{20,36},{24,40},{28,44},{... | collective-permute-start | bytes 245768 | tf_op jit(solution)/shard_map/ppermute | solution.py:373
  48.9 7.3 %collective-permute-start.8 = (bf16[2,432,128]{2,1,0:T(8,128)(2,1)S(1)}, bf16[2,432,128]{2,1,0:T(8,128)(2,1)S(1)}, u32[]{:S(2)}, u32[]{:S(2)}) collective-permute-start(bf16[2,432,128]{2,1,0:T(8,128)(2,1)S(1)} %fusion), channel_id=1, source_target_pairs={{0,8},{4,12},{8,0},{12,4},{16,24},{20,28},{24,16},{28,20},{32,40},... | collective-permute-start | bytes 663560 | tf_op jit(solution)/shard_map/ppermute | solution.py:381
  56.3 3.7 %collective-permute-start.11 = (bf16[432,128]{1,0:T(8,128)(2,1)S(1)}, bf16[432,128]{1,0:T(8,128)(2,1)S(1)}, u32[]{:S(2)}, u32[]{:S(2)}) collective-permute-start(bf16[432,128]{1,0:T(8,128)(2,1)S(1)} %fusion.2), channel_id=1, source_target_pairs={{0,32},{4,36},{8,40},{12,44},{16,48},{20,52},{24,56},{28,60},{32,0... | collective-permute-start | bytes 331784 | tf_op jit(solution)/shard_map/ppermute | solution.py:381
  60.0 4.9 %collective-permute-start.12 = (bf16[432,128]{1,0:T(8,128)(2,1)S(1)}, bf16[432,128]{1,0:T(8,128)(2,1)S(1)}, u32[]{:S(2)}, u32[]{:S(2)}) collective-permute-start(bf16[432,128]{1,0:T(8,128)(2,1)S(1)} %fusion.1), channel_id=1, source_target_pairs={{0,24},{4,28},{8,16},{12,20},{16,8},{20,12},{24,0},{28,4},{32,56},... | collective-permute-start | bytes 331784 | tf_op jit(solution)/shard_map/ppermute | solution.py:381
  62.5 7.7 %collective-permute-start.14 = (bf16[1024,128]{1,0:T(8,128)(2,1)S(1)}, bf16[1024,128]{1,0:T(8,128)(2,1)S(1)}, u32[]{:S(2)}, u32[]{:S(2)}) collective-permute-start(bf16[1024,128]{1,0:T(8,128)(2,1)S(1)} %get-tuple-element.85.refs_6_), channel_id=1, source_target_pairs={{0,1},{1,0},{2,3},{3,2},{4,5},{5,4},{6,7},{7,6},{8,9},{9,8},{10,11... | collective-permute-start | bytes 786440 | tf_op jit(solution)/shard_map/ppermute | solution.py:377
  64.9 5.2 %collective-permute-start.13 = (bf16[432,128]{1,0:T(8,128)(2,1)S(1)}, bf16[432,128]{1,0:T(8,128)(2,1)S(1)}, u32[]{:S(2)}, u32[]{:S(2)}) collective-permute-start(bf16[432,128]{1,0:T(8,128)(2,1)S(1)} %add_convert_fusion.1), channel_id=1, source_target_pairs={{0,96},{4,100},{8,104},{12,108},{16,112},{20,116},{24,120},{28,124... | collective-permute-start | bytes 331784 | tf_op jit(solution)/shard_map/ppermute | solution.py:381
  70.1 4.0 %collective-permute-start.15 = (bf16[432,128]{1,0:T(8,128)(2,1)S(1)}, bf16[432,128]{1,0:T(8,128)(2,1)S(1)}, u32[]{:S(2)}, u32[]{:S(2)}) collective-permute-start(bf16[432,128]{1,0:T(8,128)(2,1)S(1)} %add_convert_fusion.own_ref), channel_id=1, source_target_pairs={{0,32},{4,36},{8,40},{12,44},{16,48},{20,52},{24,56},{28,60},{32,0... | collective-permute-start | bytes 331784 | tf_op jit(solution)/shard_map/ppermute | solution.py:381
  74.1 5.2 %collective-permute-start.16 = (bf16[2,432,128]{2,1,0:T(8,128)(2,1)S(1)}, bf16[2,432,128]{2,1,0:T(8,128)(2,1)S(1)}, u32[]{:S(2)}, u32[]{:S(2)}) collective-permute-start(bf16[2,432,128]{2,1,0:T(8,128)(2,1)S(1)} %pad_maximum_fusion.1), channel_id=1, source_target_pairs={{0,8},{4,12},{8,0},{12,4},{16,24},{20,28},{24,16},{28,20},{32,40},... | collective-permute-start | bytes 663560 | tf_op jit(solution)/shard_map/ppermute | solution.py:381
  79.3 8.4 %collective-permute-start.17 = (bf16[4,432,128]{2,1,0:T(8,128)(2,1)S(1)}, bf16[4,432,128]{2,1,0:T(8,128)(2,1)S(1)}, u32[]{:S(2)}, u32[]{:S(2)}) collective-permute-start(bf16[4,432,128]{2,1,0:T(8,128)(2,1)S(1)} %pad_maximum_fusion), channel_id=1, source_target_pairs={{0,4},{4,0},{8,12},{12,8},{16,20},{20,16},{24,28},{28,24},{32,36},... | collective-permute-start | bytes 1327112 | tf_op jit(solution)/shard_map/ppermute | solution.py:381
where the time goes:
time: 89.7 us; the launch traced here: 89.5 us
  Pallas kernels  37 us (41%)
  starting transfers between devices  26.7 us (30%)
  waiting for transfers between devices  18.9 us (21%)
  local copies, waits for them, and re-layouts  4.34 us (5%)
  other arithmetic  1.75 us (2%)
    ppermute x8, waiting for transfers between devices, xor_send(): lax.ppermute(value, 'space', [(i, i ^ bits) for i in range(lax.axis_size(...  13.6 us
    ppermute x4, starting transfers between devices, exchange_y(): lax.ppermute(v, 'space', pairing('y', n))  11.5 us
    pallas_call x4, Pallas kernels, backward(): pl.pallas_call(functools.partial(backward_kernel, begin=index * size), ou...  9.79 us
    ppermute x8, starting transfers between devices, xor_send(): lax.ppermute(value, 'space', [(i, i ^ bits) for i in range(lax.axis_size(...  9.06 us
    pallas_call x2, Pallas kernels, forward(): pl.pallas_call(functools.partial(forward_kernel, width=512, first=first),...  8.7 us
    pallas_call x1, Pallas kernels, on_device(): pl.pallas_call(activate_kernel, in_specs=[smem] + [vmem] * 9, out_shape=[...  6.77 us
    ppermute x4, waiting for transfers between devices, exchange_x(): lax.ppermute(v, 'space', pairing('x', n))  3.91 us
    ppermute x4, starting transfers between devices, exchange_x(): lax.ppermute(v, 'space', pairing('x', n))  3.69 us
  transfers between devices with their start and end apart: 18, of which 9 were waited for; matrix products, arithmetic and copies ran while one was open for 1% of the time, Pallas kernels for 30%

commit v1 on v0

--- a/solution.py
+++ b/solution.py
@@ -450,8 +450,6 @@
         cost_estimate=cost(4e9, 5e6),
         name="weight_first",
     )(g0, grad, x, dw_halo)
-    sent = second_phase(*[tie(v, first) for v in (ya, yb, *in_x)], sides, CAP, TZ)
-    in_y = exchange_y(sent)
     kept, sent = pl.pallas_call(
         weight_second_kernel,
         in_specs=[smem] + [vmem] * 4,
@@ -460,7 +458,7 @@
         compiler_params=PARAMS,
         cost_estimate=cost(4e9, 5e6),
         name="weight_second",
-    )(sides, g1, tie(grad, tuple(sent)), first, dw_halo)
+    )(sides, g1, grad, first, dw_halo)
 
     size = ROWS // 4
 
@@ -484,37 +482,40 @@
     locals_ = []
     got = xor_send(sent, 1)
     kept, sent = halve(plus(kept, got).reshape(2, 2, -1, C), 1)
+    sent, in_x = lax.optimization_barrier((sent, in_x))
     got = xor_send(sent, 2)
     locals_.append(backward(0, tie(grad, sent)))
-    placed = pl.pallas_call(
-        return_kernel,
-        in_specs=[smem] + [vmem] * 7,
-        out_shape=shape((HALO, C), F32),
-        compiler_params=PARAMS,
-        cost_estimate=cost(3e9, 4e6),
-        name="returning",
-    )(sides, *in_x, *in_y, face_p, edge_p, tie(w, locals_[0]))
-    kept, sent = halve(plus(kept, tie(got, placed)), 2)
+    locals_.append(backward(1, tie(grad, locals_[0])))
+    kept, sent = halve(plus(kept, tie(got, locals_[1])), 2)
     got = xor_send(sent, 8)
-    locals_.append(backward(1, tie(grad, sent)))
-    own = plus(kept, tie(got, locals_[1])).astype(BF)
+    in_y = exchange_y(second_phase(*[tie(v, sent) for v in (ya, yb, *in_x)], sides, CAP, TZ))
+    own = plus(kept, got).astype(BF)
     got = xor_send(own, 6)
     act_pair = swapped(tie(act, own))
     locals_.append(backward(2, tie(grad, own)))
     own = plus(own, tie(got, locals_[2])).astype(BF)
     got = xor_send(own, 24)
+    placed = pl.pallas_call(
+        return_kernel,
+        in_specs=[smem] + [vmem] * 7,
+        out_shape=shape((HALO, C), F32),
+        compiler_params=PARAMS,
+        cost_estimate=cost(3e9, 4e6),
+        name="returning",
+    )(sides, *in_x, *in_y, face_p, edge_p, tie(w, own))
+    own = plus(own, tie(got, placed)).astype(BF)
+    one = xor_send(own, 8)
     locals_.append(backward(3, tie(grad, own)))
-    own = plus(own, tie(got, locals_[3])).astype(BF)
-    one = xor_send(own, 8)
+    one = tie(one, locals_[3])
+    two = xor_send(jnp.stack([own, one]), 2)
     mixed, input_grad = pl.pallas_call(
         final_kernel,
         out_shape=[shape((ROWS, C), BF), shape((ROWS, C), BF)],
         compiler_params=PARAMS,
         cost_estimate=cost(1e9, 3e6),
         name="final",
-    )(*locals_, tie(placed, own), rr, act, act_pair)
-    one = tie(one, input_grad)
-    two = xor_send(jnp.stack([own, one]), 2)
+    )(*locals_, tie(placed, one), rr, act, act_pair)
+    two = tie(two, input_grad)
     four = xor_send(jnp.concatenate([jnp.stack([own, one]), two], 0), 1)
     weight_grad = pl.pallas_call(
         assemble_kernel,

time: 89.7 us -> 83.5 us (0.931)
  waiting for transfers between devices: 18.9 us -> 11.6 us
  starting transfers between devices: 26.7 us -> 28 us
    ppermute x8, waiting for transfers between devices: 13.6 us -> 9.63 us  [xor_send(): lax.ppermute(value, 'space', [(i, i ^ bits) for i in range(lax.axis_size(...]
    ppermute x8, starting transfers between devices: 9.06 us -> 11.1 us  [xor_send(): lax.ppermute(value, 'space', [(i, i ^ bits) for i in range(lax.axis_size(...]
    ppermute x4, waiting for transfers between devices: 3.91 us -> 1.9 us  [exchange_x(): lax.ppermute(v, 'space', pairing('x', n))]
    ppermute x4, waiting for transfers between devices: 1.42 us -> 0.05 us  [exchange_y(): lax.ppermute(v, 'space', pairing('y', n))]
    concatenate x4, other arithmetic: 1.3 us -> 0.03 us  [second_phase(): sent.append(jnp.concatenate([own] + corners, 0))]
    add x2, other arithmetic: 0.12 us -> 1.13 us  [plus(): return one.astype(F32) + two.astype(F32)]
  transfers between devices with their start and end apart: 18 -> 18, of which waited for: 9 -> 7; matrix products, arithmetic and copies ran while one was open for 1% -> 3% of each run, Pallas kernels for 30% -> 31%
where the time goes in v1:
time: 83.5 us; the launch traced here: 83.3 us
  Pallas kernels  37 us (44%)
  starting transfers between devices  28 us (34%)
  waiting for transfers between devices  11.6 us (14%)
  local copies, waits for them, and re-layouts  4.34 us (5%)
  other arithmetic  1.5 us (2%)
  between operations  0.87 us (1%)
    ppermute x4, starting transfers between devices, exchange_y(): lax.ppermute(v, 'space', pairing('y', n))  11.6 us
    ppermute x8, starting transfers between devices, xor_send(): lax.ppermute(value, 'space', [(i, i ^ bits) for i in range(lax.axis_size(...  11.1 us
    pallas_call x4, Pallas kernels, backward(): pl.pallas_call(functools.partial(backward_kernel, begin=index * size), ou...  9.79 us
    ppermute x8, waiting for transfers between devices, xor_send(): lax.ppermute(value, 'space', [(i, i ^ bits) for i in range(lax.axis_size(...  9.63 us
    pallas_call x2, Pallas kernels, forward(): pl.pallas_call(functools.partial(forward_kernel, width=512, first=first),...  8.7 us
    pallas_call x1, Pallas kernels, on_device(): pl.pallas_call(activate_kernel, in_specs=[smem] + [vmem] * 9, out_shape=[...  6.77 us
    unnamed x16, local copies, waits for them, and re-layouts  3.58 us
    pallas_call x1, Pallas kernels, on_device(): pl.pallas_call(return_kernel, in_specs=[smem] + [vmem] * 7, out_shape=sha...  2.98 us
  transfers between devices with their start and end apart: 18, of which 7 were waited for; matrix products, arithmetic and copies ran while one was open for 3% of the time, Pallas kernels for 31%

profile of v1, /device:TPU:1, one launch (start us, length us, event | category | flops | bytes accessed | tf_op | source)
XLA Modules:
  0.0 83.3 jit_solution(9907152382102827754)
XLA Ops:
  0.6 2.2 %collective-permute-start.4 = (bf16[1024,128]{1,0:T(8,128)(2,1)}, bf16[1024,128]{1,0:T(8,128)(2,1)S(1)}, u32[]{:S(2)}, u32[]{:S(2)}) collective-permute-start(bf16[1024,128]{1,0:T(8,128)(2,1)} %bitcast.37), channel_id=1, source_target_pairs={{0,1},{1,0},{2,3},{3,2},{4,5},{5,4},{6,7},{7,6},{8,9},{9,8},{10,11... | collective-permute-start | bytes 786440 | tf_op jit(solution)/shard_map/ppermute | solution.py:377
  2.8 0.7 reshape.14.rr_ref.refs_5_
  3.5 0.1 pad_add_fusion.side_ref
  3.6 0.0 copy-start.2
  3.6 0.9 %copy-done.2 = bf16[1,1024,128]{2,1,0:T(8,128)(2,1)S(1)} copy-done((bf16[1,1024,128]{2,1,0:T(8,128)(2,1)S(1)}, bf16[1,1024,128]{2,1,0:T(8,128)(2,1)}, u32[]{:S(2)}) %copy-start.2) | copy-done | bytes 262168
  4.6 0.0 copy-start.4
  4.6 0.9 %copy-done.4 = s32[1152,27]{0,1:T(8,128)S(1)} copy-done((s32[1152,27]{0,1:T(8,128)S(1)}, s32[1152,27]{0,1:T(8,128)}, u32[]{:S(2)}) %copy-start.4) | copy-done | bytes 124440
  5.5 2.3 %start.1 = (bf16[384,128]{1,0:T(8,128)(2,1)S(1)}, bf16[384,128]{1,0:T(8,128)(2,1)S(1)}, bf16[288,128]{1,0:T(8,128)(2,1)S(1)}, bf16[288,128]{1,0:T(8,128)(2,1)S(1...) custom-call(s32[3]{0:T(128)S(1)} %pad_add_fusion.side_ref, bf16[1024,128]{1,0:T(8,128)(2,1)S(1)} %bitcast.39, ...), custom_call_target="tpu_custom_call" | custom-call | flops 2000000000 | bytes 4000000 | tf_op jit(solution)/shard_map/start/pallas_call | solution.py:410
  7.8 1.0 %collective-permute-start = (bf16[384,128]{1,0:T(8,128)(2,1)S(1)}, bf16[384,128]{1,0:T(8,128)(2,1)S(1)}, u32[]{:S(2)}, u32[]{:S(2)}) collective-permute-start(bf16[384,128]{1,0:T(8,128)(2,1)S(1)} %get-tuple-element.49), channel_id=1, source_target_pairs={{0,4},{4,0},{8,12},{12,8},{16,20},{20,16},{24,28},{28,24},{32,36},... | collective-permute-start | bytes 294920 | tf_op jit(solution)/shard_map/ppermute | solution.py:360
  8.8 1.2 %collective-permute-start.1 = (bf16[384,128]{1,0:T(8,128)(2,1)S(1)}, bf16[384,128]{1,0:T(8,128)(2,1)S(1)}, u32[]{:S(2)}, u32[]{:S(2)}) collective-permute-start(bf16[384,128]{1,0:T(8,128)(2,1)S(1)} %get-tuple-element.52), channel_id=1, source_target_pairs={{0,12},{4,8},{8,4},{12,0},{16,28},{20,24},{24,20},{28,16},{32,44},... | collective-permute-start | bytes 294920 | tf_op jit(solution)/shard_map/ppermute | solution.py:360
  10.0 0.0 copy-done
  10.0 0.0 copy-done.5
  10.0 4.3 %forward.2 = (bf16[1664,1024]{1,0:T(8,128)(2,1)S(1)}, f32[128,1024]{1,0:T(8,128)S(1)}) custom-call(bf16[1024,128]{1,0:T(8,128)(2,1)S(1)} %bitcast.40, s32[27,1024]{1,0:T(8,128)S(1)} %bitcast.44, bf16[27,128,128]{2,1,0:T(8,128)(2,1)S(1)} %bitcast.29), custom_call_target="tpu_custom_call" | custom-call | flops 7000000000 | bytes 5000000 | tf_op jit(solution)/shard_map/forward/pallas_call | solution.py:422
  14.4 0.0 copy-start.6
  14.4 1.7 %copy-done.6 = bf16[1664,1024]{1,0:T(8,128)(2,1)} copy-done((bf16[1664,1024]{1,0:T(8,128)(2,1)}, bf16[1664,1024]{1,0:T(8,128)(2,1)S(1)}, u32[]{:S(2)}) %copy-start.6) | copy-done | bytes 3407896
  16.1 0.0 collective-permute-done.1.ixb_ref
  16.1 0.0 collective-permute-done.ixa_ref
  16.1 2.5 %collective-permute-start.2 = (bf16[384,128]{1,0:T(8,128)(2,1)S(1)}, bf16[384,128]{1,0:T(8,128)(2,1)S(1)}, u32[]{:S(2)}, u32[]{:S(2)}) collective-permute-start(bf16[384,128]{1,0:T(8,128)(2,1)S(1)} %pad_maximum_fusion.2), channel_id=1, source_target_pairs={{0,16},{4,20},{8,24},{12,28},{16,0},{20,4},{24,8},{28,12},{32,48},... | collective-permute-start | bytes 294920 | tf_op jit(solution)/shard_map/ppermute | solution.py:373
  18.6 4.3 %collective-permute-start.3 = (bf16[384,128]{1,0:T(8,128)(2,1)S(1)}, bf16[384,128]{1,0:T(8,128)(2,1)S(1)}, u32[]{:S(2)}, u32[]{:S(2)}) collective-permute-start(bf16[384,128]{1,0:T(8,128)(2,1)S(1)} %pad_maximum_fusion.3), channel_id=1, source_target_pairs={{0,112},{4,116},{8,120},{12,124},{16,32},{20,36},{24,40},{28,44},{... | collective-permute-start | bytes 294920 | tf_op jit(solution)/shard_map/ppermute | solution.py:373
  22.9 0.0 copy-done.3
  22.9 4.4 %forward.3 = (bf16[1664,1024]{1,0:T(8,128)(2,1)S(1)}, f32[1024,128]{1,0:T(8,128)S(1)}) custom-call(bf16[1024,128]{1,0:T(8,128)(2,1)S(1)} %bitcast.41, s32[27,1024]{1,0:T(8,128)S(1)} %bitcast.45, bf16[27,128,128]{2,1,0:T(8,128)(2,1)S(1)} %bitcast.30, f32[128,1024]{1,0:T(8,128)S(1)} %get-tuple-element.50.refs_0_), custom_call_target="tpu_custom_call" | custom-call | flops 7000000000 | bytes 5000000 | tf_op jit(solution)/shard_map/forward/pallas_call | solution.py:422
  27.3 0.0 collective-permute-done.3.iyb_ref
  27.3 0.0 collective-permute-done.2.iya_ref
  27.3 0.0 collective-permute-done.4.pair_ref
  27.3 0.0 copy-done.1
  27.3 6.8 %activate.1 = (bf16[1024,128]{1,0:T(8,128)(2,1)S(1)}, bf16[1024,128]{1,0:T(8,128)(2,1)S(1)}, bf16[320,128]{1,0:T(8,128)(2,1)S(1)}, bf16[320,128]{1,0:T(8,128)(2,...) custom-call(s32[3]{0:T(128)S(1)} %pad_add_fusion.side_ref, ...), custom_call_target="tpu_custom_call" | custom-call | flops 4000000000 | bytes 3000000 | tf_op jit(solution)/shard_map/activate/pallas_call | solution.py:436
  34.1 0.0 copy-done.7
  34.1 1.1 %weight_first.1.first_ref = f32[1792,128]{1,0:T(8,128)S(1)} custom-call(bf16[1664,1024]{1,0:T(8,128)(2,1)S(1)} %copy-done.7, bf16[1024,128]{1,0:T(8,128)(2,1)S(1)} %get-tuple-element.85.grad_ref, bf16[1024,128]{1,0:T(8,128)(2,1)S(1)} %bitcast.42, f32[27,128,128]{2,1,0:T(8,128)S(1)} %get-tuple-element.62.halo_ref), custom_call_target="tpu_custom_call" | custom-call | flops 4000000000 | bytes 5000000 | tf_op jit(solution)/shard_map/weight_first/pallas_call | solution.py:446
  35.3 1.7 %weight_second.1 = (f32[1728,128]{1,0:T(8,128)S(1)}, bf16[1728,128]{1,0:T(8,128)(2,1)S(1)}) custom-call(s32[3]{0:T(128)S(1)} %pad_add_fusion.side_ref, bf16[1664,1024]{1,0:T(8,128)(2,1)S(1)} %get-tuple-element.60.g_ref, bf16[1024,128]{1,0:T(8,128)(2,1)S(1)} %get-tuple-element.85.grad_ref, f32[1792,128]{1,0:T(8,128)S(1)} %weight_first.1.first_ref, ...), custom_call_target="tpu_custom_call" | custom-call | flops 4000000000 | bytes 5000000 | tf_op jit(solution)/shard_map/weight_second/pallas_call | solution.py:453
  37.0 1.2 %collective-permute-start.5 = (bf16[1728,128]{1,0:T(8,128)(2,1)S(1)}, bf16[1728,128]{1,0:T(8,128)(2,1)}, u32[]{:S(2)}, u32[]{:S(2)}) collective-permute-start(bf16[1728,128]{1,0:T(8,128)(2,1)S(1)} %get-tuple-element.64), channel_id=1, source_target_pairs={{0,4},{4,0},{8,12},{12,8},{16,20},{20,16},{24,28},{28,24},{32,36},... | collective-permute-start | bytes 1327112 | tf_op jit(solution)/shard_map/ppermute | solution.py:381
  38.2 0.2 collective-permute-start.6
  38.4 0.5 collective-permute-start.7
  38.9 0.9 %collective-permute-done.5 = bf16[1728,128]{1,0:T(8,128)(2,1)} collective-permute-done((bf16[1728,128]{1,0:T(8,128)(2,1)S(1)}, bf16[1728,128]{1,0:T(8,128)(2,1)}, u32[]{:S(2)}, u32[]{:S(2)}) %collective-permute-start.5) | collective-permute-done | bytes 442400 | tf_op jit(solution)/shard_map/ppermute | solution.py:381
  39.8 1.1 %convert_add_fusion = f32[1728,128]{1,0:T(8,128)S(1)} fusion(f32[1728,128]{1,0:T(8,128)S(1)} %get-tuple-element.63, bf16[1728,128]{1,0:T(8,128)(2,1)} %collective-permute-done.5), kind=kLoop, calls=%fused_computation | loop fusion | flops 442368 | bytes 2211840 | tf_op jit(solution)/shard_map/add | solution.py:480
  40.9 0.0 collective-permute-done.6.ixa_ref
  40.9 1.9 %collective-permute-done.7.ixb_ref = bf16[320,128]{1,0:T(8,128)(2,1)S(1)} collective-permute-done((bf16[320,128]{1,0:T(8,128)(2,1)S(1)}, bf16[320,128]{1,0:T(8,128)(2,1)S(1)}, u32[]{:S(2)}, u32[]{:S(2)}) %collective-permute-start.7) | collective-permute-done | bytes 81952 | tf_op jit(solution)/shard_map/ppermute | solution.py:360
  42.8 0.3 collective-permute-start.8
  43.1 2.4 %backward.4.refs_0_ = f32[256,128]{1,0:T(8,128)S(1)} custom-call(bf16[1024,128]{1,0:T(8,128)(2,1)S(1)} %get-tuple-element.85.grad_ref, s32[27,1024]{1,0:T(8,128)S(1)} %bitcast.46, bf16[27,128,128]{2,1,0:T(8,128)(2,1)S(1)} %bitcast.32), custom_call_target="tpu_custom_call" | custom-call | flops 3000000000 | bytes 2000000 | tf_op jit(solution)/shard_map/backward/pallas_call | solution.py:466
  45.5 2.5 %backward.5.refs_1_ = f32[256,128]{1,0:T(8,128)S(1)} custom-call(bf16[1024,128]{1,0:T(8,128)(2,1)S(1)} %get-tuple-element.85.grad_ref, s32[27,1024]{1,0:T(8,128)S(1)} %bitcast.47, bf16[27,128,128]{2,1,0:T(8,128)(2,1)S(1)} %bitcast.33), custom_call_target="tpu_custom_call" | custom-call | flops 3000000000 | bytes 2000000 | tf_op jit(solution)/shard_map/backward/pallas_call | solution.py:466
  48.0 1.4 %collective-permute-done.8 = bf16[2,432,128]{2,1,0:T(8,128)(2,1)S(1)} collective-permute-done((bf16[2,432,128]{2,1,0:T(8,128)(2,1)S(1)}, bf16[2,432,128]{2,1,0:T(8,128)(2,1)S(1)}, u32[]{:S(2)}, u32[]{:S(2)}) %collective-permute-start.8) | collective-permute-done | bytes 221216 | tf_op jit(solution)/shard_map/ppermute | solution.py:381
  49.5 0.1 collective-permute-start.9
  49.7 2.0 %collective-permute-start.12 = (bf16[320,128]{1,0:T(8,128)(2,1)S(1)}, bf16[320,128]{1,0:T(8,128)(2,1)S(1)}, u32[]{:S(2)}, u32[]{:S(2)}) collective-permute-start(bf16[320,128]{1,0:T(8,128)(2,1)S(1)} %pad_maximum_fusion.4), channel_id=1, source_target_pairs={{0,16},{4,20},{8,24},{12,28},{16,0},{20,4},{24,8},{28,12},{32,48},... | collective-permute-start | bytes 245768 | tf_op jit(solution)/shard_map/ppermute | solution.py:373
  51.7 2.8 %collective-permute-start.13 = (bf16[320,128]{1,0:T(8,128)(2,1)S(1)}, bf16[320,128]{1,0:T(8,128)(2,1)S(1)}, u32[]{:S(2)}, u32[]{:S(2)}) collective-permute-start(bf16[320,128]{1,0:T(8,128)(2,1)S(1)} %pad_maximum_fusion.5), channel_id=1, source_target_pairs={{0,112},{4,116},{8,120},{12,124},{16,32},{20,36},{24,40},{28,44},{... | collective-permute-start | bytes 245768 | tf_op jit(solution)/shard_map/ppermute | solution.py:373
  54.5 0.0 collective-permute-done.9
  54.5 0.1 collective-permute-start.10
  54.6 2.4 %backward.6.refs_2_ = f32[256,128]{1,0:T(8,128)S(1)} custom-call(bf16[1024,128]{1,0:T(8,128)(2,1)S(1)} %get-tuple-element.85.grad_ref, s32[27,1024]{1,0:T(8,128)S(1)} %bitcast.48, bf16[27,128,128]{2,1,0:T(8,128)(2,1)S(1)} %bitcast.34), custom_call_target="tpu_custom_call" | custom-call | flops 3000000000 | bytes 2000000 | tf_op jit(solution)/shard_map/backward/pallas_call | solution.py:466
  57.0 0.2 collective-permute-start.15
  57.3 2.5 %collective-permute-done.10 = bf16[432,128]{1,0:T(8,128)(2,1)S(1)} collective-permute-done((bf16[432,128]{1,0:T(8,128)(2,1)S(1)}, bf16[432,128]{1,0:T(8,128)(2,1)S(1)}, u32[]{:S(2)}, u32[]{:S(2)}) %collective-permute-start.10) | collective-permute-done | bytes 110624 | tf_op jit(solution)/shard_map/ppermute | solution.py:381
  59.8 2.2 %collective-permute-start.11 = (bf16[432,128]{1,0:T(8,128)(2,1)S(1)}, bf16[432,128]{1,0:T(8,128)(2,1)S(1)}, u32[]{:S(2)}, u32[]{:S(2)}) collective-permute-start(bf16[432,128]{1,0:T(8,128)(2,1)S(1)} %add_convert_fusion.1), channel_id=1, source_target_pairs={{0,96},{4,100},{8,104},{12,108},{16,112},{20,116},{24,120},{28,124... | collective-permute-start | bytes 331784 | tf_op jit(solution)/shard_map/ppermute | solution.py:381
  62.0 0.0 collective-permute-done.12.iya_ref
  62.0 0.0 collective-permute-done.13.iyb_ref
  62.0 3.0 %returning.1.refs_4_ = f32[1152,128]{1,0:T(8,128)S(1)} custom-call(s32[3]{0:T(128)S(1)} %pad_add_fusion.side_ref, bf16[320,128]{1,0:T(8,128)(2,1)S(1)} %collective-permute-done.6.ixa_ref, bf16[320,128]{1,0:T(8,128)(2,1)S(1)} %collective-permute-done.7.ixb_ref, bf16[320,128]{1,0:T(8,128)(2,1)S(1)} %collective-permute-done.12.iya_ref, ...), custom_call_target="tpu_custom_call" | custom-call | flops 3000000000 | bytes 4000000 | tf_op jit(solution)/shard_map/returning/pallas_call | solution.py:498
  65.0 0.0 collective-permute-done.11
  65.0 1.0 %collective-permute-start.14 = (bf16[432,128]{1,0:T(8,128)(2,1)S(1)}, bf16[432,128]{1,0:T(8,128)(2,1)S(1)}, u32[]{:S(2)}, u32[]{:S(2)}) collective-permute-start(bf16[432,128]{1,0:T(8,128)(2,1)S(1)} %add_convert_fusion.own_ref), channel_id=1, source_target_pairs={{0,32},{4,36},{8,40},{12,44},{16,48},{20,52},{24,56},{28,60},{32,0... | collective-permute-start | bytes 331784 | tf_op jit(solution)/shard_map/ppermute | solution.py:381
  66.0 2.5 %backward.7.refs_3_ = f32[256,128]{1,0:T(8,128)S(1)} custom-call(bf16[1024,128]{1,0:T(8,128)(2,1)S(1)} %get-tuple-element.85.grad_ref, s32[27,1024]{1,0:T(8,128)S(1)} %bitcast.49, bf16[27,128,128]{2,1,0:T(8,128)(2,1)S(1)} %bitcast.36), custom_call_target="tpu_custom_call" | custom-call | flops 3000000000 | bytes 2000000 | tf_op jit(solution)/shard_map/backward/pallas_call | solution.py:466
  68.5 0.5 collective-permute-done.14.one_ref
  69.0 0.2 collective-permute-start.16
  69.2 0.0 collective-permute-done.15.refs_7_
  69.2 1.7 %final.1 = (bf16[1024,128]{1,0:T(8,128)(2,1)}, bf16[1024,128]{1,0:T(8,128)(2,1)}) custom-call(f32[256,128]{1,0:T(8,128)S(1)} %backward.4.refs_0_, f32[256,128]{1,0:T(8,128)S(1)} %backward.5.refs_1_, f32[256,128]{1,0:T(8,128)S(1)} %backward.6.refs_2_, f32[256,128]{1,0:T(8,128)S(1)} %backward.7.refs_3_, f32[1152,128]{1,0:T(8,128)S(1)} %returning.1.refs_4_, ...), custom_call_target="tpu_custom_call" | custom-call | flops 1000000000 | bytes 3000000 | tf_op jit(solution)/shard_map/final/pallas_call | solution.py:511
  70.9 3.0 %collective-permute-done.16.two_ref = bf16[2,432,128]{2,1,0:T(8,128)(2,1)S(1)} collective-permute-done((bf16[2,432,128]{2,1,0:T(8,128)(2,1)S(1)}, bf16[2,432,128]{2,1,0:T(8,128)(2,1)S(1)}, u32[]{:S(2)}, u32[]{:S(2)}) %collective-permute-start.16) | collective-permute-done | bytes 221216 | tf_op jit(solution)/shard_map/ppermute | solution.py:381
  73.9 6.0 %collective-permute-start.17 = (bf16[4,432,128]{2,1,0:T(8,128)(2,1)S(1)}, bf16[4,432,128]{2,1,0:T(8,128)(2,1)S(1)}, u32[]{:S(2)}, u32[]{:S(2)}) collective-permute-start(bf16[4,432,128]{2,1,0:T(8,128)(2,1)S(1)} %pad_maximum_fusion), channel_id=1, source_target_pairs={{0,4},{4,0},{8,12},{12,8},{16,20},{20,16},{24,28},{28,24},{32,36},... | collective-permute-start | bytes 1327112 | tf_op jit(solution)/shard_map/ppermute | solution.py:381
  80.0 0.1 pad_add_fusion.1.bits_ref
  80.0 1.3 %collective-permute-done.17.four_ref = bf16[4,432,128]{2,1,0:T(8,128)(2,1)S(1)} collective-permute-done((bf16[4,432,128]{2,1,0:T(8,128)(2,1)S(1)}, bf16[4,432,128]{2,1,0:T(8,128)(2,1)S(1)}, u32[]{:S(2)}, u32[]{:S(2)}) %collective-permute-start.17) | collective-permute-done | bytes 442400 | tf_op jit(solution)/shard_map/ppermute | solution.py:381
  81.4 1.9 %assemble.1 = f32[8,432,128]{2,1,0:T(8,128)} custom-call(s32[3]{0:T(128)S(1)} %pad_add_fusion.1.bits_ref, bf16[432,128]{1,0:T(8,128)(2,1)S(1)} %add_convert_fusion.own_ref, bf16[432,128]{1,0:T(8,128)(2,1)S(1)} %collective-permute-done.14.one_ref, bf16[2,432,128]{2,1,0:T(8,128)(2,1)S(1)} %collective-permute-done.16.two_ref, ...), custom_call_target="tpu_custom_call" | custom-call | flops 1000000 | bytes 3000000 | tf_op jit(solution)/shard_map/assemble/pallas_call | solution.py:520
  (20 shorter events, 0.3 us)
Async XLA Ops:
  0.6 26.7 %collective-permute-start.4 = (bf16[1024,128]{1,0:T(8,128)(2,1)}, bf16[1024,128]{1,0:T(8,128)(2,1)S(1)}, u32[]{:S(2)}, u32[]{:S(2)}) collective-permute-start(bf16[1024,128]{1,0:T(8,128)(2,1)} %bitcast.37), channel_id=1, source_target_pairs={{0,1},{1,0},{2,3},{3,2},{4,5},{5,4},{6,7},{7,6},{8,9},{9,8},{10,11... | collective-permute-start | bytes 786440 | tf_op jit(solution)/shard_map/ppermute | solution.py:377
  3.6 1.0 %copy-start.2 = (bf16[1,1024,128]{2,1,0:T(8,128)(2,1)S(1)}, bf16[1,1024,128]{2,1,0:T(8,128)(2,1)}, u32[]{:S(2)}) copy-start(bf16[1,1024,128]{2,1,0:T(8,128)(2,1)} %param.6) | copy-start | bytes 786436
  4.6 0.9 %copy-start.4 = (s32[1152,27]{0,1:T(8,128)S(1)}, s32[1152,27]{0,1:T(8,128)}, u32[]{:S(2)}) copy-start(s32[1152,27]{0,1:T(8,128)} %param.10) | copy-start | bytes 373252
  5.5 4.5 %copy-start = (bf16[1,27,128,128]{3,2,1,0:T(8,128)(2,1)S(1)}, bf16[1,27,128,128]{3,2,1,0:T(8,128)(2,1)}, u32[]{:S(2)}) copy-start(bf16[1,27,128,128]{3,2,1,0:T(8,128)(2,1)} %param.7) | copy-start | bytes 2654212
  5.5 4.5 %copy-start.5 = (s32[1024,27]{0,1:T(8,128)S(1)}, s32[1024,27]{0,1:T(8,128)}, u32[]{:S(2)}) copy-start(s32[1024,27]{0,1:T(8,128)} %param.9) | copy-start | bytes 331780
  7.8 8.3 %collective-permute-start = (bf16[384,128]{1,0:T(8,128)(2,1)S(1)}, bf16[384,128]{1,0:T(8,128)(2,1)S(1)}, u32[]{:S(2)}, u32[]{:S(2)}) collective-permute-start(bf16[384,128]{1,0:T(8,128)(2,1)S(1)} %get-tuple-element.49), channel_id=1, source_target_pairs={{0,4},{4,0},{8,12},{12,8},{16,20},{20,16},{24,28},{28,24},{32,36},... | collective-permute-start | bytes 294920 | tf_op jit(solution)/shard_map/ppermute | solution.py:360
  8.8 7.2 %collective-permute-start.1 = (bf16[384,128]{1,0:T(8,128)(2,1)S(1)}, bf16[384,128]{1,0:T(8,128)(2,1)S(1)}, u32[]{:S(2)}, u32[]{:S(2)}) collective-permute-start(bf16[384,128]{1,0:T(8,128)(2,1)S(1)} %get-tuple-element.52), channel_id=1, source_target_pairs={{0,12},{4,8},{8,4},{12,0},{16,28},{20,24},{24,20},{28,16},{32,44},... | collective-permute-start | bytes 294920 | tf_op jit(solution)/shard_map/ppermute | solution.py:360
  10.0 12.9 %copy-start.3 = (bf16[1,1024,128]{2,1,0:T(8,128)(2,1)S(1)}, bf16[1,1024,128]{2,1,0:T(8,128)(2,1)}, u32[]{:S(2)}) copy-start(bf16[1,1024,128]{2,1,0:T(8,128)(2,1)} %param.6) | copy-start | bytes 786436
  14.4 1.7 %copy-start.6 = (bf16[1664,1024]{1,0:T(8,128)(2,1)}, bf16[1664,1024]{1,0:T(8,128)(2,1)S(1)}, u32[]{:S(2)}) copy-start(bf16[1664,1024]{1,0:T(8,128)(2,1)S(1)} %get-tuple-element.61.g_ref) | copy-start | bytes 10223620
  16.1 11.2 %collective-permute-start.2 = (bf16[384,128]{1,0:T(8,128)(2,1)S(1)}, bf16[384,128]{1,0:T(8,128)(2,1)S(1)}, u32[]{:S(2)}, u32[]{:S(2)}) collective-permute-start(bf16[384,128]{1,0:T(8,128)(2,1)S(1)} %pad_maximum_fusion.2), channel_id=1, source_target_pairs={{0,16},{4,20},{8,24},{12,28},{16,0},{20,4},{24,8},{28,12},{32,48},... | collective-permute-start | bytes 294920 | tf_op jit(solution)/shard_map/ppermute | solution.py:373
  18.6 8.7 %copy-start.1 = (bf16[1,1024,128]{2,1,0:T(8,128)(2,1)S(1)}, bf16[1,1024,128]{2,1,0:T(8,128)(2,1)}, u32[]{:S(2)}) copy-start(bf16[1,1024,128]{2,1,0:T(8,128)(2,1)} %param.8) | copy-start | bytes 786436
  18.6 8.7 %collective-permute-start.3 = (bf16[384,128]{1,0:T(8,128)(2,1)S(1)}, bf16[384,128]{1,0:T(8,128)(2,1)S(1)}, u32[]{:S(2)}, u32[]{:S(2)}) collective-permute-start(bf16[384,128]{1,0:T(8,128)(2,1)S(1)} %pad_maximum_fusion.3), channel_id=1, source_target_pairs={{0,112},{4,116},{8,120},{12,124},{16,32},{20,36},{24,40},{28,44},{... | collective-permute-start | bytes 294920 | tf_op jit(solution)/shard_map/ppermute | solution.py:373
  27.3 6.8 %copy-start.7 = (bf16[1664,1024]{1,0:T(8,128)(2,1)S(1)}, bf16[1664,1024]{1,0:T(8,128)(2,1)}, u32[]{:S(2)}) copy-start(bf16[1664,1024]{1,0:T(8,128)(2,1)} %copy-done.6) | copy-start | bytes 10223620
  37.0 2.8 %collective-permute-start.5 = (bf16[1728,128]{1,0:T(8,128)(2,1)S(1)}, bf16[1728,128]{1,0:T(8,128)(2,1)}, u32[]{:S(2)}, u32[]{:S(2)}) collective-permute-start(bf16[1728,128]{1,0:T(8,128)(2,1)S(1)} %get-tuple-element.64), channel_id=1, source_target_pairs={{0,4},{4,0},{8,12},{12,8},{16,20},{20,16},{24,28},{28,24},{32,36},... | collective-permute-start | bytes 1327112 | tf_op jit(solution)/shard_map/ppermute | solution.py:381
  38.2 2.7 %collective-permute-start.6 = (bf16[320,128]{1,0:T(8,128)(2,1)S(1)}, bf16[320,128]{1,0:T(8,128)(2,1)S(1)}, u32[]{:S(2)}, u32[]{:S(2)}) collective-permute-start(bf16[320,128]{1,0:T(8,128)(2,1)S(1)} %get-tuple-element.65), channel_id=1, source_target_pairs={{0,4},{4,0},{8,12},{12,8},{16,20},{20,16},{24,28},{28,24},{32,36},... | collective-permute-start | bytes 245768 | tf_op jit(solution)/shard_map/ppermute | solution.py:360
  38.4 4.4 %collective-permute-start.7 = (bf16[320,128]{1,0:T(8,128)(2,1)S(1)}, bf16[320,128]{1,0:T(8,128)(2,1)S(1)}, u32[]{:S(2)}, u32[]{:S(2)}) collective-permute-start(bf16[320,128]{1,0:T(8,128)(2,1)S(1)} %get-tuple-element.66), channel_id=1, source_target_pairs={{0,12},{4,8},{8,4},{12,0},{16,28},{20,24},{24,20},{28,16},{32,44},... | collective-permute-start | bytes 245768 | tf_op jit(solution)/shard_map/ppermute | solution.py:360
  42.8 6.6 %collective-permute-start.8 = (bf16[2,432,128]{2,1,0:T(8,128)(2,1)S(1)}, bf16[2,432,128]{2,1,0:T(8,128)(2,1)S(1)}, u32[]{:S(2)}, u32[]{:S(2)}) collective-permute-start(bf16[2,432,128]{2,1,0:T(8,128)(2,1)S(1)} %fusion), channel_id=1, source_target_pairs={{0,8},{4,12},{8,0},{12,4},{16,24},{20,28},{24,16},{28,20},{32,40},... | collective-permute-start | bytes 663560 | tf_op jit(solution)/shard_map/ppermute | solution.py:381
  49.5 4.9 %collective-permute-start.9 = (bf16[432,128]{1,0:T(8,128)(2,1)S(1)}, bf16[432,128]{1,0:T(8,128)(2,1)S(1)}, u32[]{:S(2)}, u32[]{:S(2)}) collective-permute-start(bf16[432,128]{1,0:T(8,128)(2,1)S(1)} %fusion.2), channel_id=1, source_target_pairs={{0,32},{4,36},{8,40},{12,44},{16,48},{20,52},{24,56},{28,60},{32,0... | collective-permute-start | bytes 331784 | tf_op jit(solution)/shard_map/ppermute | solution.py:381
  49.7 12.3 %collective-permute-start.12 = (bf16[320,128]{1,0:T(8,128)(2,1)S(1)}, bf16[320,128]{1,0:T(8,128)(2,1)S(1)}, u32[]{:S(2)}, u32[]{:S(2)}) collective-permute-start(bf16[320,128]{1,0:T(8,128)(2,1)S(1)} %pad_maximum_fusion.4), channel_id=1, source_target_pairs={{0,16},{4,20},{8,24},{12,28},{16,0},{20,4},{24,8},{28,12},{32,48},... | collective-permute-start | bytes 245768 | tf_op jit(solution)/shard_map/ppermute | solution.py:373
  51.7 10.3 %collective-permute-start.13 = (bf16[320,128]{1,0:T(8,128)(2,1)S(1)}, bf16[320,128]{1,0:T(8,128)(2,1)S(1)}, u32[]{:S(2)}, u32[]{:S(2)}) collective-permute-start(bf16[320,128]{1,0:T(8,128)(2,1)S(1)} %pad_maximum_fusion.5), channel_id=1, source_target_pairs={{0,112},{4,116},{8,120},{12,124},{16,32},{20,36},{24,40},{28,44},{... | collective-permute-start | bytes 245768 | tf_op jit(solution)/shard_map/ppermute | solution.py:373
  54.5 5.3 %collective-permute-start.10 = (bf16[432,128]{1,0:T(8,128)(2,1)S(1)}, bf16[432,128]{1,0:T(8,128)(2,1)S(1)}, u32[]{:S(2)}, u32[]{:S(2)}) collective-permute-start(bf16[432,128]{1,0:T(8,128)(2,1)S(1)} %fusion.1), channel_id=1, source_target_pairs={{0,24},{4,28},{8,16},{12,20},{16,8},{20,12},{24,0},{28,4},{32,56},... | collective-permute-start | bytes 331784 | tf_op jit(solution)/shard_map/ppermute | solution.py:381
  57.0 12.2 %collective-permute-start.15 = (bf16[1024,128]{1,0:T(8,128)(2,1)S(1)}, bf16[1024,128]{1,0:T(8,128)(2,1)S(1)}, u32[]{:S(2)}, u32[]{:S(2)}) collective-permute-start(bf16[1024,128]{1,0:T(8,128)(2,1)S(1)} %get-tuple-element.89.refs_6_), channel_id=1, source_target_pairs={{0,1},{1,0},{2,3},{3,2},{4,5},{5,4},{6,7},{7,6},{8,9},{9,8},{10,11... | collective-permute-start | bytes 786440 | tf_op jit(solution)/shard_map/ppermute | solution.py:377
  59.8 5.2 %collective-permute-start.11 = (bf16[432,128]{1,0:T(8,128)(2,1)S(1)}, bf16[432,128]{1,0:T(8,128)(2,1)S(1)}, u32[]{:S(2)}, u32[]{:S(2)}) collective-permute-start(bf16[432,128]{1,0:T(8,128)(2,1)S(1)} %add_convert_fusion.1), channel_id=1, source_target_pairs={{0,96},{4,100},{8,104},{12,108},{16,112},{20,116},{24,120},{28,124... | collective-permute-start | bytes 331784 | tf_op jit(solution)/shard_map/ppermute | solution.py:381
  65.0 3.9 %collective-permute-start.14 = (bf16[432,128]{1,0:T(8,128)(2,1)S(1)}, bf16[432,128]{1,0:T(8,128)(2,1)S(1)}, u32[]{:S(2)}, u32[]{:S(2)}) collective-permute-start(bf16[432,128]{1,0:T(8,128)(2,1)S(1)} %add_convert_fusion.own_ref), channel_id=1, source_target_pairs={{0,32},{4,36},{8,40},{12,44},{16,48},{20,52},{24,56},{28,60},{32,0... | collective-permute-start | bytes 331784 | tf_op jit(solution)/shard_map/ppermute | solution.py:381
  69.0 4.9 %collective-permute-start.16 = (bf16[2,432,128]{2,1,0:T(8,128)(2,1)S(1)}, bf16[2,432,128]{2,1,0:T(8,128)(2,1)S(1)}, u32[]{:S(2)}, u32[]{:S(2)}) collective-permute-start(bf16[2,432,128]{2,1,0:T(8,128)(2,1)S(1)} %pad_maximum_fusion.1), channel_id=1, source_target_pairs={{0,8},{4,12},{8,0},{12,4},{16,24},{20,28},{24,16},{28,20},{32,40},... | collective-permute-start | bytes 663560 | tf_op jit(solution)/shard_map/ppermute | solution.py:381
  73.9 7.5 %collective-permute-start.17 = (bf16[4,432,128]{2,1,0:T(8,128)(2,1)S(1)}, bf16[4,432,128]{2,1,0:T(8,128)(2,1)S(1)}, u32[]{:S(2)}, u32[]{:S(2)}) collective-permute-start(bf16[4,432,128]{2,1,0:T(8,128)(2,1)S(1)} %pad_maximum_fusion), channel_id=1, source_target_pairs={{0,4},{4,0},{8,12},{12,8},{16,20},{20,16},{24,28},{28,24},{32,36},... | collective-permute-start | bytes 1327112 | tf_op jit(solution)/shard_map/ppermute | solution.py:381

commit v2 on v1

--- a/solution.py
+++ b/solution.py
@@ -141,7 +141,7 @@
 
 def start_kernel(side_ref, x_ref, rr_ref, sm_ref, xa_ref, xb_ref, ya_ref, yb_ref, face_p_ref, edge_p_ref):
     lists = [None] * 8
-    row = rr_ref[...]
+    row = rr_ref[...].reshape(1, HALO)
     column = column_of(row)
     listed = dot(x_ref[...].astype(F32).T.astype(BF), hot(row, ROWS)).T.astype(BF)
     for place, number in enumerate(FACES):
@@ -230,7 +230,7 @@
     for place, number in enumerate(CORNERS):
         sums[number] = total[place * TZ : (place + 1) * TZ]
 
-    selector = hot(rr_ref[...], ROWS)
+    selector = hot(rr_ref[...].reshape(1, HALO), ROWS)
     both = dot(selector, high_low(jnp.concatenate(sums, 0)))
     pre = pre_ref[...] + both[:, :C] + both[:, C:]
     gate = 1.0 / (1.0 + jnp.exp(-pre))
@@ -314,7 +314,7 @@
 
 def final_kernel(*refs):
     placed_ref, rr_ref, act_ref, pair_ref, mixed_ref, out_ref = refs[-6:]
-    both = dot(hot(rr_ref[...], ROWS), high_low(placed_ref[...]))
+    both = dot(hot(rr_ref[...].reshape(1, HALO), ROWS), high_low(placed_ref[...]))
     both = both[:, :C] + both[:, C:]
     size = ROWS // len(refs[:-6])
     for index, ref in enumerate(refs[:-6]):
@@ -323,11 +323,16 @@
     mixed_ref[...] = (act_ref[...].astype(F32) + pair_ref[...].astype(F32)).astype(BF)
 
 
-def assemble_kernel(bits_ref, own_ref, one_ref, two_ref, four_ref, out_ref):
+def assemble_kernel(bits_ref, low_ref, high_ref, *refs, distances):
+    out_ref, held, sems = refs[-3:]
     place = bits_ref[0] * 4 + bits_ref[1] * 2 + bits_ref[2]
-    blocks = [own_ref[...], one_ref[...]] + [two_ref[i] for i in range(2)] + [four_ref[i] for i in range(4)]
-    for distance, block in enumerate(blocks):
-        out_ref[place ^ distance] = block.astype(F32)
+    copies = []
+    for index, distance in enumerate(distances):
+        held[index] = (low_ref if index < 2 else high_ref)[index % 2].astype(F32)
+        copies.append(pltpu.make_async_copy(held.at[index], out_ref.at[place ^ distance], sems.at[index]))
+        copies[-1].start()
+    for copy in copies:
+        copy.wait()
 
 
 PARAMS = pltpu.CompilerParams(vmem_limit_bytes=30 * 2**20)
@@ -399,7 +404,7 @@
     cot = cotangent[0]
     lm = local_map.T
     sm = send_map.T
-    rr = recv_map.reshape(1, HALO)
+    rr = recv_map
     me = lax.axis_index("space")
     sides = jnp.stack([me % 2, me // TILES_X % 2, me % 2]).astype(jnp.int32)
     smem = pl.BlockSpec(memory_space=pltpu.SMEM)
@@ -507,7 +512,9 @@
     one = xor_send(own, 8)
     locals_.append(backward(3, tie(grad, own)))
     one = tie(one, locals_[3])
-    two = xor_send(jnp.stack([own, one]), 2)
+    pair = jnp.stack([own, one])
+    two = xor_send(pair, 2)
+    cross = xor_send(pair, 1)
     mixed, input_grad = pl.pallas_call(
         final_kernel,
         out_shape=[shape((ROWS, C), BF), shape((ROWS, C), BF)],
@@ -515,17 +522,27 @@
         cost_estimate=cost(1e9, 3e6),
         name="final",
     )(*locals_, tie(placed, one), rr, act, act_pair)
-    two = tie(two, input_grad)
-    four = xor_send(jnp.concatenate([jnp.stack([own, one]), two], 0), 1)
-    weight_grad = pl.pallas_call(
-        assemble_kernel,
-        in_specs=[smem] + [vmem] * 4,
-        out_shape=shape((8,) + own.shape, F32),
-        compiler_params=PARAMS,
-        cost_estimate=cost(1e6, 3e6),
-        name="assemble",
-    )(jnp.stack(bits).astype(jnp.int32), own, one, two, four)
-    return (mixed[None], input_grad[None], weight_grad.reshape(w.shape)[None])
+
+    def assemble(low, high, distances, *before):
+        hbm = pl.BlockSpec(memory_space=pltpu.HBM)
+        return pl.pallas_call(
+            functools.partial(assemble_kernel, distances=distances),
+            in_specs=[smem, vmem, vmem] + [hbm] * len(before),
+            out_specs=hbm,
+            out_shape=shape((8,) + own.shape, F32),
+            input_output_aliases={3: 0} if before else {},
+            scratch_shapes=[pltpu.VMEM((4,) + own.shape, F32), pltpu.SemaphoreType.DMA((4,))],
+            compiler_params=PARAMS,
+            cost_estimate=cost(1e6, 3e6),
+            name="assemble",
+        )(jnp.stack(bits).astype(jnp.int32), low, high, *before)
+
+    near = assemble(pair, cross, (0, 1, 4, 5))
+    two = tie(two, (input_grad, near))
+    far = xor_send(two, 1)
+    weight_grad = assemble(two, far, (2, 3, 6, 7), near)
+    weight_grad = weight_grad.reshape(w.shape)
+    return (mixed[None], input_grad[None], weight_grad[None])
 
 
 def solution(mesh):

time: 83.5 us -> 84.8 us (1.016)
  Pallas kernels: 37 us -> 38 us
    pallas_call x1 -> x2, Pallas kernels: 1.87 us -> 2.99 us  [assemble(): pl.pallas_call(functools.partial(assemble_kernel, distances=distances), i...]
    unnamed x16 -> x20, local copies, waits for them, and re-layouts: 3.58 us -> 4.28 us
    ppermute x8 -> x9, waiting for transfers between devices: 9.63 us -> 10.2 us  [xor_send(): lax.ppermute(value, 'space', [(i, i ^ bits) for i in range(lax.axis_size(...]
    ppermute x8 -> x9, starting transfers between devices: 11.1 us -> 10.6 us  [xor_send(): lax.ppermute(value, 'space', [(i, i ^ bits) for i in range(lax.axis_size(...]
  transfers between devices with their start and end apart: 18 -> 19, of which waited for: 7 -> 8; matrix products, arithmetic and copies ran while one was open for 3% -> 2% of each run, Pallas kernels for 31% -> 32%
where the time goes in v2:
time: 84.8 us; the launch traced here: 84.5 us
  Pallas kernels  38 us (45%)
  starting transfers between devices  27.5 us (32%)
  waiting for transfers between devices  12.2 us (14%)
  local copies, waits for them, and re-layouts  4.34 us (5%)
  other arithmetic  1.44 us (2%)
  between operations  1.1 us (1%)
    ppermute x4, starting transfers between devices, exchange_y(): lax.ppermute(v, 'space', pairing('y', n))  11.6 us
    ppermute x9, starting transfers between devices, xor_send(): lax.ppermute(value, 'space', [(i, i ^ bits) for i in range(lax.axis_size(...  10.6 us
    ppermute x9, waiting for transfers between devices, xor_send(): lax.ppermute(value, 'space', [(i, i ^ bits) for i in range(lax.axis_size(...  10.2 us
    pallas_call x4, Pallas kernels, backward(): pl.pallas_call(functools.partial(backward_kernel, begin=index * size), ou...  9.72 us
    pallas_call x2, Pallas kernels, forward(): pl.pallas_call(functools.partial(forward_kernel, width=512, first=first),...  8.67 us
    pallas_call x1, Pallas kernels, on_device(): pl.pallas_call(activate_kernel, in_specs=[smem] + [vmem] * 9, out_shape=[...  6.77 us
    unnamed x20, local copies, waits for them, and re-layouts  4.28 us
    pallas_call x2, Pallas kernels, assemble(): pl.pallas_call(functools.partial(assemble_kernel, distances=distances), i...  2.99 us
  transfers between devices with their start and end apart: 19, of which 8 were waited for; matrix products, arithmetic and copies ran while one was open for 2% of the time, Pallas kernels for 32%

profile of v2, /device:TPU:1, one launch (start us, length us, event | category | flops | bytes accessed | tf_op | source)
XLA Modules:
  0.0 84.5 jit_solution(926153167476573442)
XLA Ops:
  0.6 2.2 %collective-permute-start.4 = (bf16[1024,128]{1,0:T(8,128)(2,1)}, bf16[1024,128]{1,0:T(8,128)(2,1)S(1)}, u32[]{:S(2)}, u32[]{:S(2)}) collective-permute-start(bf16[1024,128]{1,0:T(8,128)(2,1)} %bitcast.33), channel_id=1, source_target_pairs={{0,1},{1,0},{2,3},{3,2},{4,5},{5,4},{6,7},{7,6},{8,9},{9,8},{10,11... | collective-permute-start | bytes 786440 | tf_op jit(solution)/shard_map/ppermute | solution.py:382
  2.8 0.1 pad_add_fusion.side_ref
  2.9 0.9 %copy-done.2 = bf16[1,1024,128]{2,1,0:T(8,128)(2,1)S(1)} copy-done((bf16[1,1024,128]{2,1,0:T(8,128)(2,1)S(1)}, bf16[1,1024,128]{2,1,0:T(8,128)(2,1)}, u32[]{:S(2)}) %copy-start.2) | copy-done | bytes 262168
  3.9 0.9 %copy-done.4 = s32[1152,27]{0,1:T(8,128)S(1)} copy-done((s32[1152,27]{0,1:T(8,128)S(1)}, s32[1152,27]{0,1:T(8,128)}, u32[]{:S(2)}) %copy-start.4) | copy-done | bytes 124440
  4.8 0.7 copy-done.6
  5.5 2.3 %start.1 = (bf16[384,128]{1,0:T(8,128)(2,1)S(1)}, bf16[384,128]{1,0:T(8,128)(2,1)S(1)}, bf16[288,128]{1,0:T(8,128)(2,1)S(1)}, bf16[288,128]{1,0:T(8,128)(2,1)S(1...) custom-call(s32[3]{0:T(128)S(1)} %pad_add_fusion.side_ref, bf16[1024,128]{1,0:T(8,128)(2,1)S(1)} %bitcast.35, ...), custom_call_target="tpu_custom_call" | custom-call | flops 2000000000 | bytes 4000000 | tf_op jit(solution)/shard_map/start/pallas_call | solution.py:415
  7.8 1.0 %collective-permute-start = (bf16[384,128]{1,0:T(8,128)(2,1)S(1)}, bf16[384,128]{1,0:T(8,128)(2,1)S(1)}, u32[]{:S(2)}, u32[]{:S(2)}) collective-permute-start(bf16[384,128]{1,0:T(8,128)(2,1)S(1)} %get-tuple-element.49), channel_id=1, source_target_pairs={{0,4},{4,0},{8,12},{12,8},{16,20},{20,16},{24,28},{28,24},{32,36},... | collective-permute-start | bytes 294920 | tf_op jit(solution)/shard_map/ppermute | solution.py:365
  8.8 1.2 %collective-permute-start.1 = (bf16[384,128]{1,0:T(8,128)(2,1)S(1)}, bf16[384,128]{1,0:T(8,128)(2,1)S(1)}, u32[]{:S(2)}, u32[]{:S(2)}) collective-permute-start(bf16[384,128]{1,0:T(8,128)(2,1)S(1)} %get-tuple-element.52), channel_id=1, source_target_pairs={{0,12},{4,8},{8,4},{12,0},{16,28},{20,24},{24,20},{28,16},{32,44},... | collective-permute-start | bytes 294920 | tf_op jit(solution)/shard_map/ppermute | solution.py:365
  10.0 0.0 copy-done
  10.0 0.0 copy-done.5
  10.0 4.3 %forward.2 = (bf16[1664,1024]{1,0:T(8,128)(2,1)S(1)}, f32[128,1024]{1,0:T(8,128)S(1)}) custom-call(bf16[1024,128]{1,0:T(8,128)(2,1)S(1)} %bitcast.36, s32[27,1024]{1,0:T(8,128)S(1)} %bitcast.40, bf16[27,128,128]{2,1,0:T(8,128)(2,1)S(1)} %bitcast.25), custom_call_target="tpu_custom_call" | custom-call | flops 7000000000 | bytes 5000000 | tf_op jit(solution)/shard_map/forward/pallas_call | solution.py:427
  14.3 0.0 copy-start.8
  14.3 1.7 %copy-done.8 = bf16[1664,1024]{1,0:T(8,128)(2,1)} copy-done((bf16[1664,1024]{1,0:T(8,128)(2,1)}, bf16[1664,1024]{1,0:T(8,128)(2,1)S(1)}, u32[]{:S(2)}) %copy-start.8) | copy-done | bytes 3407896
  16.0 0.0 collective-permute-done.1.ixb_ref
  16.0 0.0 collective-permute-done.ixa_ref
  16.1 2.5 %collective-permute-start.2 = (bf16[384,128]{1,0:T(8,128)(2,1)S(1)}, bf16[384,128]{1,0:T(8,128)(2,1)S(1)}, u32[]{:S(2)}, u32[]{:S(2)}) collective-permute-start(bf16[384,128]{1,0:T(8,128)(2,1)S(1)} %pad_maximum_fusion.1), channel_id=1, source_target_pairs={{0,16},{4,20},{8,24},{12,28},{16,0},{20,4},{24,8},{28,12},{32,48},... | collective-permute-start | bytes 294920 | tf_op jit(solution)/shard_map/ppermute | solution.py:378
  18.6 0.0 copy-start.7
  18.6 4.3 %collective-permute-start.3 = (bf16[384,128]{1,0:T(8,128)(2,1)S(1)}, bf16[384,128]{1,0:T(8,128)(2,1)S(1)}, u32[]{:S(2)}, u32[]{:S(2)}) collective-permute-start(bf16[384,128]{1,0:T(8,128)(2,1)S(1)} %pad_maximum_fusion.2), channel_id=1, source_target_pairs={{0,112},{4,116},{8,120},{12,124},{16,32},{20,36},{24,40},{28,44},{... | collective-permute-start | bytes 294920 | tf_op jit(solution)/shard_map/ppermute | solution.py:378
  22.9 0.0 copy-done.3
  22.9 4.4 %forward.3 = (bf16[1664,1024]{1,0:T(8,128)(2,1)S(1)}, f32[1024,128]{1,0:T(8,128)S(1)}) custom-call(bf16[1024,128]{1,0:T(8,128)(2,1)S(1)} %bitcast.37, s32[27,1024]{1,0:T(8,128)S(1)} %bitcast.41, bf16[27,128,128]{2,1,0:T(8,128)(2,1)S(1)} %bitcast.26, f32[128,1024]{1,0:T(8,128)S(1)} %get-tuple-element.50.refs_0_), custom_call_target="tpu_custom_call" | custom-call | flops 7000000000 | bytes 5000000 | tf_op jit(solution)/shard_map/forward/pallas_call | solution.py:427
  27.3 0.1 collective-permute-done.3.iyb_ref
  27.3 0.0 collective-permute-done.2.iya_ref
  27.3 0.0 collective-permute-done.4.pair_ref
  27.3 6.8 %activate.1 = (bf16[1024,128]{1,0:T(8,128)(2,1)S(1)}, bf16[1024,128]{1,0:T(8,128)(2,1)S(1)}, bf16[320,128]{1,0:T(8,128)(2,1)S(1)}, bf16[320,128]{1,0:T(8,128)(2,...) custom-call(s32[3]{0:T(128)S(1)} %pad_add_fusion.side_ref, ...), custom_call_target="tpu_custom_call" | custom-call | flops 4000000000 | bytes 3000000 | tf_op jit(solution)/shard_map/activate/pallas_call | solution.py:441
  34.1 1.1 %weight_first.1.first_ref = f32[1792,128]{1,0:T(8,128)S(1)} custom-call(bf16[1664,1024]{1,0:T(8,128)(2,1)S(1)} %copy-done.9, bf16[1024,128]{1,0:T(8,128)(2,1)S(1)} %get-tuple-element.85.grad_ref, bf16[1024,128]{1,0:T(8,128)(2,1)S(1)} %bitcast.38, f32[27,128,128]{2,1,0:T(8,128)S(1)} %get-tuple-element.62.halo_ref), custom_call_target="tpu_custom_call" | custom-call | flops 4000000000 | bytes 5000000 | tf_op jit(solution)/shard_map/weight_first/pallas_call | solution.py:451
  35.3 1.7 %weight_second.1 = (f32[1728,128]{1,0:T(8,128)S(1)}, bf16[1728,128]{1,0:T(8,128)(2,1)S(1)}) custom-call(s32[3]{0:T(128)S(1)} %pad_add_fusion.side_ref, bf16[1664,1024]{1,0:T(8,128)(2,1)S(1)} %get-tuple-element.60.g_ref, bf16[1024,128]{1,0:T(8,128)(2,1)S(1)} %get-tuple-element.85.grad_ref, f32[1792,128]{1,0:T(8,128)S(1)} %weight_first.1.first_ref, ...), custom_call_target="tpu_custom_call" | custom-call | flops 4000000000 | bytes 5000000 | tf_op jit(solution)/shard_map/weight_second/pallas_call | solution.py:458
  37.0 1.2 %collective-permute-start.5 = (bf16[1728,128]{1,0:T(8,128)(2,1)S(1)}, bf16[1728,128]{1,0:T(8,128)(2,1)}, u32[]{:S(2)}, u32[]{:S(2)}) collective-permute-start(bf16[1728,128]{1,0:T(8,128)(2,1)S(1)} %get-tuple-element.64), channel_id=1, source_target_pairs={{0,4},{4,0},{8,12},{12,8},{16,20},{20,16},{24,28},{28,24},{32,36},... | collective-permute-start | bytes 1327112 | tf_op jit(solution)/shard_map/ppermute | solution.py:386
  38.2 0.2 collective-permute-start.6
  38.4 0.5 collective-permute-start.7
  38.9 0.9 %collective-permute-done.5 = bf16[1728,128]{1,0:T(8,128)(2,1)} collective-permute-done((bf16[1728,128]{1,0:T(8,128)(2,1)S(1)}, bf16[1728,128]{1,0:T(8,128)(2,1)}, u32[]{:S(2)}, u32[]{:S(2)}) %collective-permute-start.5) | collective-permute-done | bytes 442400 | tf_op jit(solution)/shard_map/ppermute | solution.py:386
  39.8 1.1 %convert_add_fusion = f32[1728,128]{1,0:T(8,128)S(1)} fusion(f32[1728,128]{1,0:T(8,128)S(1)} %get-tuple-element.63, bf16[1728,128]{1,0:T(8,128)(2,1)} %collective-permute-done.5), kind=kLoop, calls=%fused_computation | loop fusion | flops 442368 | bytes 2211840 | tf_op jit(solution)/shard_map/add | solution.py:485
  40.9 0.0 collective-permute-done.6.ixa_ref
  40.9 1.9 %collective-permute-done.7.ixb_ref = bf16[320,128]{1,0:T(8,128)(2,1)S(1)} collective-permute-done((bf16[320,128]{1,0:T(8,128)(2,1)S(1)}, bf16[320,128]{1,0:T(8,128)(2,1)S(1)}, u32[]{:S(2)}, u32[]{:S(2)}) %collective-permute-start.7) | collective-permute-done | bytes 81952 | tf_op jit(solution)/shard_map/ppermute | solution.py:365
  42.8 0.3 collective-permute-start.8
  43.1 2.4 %backward.4.refs_0_ = f32[256,128]{1,0:T(8,128)S(1)} custom-call(bf16[1024,128]{1,0:T(8,128)(2,1)S(1)} %get-tuple-element.85.grad_ref, s32[27,1024]{1,0:T(8,128)S(1)} %bitcast.42, bf16[27,128,128]{2,1,0:T(8,128)(2,1)S(1)} %bitcast.28), custom_call_target="tpu_custom_call" | custom-call | flops 3000000000 | bytes 2000000 | tf_op jit(solution)/shard_map/backward/pallas_call | solution.py:471
  45.5 2.4 %backward.5.refs_1_ = f32[256,128]{1,0:T(8,128)S(1)} custom-call(bf16[1024,128]{1,0:T(8,128)(2,1)S(1)} %get-tuple-element.85.grad_ref, s32[27,1024]{1,0:T(8,128)S(1)} %bitcast.43, bf16[27,128,128]{2,1,0:T(8,128)(2,1)S(1)} %bitcast.29), custom_call_target="tpu_custom_call" | custom-call | flops 3000000000 | bytes 2000000 | tf_op jit(solution)/shard_map/backward/pallas_call | solution.py:471
  47.9 1.5 %collective-permute-done.8 = bf16[2,432,128]{2,1,0:T(8,128)(2,1)S(1)} collective-permute-done((bf16[2,432,128]{2,1,0:T(8,128)(2,1)S(1)}, bf16[2,432,128]{2,1,0:T(8,128)(2,1)S(1)}, u32[]{:S(2)}, u32[]{:S(2)}) %collective-permute-start.8) | collective-permute-done | bytes 221216 | tf_op jit(solution)/shard_map/ppermute | solution.py:386
  49.5 0.1 collective-permute-start.9
  49.6 2.0 %collective-permute-start.12 = (bf16[320,128]{1,0:T(8,128)(2,1)S(1)}, bf16[320,128]{1,0:T(8,128)(2,1)S(1)}, u32[]{:S(2)}, u32[]{:S(2)}) collective-permute-start(bf16[320,128]{1,0:T(8,128)(2,1)S(1)} %pad_maximum_fusion.3), channel_id=1, source_target_pairs={{0,16},{4,20},{8,24},{12,28},{16,0},{20,4},{24,8},{28,12},{32,48},... | collective-permute-start | bytes 245768 | tf_op jit(solution)/shard_map/ppermute | solution.py:378
  51.7 2.8 %collective-permute-start.13 = (bf16[320,128]{1,0:T(8,128)(2,1)S(1)}, bf16[320,128]{1,0:T(8,128)(2,1)S(1)}, u32[]{:S(2)}, u32[]{:S(2)}) collective-permute-start(bf16[320,128]{1,0:T(8,128)(2,1)S(1)} %pad_maximum_fusion.4), channel_id=1, source_target_pairs={{0,112},{4,116},{8,120},{12,124},{16,32},{20,36},{24,40},{28,44},{... | collective-permute-start | bytes 245768 | tf_op jit(solution)/shard_map/ppermute | solution.py:378
  54.4 0.0 collective-permute-done.9
  54.5 0.1 collective-permute-start.10
  54.6 2.4 %backward.6.refs_2_ = f32[256,128]{1,0:T(8,128)S(1)} custom-call(bf16[1024,128]{1,0:T(8,128)(2,1)S(1)} %get-tuple-element.85.grad_ref, s32[27,1024]{1,0:T(8,128)S(1)} %bitcast.44, bf16[27,128,128]{2,1,0:T(8,128)(2,1)S(1)} %bitcast.30), custom_call_target="tpu_custom_call" | custom-call | flops 3000000000 | bytes 2000000 | tf_op jit(solution)/shard_map/backward/pallas_call | solution.py:471
  57.0 0.3 collective-permute-start.15
  57.3 2.5 %collective-permute-done.10 = bf16[432,128]{1,0:T(8,128)(2,1)S(1)} collective-permute-done((bf16[432,128]{1,0:T(8,128)(2,1)S(1)}, bf16[432,128]{1,0:T(8,128)(2,1)S(1)}, u32[]{:S(2)}, u32[]{:S(2)}) %collective-permute-start.10) | collective-permute-done | bytes 110624 | tf_op jit(solution)/shard_map/ppermute | solution.py:386
  59.8 2.2 %collective-permute-start.11 = (bf16[432,128]{1,0:T(8,128)(2,1)S(1)}, bf16[432,128]{1,0:T(8,128)(2,1)S(1)}, u32[]{:S(2)}, u32[]{:S(2)}) collective-permute-start(bf16[432,128]{1,0:T(8,128)(2,1)S(1)} %add_convert_fusion.1), channel_id=1, source_target_pairs={{0,96},{4,100},{8,104},{12,108},{16,112},{20,116},{24,120},{28,124... | collective-permute-start | bytes 331784 | tf_op jit(solution)/shard_map/ppermute | solution.py:386
  62.0 0.0 collective-permute-done.12.iya_ref
  62.0 0.0 collective-permute-done.13.iyb_ref
  62.0 3.0 %returning.1.refs_4_ = f32[1152,128]{1,0:T(8,128)S(1)} custom-call(s32[3]{0:T(128)S(1)} %pad_add_fusion.side_ref, bf16[320,128]{1,0:T(8,128)(2,1)S(1)} %collective-permute-done.6.ixa_ref, bf16[320,128]{1,0:T(8,128)(2,1)S(1)} %collective-permute-done.7.ixb_ref, bf16[320,128]{1,0:T(8,128)(2,1)S(1)} %collective-permute-done.12.iya_ref, ...), custom_call_target="tpu_custom_call" | custom-call | flops 3000000000 | bytes 4000000 | tf_op jit(solution)/shard_map/returning/pallas_call | solution.py:503
  65.0 0.0 collective-permute-done.11
  65.0 1.0 %collective-permute-start.14 = (bf16[432,128]{1,0:T(8,128)(2,1)S(1)}, bf16[432,128]{1,0:T(8,128)(2,1)S(1)}, u32[]{:S(2)}, u32[]{:S(2)}) collective-permute-start(bf16[432,128]{1,0:T(8,128)(2,1)S(1)} %add_convert_fusion), channel_id=1, source_target_pairs={{0,32},{4,36},{8,40},{12,44},{16,48},{20,52},{24,56},{28,60},{32,0... | collective-permute-start | bytes 331784 | tf_op jit(solution)/shard_map/ppermute | solution.py:386
  66.0 2.4 %backward.7.refs_3_ = f32[256,128]{1,0:T(8,128)S(1)} custom-call(bf16[1024,128]{1,0:T(8,128)(2,1)S(1)} %get-tuple-element.85.grad_ref, s32[27,1024]{1,0:T(8,128)S(1)} %bitcast.45, bf16[27,128,128]{2,1,0:T(8,128)(2,1)S(1)} %bitcast.32), custom_call_target="tpu_custom_call" | custom-call | flops 3000000000 | bytes 2000000 | tf_op jit(solution)/shard_map/backward/pallas_call | solution.py:471
  68.5 0.5 collective-permute-done.14
  69.0 4.9 %collective-permute-start.17 = (bf16[2,432,128]{2,1,0:T(8,128)(2,1)S(1)}, bf16[2,432,128]{2,1,0:T(8,128)(2,1)S(1)}, u32[]{:S(2)}, u32[]{:S(2)}) collective-permute-start(bf16[2,432,128]{2,1,0:T(8,128)(2,1)S(1)} %pad_maximum_fusion.low_ref), channel_id=1, source_target_pairs={{0,4},{4,0},{8,12},{12,8},{16,20},{20,16},{24,28},{28,24},{32,36},... | collective-permute-start | bytes 663560 | tf_op jit(solution)/shard_map/ppermute | solution.py:386
  73.9 0.0 collective-permute-start.16
  73.9 0.1 pad_add_fusion.1.bits_ref
  74.0 0.0 collective-permute-done.15.refs_7_
  74.0 1.7 %final.1 = (bf16[1024,128]{1,0:T(8,128)(2,1)}, bf16[1024,128]{1,0:T(8,128)(2,1)}) custom-call(f32[256,128]{1,0:T(8,128)S(1)} %backward.4.refs_0_, f32[256,128]{1,0:T(8,128)S(1)} %backward.5.refs_1_, f32[256,128]{1,0:T(8,128)S(1)} %backward.6.refs_2_, f32[256,128]{1,0:T(8,128)S(1)} %backward.7.refs_3_, f32[1152,128]{1,0:T(8,128)S(1)} %returning.1.refs_4_, ...), custom_call_target="tpu_custom_call" | custom-call | flops 1000000000 | bytes 3000000 | tf_op jit(solution)/shard_map/final/pallas_call | solution.py:518
  75.7 0.0 collective-permute-done.17.high_ref
  75.7 1.5 %assemble.2.refs_0_ = f32[8,432,128]{2,1,0:T(8,128)} custom-call(s32[3]{0:T(128)S(1)} %pad_add_fusion.1.bits_ref, bf16[2,432,128]{2,1,0:T(8,128)(2,1)S(1)} %pad_maximum_fusion.low_ref, bf16[2,432,128]{2,1,0:T(8,128)(2,1)S(1)} %collective-permute-done.17.high_ref), custom_call_target="tpu_custom_call" | custom-call | flops 1000000 | bytes 3000000 | tf_op jit(solution)/shard_map/assemble/pallas_call | solution.py:528
  77.2 3.7 %collective-permute-done.16.low_ref = bf16[2,432,128]{2,1,0:T(8,128)(2,1)S(1)} collective-permute-done((bf16[2,432,128]{2,1,0:T(8,128)(2,1)S(1)}, bf16[2,432,128]{2,1,0:T(8,128)(2,1)S(1)}, u32[]{:S(2)}, u32[]{:S(2)}) %collective-permute-start.16) | collective-permute-done | bytes 221216 | tf_op jit(solution)/shard_map/ppermute | solution.py:386
  80.9 0.9 %collective-permute-start.18 = (bf16[2,432,128]{2,1,0:T(8,128)(2,1)S(1)}, bf16[2,432,128]{2,1,0:T(8,128)(2,1)S(1)}, u32[]{:S(2)}, u32[]{:S(2)}) collective-permute-start(bf16[2,432,128]{2,1,0:T(8,128)(2,1)S(1)} %collective-permute-done.16.low_ref), channel_id=1, source_target_pairs={{0,4},{4,0},{8,12},{12,8},{16,20},{20,16},{24,28},{28,24},{32,36},... | collective-permute-start | bytes 663560 | tf_op jit(solution)/shard_map/ppermute | solution.py:386
  81.7 1.1 %collective-permute-done.18.high_ref = bf16[2,432,128]{2,1,0:T(8,128)(2,1)S(1)} collective-permute-done((bf16[2,432,128]{2,1,0:T(8,128)(2,1)S(1)}, bf16[2,432,128]{2,1,0:T(8,128)(2,1)S(1)}, u32[]{:S(2)}, u32[]{:S(2)}) %collective-permute-start.18) | collective-permute-done | bytes 221216 | tf_op jit(solution)/shard_map/ppermute | solution.py:386
  82.8 1.5 %assemble.3 = f32[8,432,128]{2,1,0:T(8,128)} custom-call(s32[3]{0:T(128)S(1)} %pad_add_fusion.1.bits_ref, bf16[2,432,128]{2,1,0:T(8,128)(2,1)S(1)} %collective-permute-done.16.low_ref, bf16[2,432,128]{2,1,0:T(8,128)(2,1)S(1)} %collective-permute-done.18.high_ref, f32[8,432,128]{2,1,0:T(8,128)} %assemble.2.refs_0_), custom_call_target="tpu_custom_call", output_to_operand_aliasing={{}: (3, {})} | custom-call | flops 1000000 | bytes 3000000 | tf_op jit(solution)/shard_map/assemble/pallas_call | solution.py:528
  (25 shorter events, 0.3 us)
Async XLA Ops:
  0.6 26.7 %collective-permute-start.4 = (bf16[1024,128]{1,0:T(8,128)(2,1)}, bf16[1024,128]{1,0:T(8,128)(2,1)S(1)}, u32[]{:S(2)}, u32[]{:S(2)}) collective-permute-start(bf16[1024,128]{1,0:T(8,128)(2,1)} %bitcast.33), channel_id=1, source_target_pairs={{0,1},{1,0},{2,3},{3,2},{4,5},{5,4},{6,7},{7,6},{8,9},{9,8},{10,11... | collective-permute-start | bytes 786440 | tf_op jit(solution)/shard_map/ppermute | solution.py:382
  2.9 1.0 %copy-start.2 = (bf16[1,1024,128]{2,1,0:T(8,128)(2,1)S(1)}, bf16[1,1024,128]{2,1,0:T(8,128)(2,1)}, u32[]{:S(2)}) copy-start(bf16[1,1024,128]{2,1,0:T(8,128)(2,1)} %param.6) | copy-start | bytes 786436
  3.9 0.9 %copy-start.4 = (s32[1152,27]{0,1:T(8,128)S(1)}, s32[1152,27]{0,1:T(8,128)}, u32[]{:S(2)}) copy-start(s32[1152,27]{0,1:T(8,128)} %param.10) | copy-start | bytes 373252
  4.8 0.7 copy-start.6
  5.5 4.5 %copy-start = (bf16[1,27,128,128]{3,2,1,0:T(8,128)(2,1)S(1)}, bf16[1,27,128,128]{3,2,1,0:T(8,128)(2,1)}, u32[]{:S(2)}) copy-start(bf16[1,27,128,128]{3,2,1,0:T(8,128)(2,1)} %param.7) | copy-start | bytes 2654212
  5.5 4.5 %copy-start.5 = (s32[1024,27]{0,1:T(8,128)S(1)}, s32[1024,27]{0,1:T(8,128)}, u32[]{:S(2)}) copy-start(s32[1024,27]{0,1:T(8,128)} %param.9) | copy-start | bytes 331780
  7.8 8.3 %collective-permute-start = (bf16[384,128]{1,0:T(8,128)(2,1)S(1)}, bf16[384,128]{1,0:T(8,128)(2,1)S(1)}, u32[]{:S(2)}, u32[]{:S(2)}) collective-permute-start(bf16[384,128]{1,0:T(8,128)(2,1)S(1)} %get-tuple-element.49), channel_id=1, source_target_pairs={{0,4},{4,0},{8,12},{12,8},{16,20},{20,16},{24,28},{28,24},{32,36},... | collective-permute-start | bytes 294920 | tf_op jit(solution)/shard_map/ppermute | solution.py:365
  8.8 7.2 %collective-permute-start.1 = (bf16[384,128]{1,0:T(8,128)(2,1)S(1)}, bf16[384,128]{1,0:T(8,128)(2,1)S(1)}, u32[]{:S(2)}, u32[]{:S(2)}) collective-permute-start(bf16[384,128]{1,0:T(8,128)(2,1)S(1)} %get-tuple-element.52), channel_id=1, source_target_pairs={{0,12},{4,8},{8,4},{12,0},{16,28},{20,24},{24,20},{28,16},{32,44},... | collective-permute-start | bytes 294920 | tf_op jit(solution)/shard_map/ppermute | solution.py:365
  10.0 12.9 %copy-start.3 = (bf16[1,1024,128]{2,1,0:T(8,128)(2,1)S(1)}, bf16[1,1024,128]{2,1,0:T(8,128)(2,1)}, u32[]{:S(2)}) copy-start(bf16[1,1024,128]{2,1,0:T(8,128)(2,1)} %param.6) | copy-start | bytes 786436
  14.3 1.7 %copy-start.8 = (bf16[1664,1024]{1,0:T(8,128)(2,1)}, bf16[1664,1024]{1,0:T(8,128)(2,1)S(1)}, u32[]{:S(2)}) copy-start(bf16[1664,1024]{1,0:T(8,128)(2,1)S(1)} %get-tuple-element.61.g_ref) | copy-start | bytes 10223620
  16.1 11.3 %collective-permute-start.2 = (bf16[384,128]{1,0:T(8,128)(2,1)S(1)}, bf16[384,128]{1,0:T(8,128)(2,1)S(1)}, u32[]{:S(2)}, u32[]{:S(2)}) collective-permute-start(bf16[384,128]{1,0:T(8,128)(2,1)S(1)} %pad_maximum_fusion.1), channel_id=1, source_target_pairs={{0,16},{4,20},{8,24},{12,28},{16,0},{20,4},{24,8},{28,12},{32,48},... | collective-permute-start | bytes 294920 | tf_op jit(solution)/shard_map/ppermute | solution.py:378
  18.6 8.7 %copy-start.1 = (bf16[1,1024,128]{2,1,0:T(8,128)(2,1)S(1)}, bf16[1,1024,128]{2,1,0:T(8,128)(2,1)}, u32[]{:S(2)}) copy-start(bf16[1,1024,128]{2,1,0:T(8,128)(2,1)} %param.8) | copy-start | bytes 786436
  18.6 8.7 %copy-start.7 = (s32[1152]{0:T(1024)S(1)}, s32[1152]{0:T(1024)}, u32[]{:S(2)}) copy-start(s32[1152]{0:T(1024)} %refs_5_.1) | copy-start | bytes 13828
  18.6 8.7 %collective-permute-start.3 = (bf16[384,128]{1,0:T(8,128)(2,1)S(1)}, bf16[384,128]{1,0:T(8,128)(2,1)S(1)}, u32[]{:S(2)}, u32[]{:S(2)}) collective-permute-start(bf16[384,128]{1,0:T(8,128)(2,1)S(1)} %pad_maximum_fusion.2), channel_id=1, source_target_pairs={{0,112},{4,116},{8,120},{12,124},{16,32},{20,36},{24,40},{28,44},{... | collective-permute-start | bytes 294920 | tf_op jit(solution)/shard_map/ppermute | solution.py:378
  27.3 6.8 %copy-start.9 = (bf16[1664,1024]{1,0:T(8,128)(2,1)S(1)}, bf16[1664,1024]{1,0:T(8,128)(2,1)}, u32[]{:S(2)}) copy-start(bf16[1664,1024]{1,0:T(8,128)(2,1)} %copy-done.8) | copy-start | bytes 10223620
  37.0 2.8 %collective-permute-start.5 = (bf16[1728,128]{1,0:T(8,128)(2,1)S(1)}, bf16[1728,128]{1,0:T(8,128)(2,1)}, u32[]{:S(2)}, u32[]{:S(2)}) collective-permute-start(bf16[1728,128]{1,0:T(8,128)(2,1)S(1)} %get-tuple-element.64), channel_id=1, source_target_pairs={{0,4},{4,0},{8,12},{12,8},{16,20},{20,16},{24,28},{28,24},{32,36},... | collective-permute-start | bytes 1327112 | tf_op jit(solution)/shard_map/ppermute | solution.py:386
  38.2 2.7 %collective-permute-start.6 = (bf16[320,128]{1,0:T(8,128)(2,1)S(1)}, bf16[320,128]{1,0:T(8,128)(2,1)S(1)}, u32[]{:S(2)}, u32[]{:S(2)}) collective-permute-start(bf16[320,128]{1,0:T(8,128)(2,1)S(1)} %get-tuple-element.65), channel_id=1, source_target_pairs={{0,4},{4,0},{8,12},{12,8},{16,20},{20,16},{24,28},{28,24},{32,36},... | collective-permute-start | bytes 245768 | tf_op jit(solution)/shard_map/ppermute | solution.py:365
  38.4 4.4 %collective-permute-start.7 = (bf16[320,128]{1,0:T(8,128)(2,1)S(1)}, bf16[320,128]{1,0:T(8,128)(2,1)S(1)}, u32[]{:S(2)}, u32[]{:S(2)}) collective-permute-start(bf16[320,128]{1,0:T(8,128)(2,1)S(1)} %get-tuple-element.66), channel_id=1, source_target_pairs={{0,12},{4,8},{8,4},{12,0},{16,28},{20,24},{24,20},{28,16},{32,44},... | collective-permute-start | bytes 245768 | tf_op jit(solution)/shard_map/ppermute | solution.py:365
  42.8 6.6 %collective-permute-start.8 = (bf16[2,432,128]{2,1,0:T(8,128)(2,1)S(1)}, bf16[2,432,128]{2,1,0:T(8,128)(2,1)S(1)}, u32[]{:S(2)}, u32[]{:S(2)}) collective-permute-start(bf16[2,432,128]{2,1,0:T(8,128)(2,1)S(1)} %fusion), channel_id=1, source_target_pairs={{0,8},{4,12},{8,0},{12,4},{16,24},{20,28},{24,16},{28,20},{32,40},... | collective-permute-start | bytes 663560 | tf_op jit(solution)/shard_map/ppermute | solution.py:386
  49.5 4.9 %collective-permute-start.9 = (bf16[432,128]{1,0:T(8,128)(2,1)S(1)}, bf16[432,128]{1,0:T(8,128)(2,1)S(1)}, u32[]{:S(2)}, u32[]{:S(2)}) collective-permute-start(bf16[432,128]{1,0:T(8,128)(2,1)S(1)} %fusion.2), channel_id=1, source_target_pairs={{0,32},{4,36},{8,40},{12,44},{16,48},{20,52},{24,56},{28,60},{32,0... | collective-permute-start | bytes 331784 | tf_op jit(solution)/shard_map/ppermute | solution.py:386
  49.6 12.3 %collective-permute-start.12 = (bf16[320,128]{1,0:T(8,128)(2,1)S(1)}, bf16[320,128]{1,0:T(8,128)(2,1)S(1)}, u32[]{:S(2)}, u32[]{:S(2)}) collective-permute-start(bf16[320,128]{1,0:T(8,128)(2,1)S(1)} %pad_maximum_fusion.3), channel_id=1, source_target_pairs={{0,16},{4,20},{8,24},{12,28},{16,0},{20,4},{24,8},{28,12},{32,48},... | collective-permute-start | bytes 245768 | tf_op jit(solution)/shard_map/ppermute | solution.py:378
  51.7 10.3 %collective-permute-start.13 = (bf16[320,128]{1,0:T(8,128)(2,1)S(1)}, bf16[320,128]{1,0:T(8,128)(2,1)S(1)}, u32[]{:S(2)}, u32[]{:S(2)}) collective-permute-start(bf16[320,128]{1,0:T(8,128)(2,1)S(1)} %pad_maximum_fusion.4), channel_id=1, source_target_pairs={{0,112},{4,116},{8,120},{12,124},{16,32},{20,36},{24,40},{28,44},{... | collective-permute-start | bytes 245768 | tf_op jit(solution)/shard_map/ppermute | solution.py:378
  54.5 5.3 %collective-permute-start.10 = (bf16[432,128]{1,0:T(8,128)(2,1)S(1)}, bf16[432,128]{1,0:T(8,128)(2,1)S(1)}, u32[]{:S(2)}, u32[]{:S(2)}) collective-permute-start(bf16[432,128]{1,0:T(8,128)(2,1)S(1)} %fusion.1), channel_id=1, source_target_pairs={{0,24},{4,28},{8,16},{12,20},{16,8},{20,12},{24,0},{28,4},{32,56},... | collective-permute-start | bytes 331784 | tf_op jit(solution)/shard_map/ppermute | solution.py:386
  57.0 17.0 %collective-permute-start.15 = (bf16[1024,128]{1,0:T(8,128)(2,1)S(1)}, bf16[1024,128]{1,0:T(8,128)(2,1)S(1)}, u32[]{:S(2)}, u32[]{:S(2)}) collective-permute-start(bf16[1024,128]{1,0:T(8,128)(2,1)S(1)} %get-tuple-element.89.refs_6_), channel_id=1, source_target_pairs={{0,1},{1,0},{2,3},{3,2},{4,5},{5,4},{6,7},{7,6},{8,9},{9,8},{10,11... | collective-permute-start | bytes 786440 | tf_op jit(solution)/shard_map/ppermute | solution.py:382
  59.8 5.2 %collective-permute-start.11 = (bf16[432,128]{1,0:T(8,128)(2,1)S(1)}, bf16[432,128]{1,0:T(8,128)(2,1)S(1)}, u32[]{:S(2)}, u32[]{:S(2)}) collective-permute-start(bf16[432,128]{1,0:T(8,128)(2,1)S(1)} %add_convert_fusion.1), channel_id=1, source_target_pairs={{0,96},{4,100},{8,104},{12,108},{16,112},{20,116},{24,120},{28,124... | collective-permute-start | bytes 331784 | tf_op jit(solution)/shard_map/ppermute | solution.py:386
  65.0 3.9 %collective-permute-start.14 = (bf16[432,128]{1,0:T(8,128)(2,1)S(1)}, bf16[432,128]{1,0:T(8,128)(2,1)S(1)}, u32[]{:S(2)}, u32[]{:S(2)}) collective-permute-start(bf16[432,128]{1,0:T(8,128)(2,1)S(1)} %add_convert_fusion), channel_id=1, source_target_pairs={{0,32},{4,36},{8,40},{12,44},{16,48},{20,52},{24,56},{28,60},{32,0... | collective-permute-start | bytes 331784 | tf_op jit(solution)/shard_map/ppermute | solution.py:386
  69.0 6.7 %collective-permute-start.17 = (bf16[2,432,128]{2,1,0:T(8,128)(2,1)S(1)}, bf16[2,432,128]{2,1,0:T(8,128)(2,1)S(1)}, u32[]{:S(2)}, u32[]{:S(2)}) collective-permute-start(bf16[2,432,128]{2,1,0:T(8,128)(2,1)S(1)} %pad_maximum_fusion.low_ref), channel_id=1, source_target_pairs={{0,4},{4,0},{8,12},{12,8},{16,20},{20,16},{24,28},{28,24},{32,36},... | collective-permute-start | bytes 663560 | tf_op jit(solution)/shard_map/ppermute | solution.py:386
  73.9 7.0 %collective-permute-start.16 = (bf16[2,432,128]{2,1,0:T(8,128)(2,1)S(1)}, bf16[2,432,128]{2,1,0:T(8,128)(2,1)S(1)}, u32[]{:S(2)}, u32[]{:S(2)}) collective-permute-start(bf16[2,432,128]{2,1,0:T(8,128)(2,1)S(1)} %pad_maximum_fusion.low_ref), channel_id=1, source_target_pairs={{0,8},{4,12},{8,0},{12,4},{16,24},{20,28},{24,16},{28,20},{32,40},... | collective-permute-start | bytes 663560 | tf_op jit(solution)/shard_map/ppermute | solution.py:386
  80.9 2.0 %collective-permute-start.18 = (bf16[2,432,128]{2,1,0:T(8,128)(2,1)S(1)}, bf16[2,432,128]{2,1,0:T(8,128)(2,1)S(1)}, u32[]{:S(2)}, u32[]{:S(2)}) collective-permute-start(bf16[2,432,128]{2,1,0:T(8,128)(2,1)S(1)} %collective-permute-done.16.low_ref), channel_id=1, source_target_pairs={{0,4},{4,0},{8,12},{12,8},{16,20},{20,16},{24,28},{28,24},{32,36},... | collective-permute-start | bytes 663560 | tf_op jit(solution)/shard_map/ppermute | solution.py:386

commit v3 on v1

--- a/solution.py
+++ b/solution.py
@@ -442,7 +442,6 @@
         name="activate",
     )(sides, pre, *in_x, *in_y, rr, cot, cot_pair, w)
     half = 27 * C // 2
-    in_x = exchange_x(xa, xb)
     first = pl.pallas_call(
         weight_first_kernel,
         out_shape=shape((14 * C, C), F32),
@@ -482,16 +481,16 @@
     locals_ = []
     got = xor_send(sent, 1)
     kept, sent = halve(plus(kept, got).reshape(2, 2, -1, C), 1)
-    sent, in_x = lax.optimization_barrier((sent, in_x))
     got = xor_send(sent, 2)
+    act_pair = swapped(tie(act, sent))
     locals_.append(backward(0, tie(grad, sent)))
     locals_.append(backward(1, tie(grad, locals_[0])))
     kept, sent = halve(plus(kept, tie(got, locals_[1])), 2)
     got = xor_send(sent, 8)
-    in_y = exchange_y(second_phase(*[tie(v, sent) for v in (ya, yb, *in_x)], sides, CAP, TZ))
+    in_x = exchange_x(tie(xa, sent), tie(xb, sent))
     own = plus(kept, got).astype(BF)
     got = xor_send(own, 6)
-    act_pair = swapped(tie(act, own))
+    in_y = exchange_y(second_phase(*[tie(v, own) for v in (ya, yb, *in_x)], sides, CAP, TZ))
     locals_.append(backward(2, tie(grad, own)))
     own = plus(own, tie(got, locals_[2])).astype(BF)
     got = xor_send(own, 24)

time: 83.5 us -> 84.5 us (1.012)
  waiting for transfers between devices: 11.6 us -> 13.5 us
  starting transfers between devices: 28 us -> 27 us
    ppermute x8, starting transfers between devices: 11.1 us -> 8.95 us  [xor_send(): lax.ppermute(value, 'space', [(i, i ^ bits) for i in range(lax.axis_size(...]
    ppermute x4, waiting for transfers between devices: 0.05 us -> 1.27 us  [exchange_y(): lax.ppermute(v, 'space', pairing('y', n))]
    ppermute x4, starting transfers between devices: 2.88 us -> 3.85 us  [exchange_x(): lax.ppermute(v, 'space', pairing('x', n))]
  transfers between devices with their start and end apart: 18 -> 18, of which waited for: 7 -> 8; matrix products, arithmetic and copies ran while one was open for 3% -> 1% of each run, Pallas kernels for 31% -> 30%
where the time goes in v3:
time: 84.5 us; the launch traced here: 84.2 us
  Pallas kernels  37 us (44%)
  starting transfers between devices  27 us (32%)
  waiting for transfers between devices  13.5 us (16%)
  local copies, waits for them, and re-layouts  4.34 us (5%)
  other arithmetic  1.49 us (2%)
  between operations  0.9 us (1%)
    ppermute x4, starting transfers between devices, exchange_y(): lax.ppermute(v, 'space', pairing('y', n))  11.8 us
    ppermute x8, waiting for transfers between devices, xor_send(): lax.ppermute(value, 'space', [(i, i ^ bits) for i in range(lax.axis_size(...  10.3 us
    pallas_call x4, Pallas kernels, backward(): pl.pallas_call(functools.partial(backward_kernel, begin=index * size), ou...  9.79 us
    ppermute x8, starting transfers between devices, xor_send(): lax.ppermute(value, 'space', [(i, i ^ bits) for i in range(lax.axis_size(...  8.95 us
    pallas_call x2, Pallas kernels, forward(): pl.pallas_call(functools.partial(forward_kernel, width=512, first=first),...  8.7 us
    pallas_call x1, Pallas kernels, on_device(): pl.pallas_call(activate_kernel, in_specs=[smem] + [vmem] * 9, out_shape=[...  6.77 us
    ppermute x4, starting transfers between devices, exchange_x(): lax.ppermute(v, 'space', pairing('x', n))  3.85 us
    unnamed x16, local copies, waits for them, and re-layouts  3.58 us
  transfers between devices with their start and end apart: 18, of which 8 were waited for; matrix products, arithmetic and copies ran while one was open for 1% of the time, Pallas kernels for 30%

profile of v3, /device:TPU:1, one launch (start us, length us, event | category | flops | bytes accessed | tf_op | source)
XLA Modules:
  0.0 84.2 jit_solution(13851297041953737284)
XLA Ops:
  0.6 2.2 %collective-permute-start.4 = (bf16[1024,128]{1,0:T(8,128)(2,1)}, bf16[1024,128]{1,0:T(8,128)(2,1)S(1)}, u32[]{:S(2)}, u32[]{:S(2)}) collective-permute-start(bf16[1024,128]{1,0:T(8,128)(2,1)} %bitcast.37), channel_id=1, source_target_pairs={{0,1},{1,0},{2,3},{3,2},{4,5},{5,4},{6,7},{7,6},{8,9},{9,8},{10,11... | collective-permute-start | bytes 786440 | tf_op jit(solution)/shard_map/ppermute | solution.py:377
  2.8 0.7 reshape.14.rr_ref.refs_5_
  3.5 0.1 pad_add_fusion.side_ref
  3.6 0.0 copy-start.2
  3.6 0.9 %copy-done.2 = bf16[1,1024,128]{2,1,0:T(8,128)(2,1)S(1)} copy-done((bf16[1,1024,128]{2,1,0:T(8,128)(2,1)S(1)}, bf16[1,1024,128]{2,1,0:T(8,128)(2,1)}, u32[]{:S(2)}) %copy-start.2) | copy-done | bytes 262168
  4.6 0.0 copy-start.4
  4.6 0.9 %copy-done.4 = s32[1152,27]{0,1:T(8,128)S(1)} copy-done((s32[1152,27]{0,1:T(8,128)S(1)}, s32[1152,27]{0,1:T(8,128)}, u32[]{:S(2)}) %copy-start.4) | copy-done | bytes 124440
  5.5 2.3 %start.1 = (bf16[384,128]{1,0:T(8,128)(2,1)S(1)}, bf16[384,128]{1,0:T(8,128)(2,1)S(1)}, bf16[288,128]{1,0:T(8,128)(2,1)S(1)}, bf16[288,128]{1,0:T(8,128)(2,1)S(1...) custom-call(s32[3]{0:T(128)S(1)} %pad_add_fusion.side_ref, bf16[1024,128]{1,0:T(8,128)(2,1)S(1)} %bitcast.39, ...), custom_call_target="tpu_custom_call" | custom-call | flops 2000000000 | bytes 4000000 | tf_op jit(solution)/shard_map/start/pallas_call | solution.py:410
  7.8 1.0 %collective-permute-start = (bf16[384,128]{1,0:T(8,128)(2,1)S(1)}, bf16[384,128]{1,0:T(8,128)(2,1)S(1)}, u32[]{:S(2)}, u32[]{:S(2)}) collective-permute-start(bf16[384,128]{1,0:T(8,128)(2,1)S(1)} %get-tuple-element.48), channel_id=1, source_target_pairs={{0,4},{4,0},{8,12},{12,8},{16,20},{20,16},{24,28},{28,24},{32,36},... | collective-permute-start | bytes 294920 | tf_op jit(solution)/shard_map/ppermute | solution.py:360
  8.8 1.2 %collective-permute-start.1 = (bf16[384,128]{1,0:T(8,128)(2,1)S(1)}, bf16[384,128]{1,0:T(8,128)(2,1)S(1)}, u32[]{:S(2)}, u32[]{:S(2)}) collective-permute-start(bf16[384,128]{1,0:T(8,128)(2,1)S(1)} %get-tuple-element.51), channel_id=1, source_target_pairs={{0,12},{4,8},{8,4},{12,0},{16,28},{20,24},{24,20},{28,16},{32,44},... | collective-permute-start | bytes 294920 | tf_op jit(solution)/shard_map/ppermute | solution.py:360
  10.0 0.0 copy-done
  10.0 0.0 copy-done.5
  10.0 4.3 %forward.2 = (bf16[1664,1024]{1,0:T(8,128)(2,1)S(1)}, f32[128,1024]{1,0:T(8,128)S(1)}) custom-call(bf16[1024,128]{1,0:T(8,128)(2,1)S(1)} %bitcast.40, s32[27,1024]{1,0:T(8,128)S(1)} %bitcast.44, bf16[27,128,128]{2,1,0:T(8,128)(2,1)S(1)} %bitcast.29), custom_call_target="tpu_custom_call" | custom-call | flops 7000000000 | bytes 5000000 | tf_op jit(solution)/shard_map/forward/pallas_call | solution.py:422
  14.4 0.0 copy-start.6
  14.4 1.7 %copy-done.6 = bf16[1664,1024]{1,0:T(8,128)(2,1)} copy-done((bf16[1664,1024]{1,0:T(8,128)(2,1)}, bf16[1664,1024]{1,0:T(8,128)(2,1)S(1)}, u32[]{:S(2)}) %copy-start.6) | copy-done | bytes 3407896
  16.1 0.0 collective-permute-done.1.ixb_ref
  16.1 0.0 collective-permute-done.ixa_ref
  16.1 2.5 %collective-permute-start.2 = (bf16[384,128]{1,0:T(8,128)(2,1)S(1)}, bf16[384,128]{1,0:T(8,128)(2,1)S(1)}, u32[]{:S(2)}, u32[]{:S(2)}) collective-permute-start(bf16[384,128]{1,0:T(8,128)(2,1)S(1)} %pad_maximum_fusion.2), channel_id=1, source_target_pairs={{0,16},{4,20},{8,24},{12,28},{16,0},{20,4},{24,8},{28,12},{32,48},... | collective-permute-start | bytes 294920 | tf_op jit(solution)/shard_map/ppermute | solution.py:373
  18.6 4.3 %collective-permute-start.3 = (bf16[384,128]{1,0:T(8,128)(2,1)S(1)}, bf16[384,128]{1,0:T(8,128)(2,1)S(1)}, u32[]{:S(2)}, u32[]{:S(2)}) collective-permute-start(bf16[384,128]{1,0:T(8,128)(2,1)S(1)} %pad_maximum_fusion.3), channel_id=1, source_target_pairs={{0,112},{4,116},{8,120},{12,124},{16,32},{20,36},{24,40},{28,44},{... | collective-permute-start | bytes 294920 | tf_op jit(solution)/shard_map/ppermute | solution.py:373
  22.9 0.0 copy-done.3
  22.9 4.4 %forward.3 = (bf16[1664,1024]{1,0:T(8,128)(2,1)S(1)}, f32[1024,128]{1,0:T(8,128)S(1)}) custom-call(bf16[1024,128]{1,0:T(8,128)(2,1)S(1)} %bitcast.41, s32[27,1024]{1,0:T(8,128)S(1)} %bitcast.45, bf16[27,128,128]{2,1,0:T(8,128)(2,1)S(1)} %bitcast.30, f32[128,1024]{1,0:T(8,128)S(1)} %get-tuple-element.49.refs_0_), custom_call_target="tpu_custom_call" | custom-call | flops 7000000000 | bytes 5000000 | tf_op jit(solution)/shard_map/forward/pallas_call | solution.py:422
  27.3 0.0 collective-permute-done.3.iyb_ref
  27.3 0.0 collective-permute-done.2.iya_ref
  27.3 0.0 collective-permute-done.4.pair_ref
  27.3 0.0 copy-done.1
  27.3 6.8 %activate.1 = (bf16[1024,128]{1,0:T(8,128)(2,1)S(1)}, bf16[1024,128]{1,0:T(8,128)(2,1)S(1)}, bf16[320,128]{1,0:T(8,128)(2,1)S(1)}, bf16[320,128]{1,0:T(8,128)(2,...) custom-call(s32[3]{0:T(128)S(1)} %pad_add_fusion.side_ref, ...), custom_call_target="tpu_custom_call" | custom-call | flops 4000000000 | bytes 3000000 | tf_op jit(solution)/shard_map/activate/pallas_call | solution.py:436
  34.1 0.0 copy-done.7
  34.1 1.1 %weight_first.1.first_ref = f32[1792,128]{1,0:T(8,128)S(1)} custom-call(bf16[1664,1024]{1,0:T(8,128)(2,1)S(1)} %copy-done.7, bf16[1024,128]{1,0:T(8,128)(2,1)S(1)} %get-tuple-element.83.grad_ref, bf16[1024,128]{1,0:T(8,128)(2,1)S(1)} %bitcast.42, f32[27,128,128]{2,1,0:T(8,128)S(1)} %get-tuple-element.61.halo_ref), custom_call_target="tpu_custom_call" | custom-call | flops 4000000000 | bytes 5000000 | tf_op jit(solution)/shard_map/weight_first/pallas_call | solution.py:445
  35.3 1.7 %weight_second.1 = (f32[1728,128]{1,0:T(8,128)S(1)}, bf16[1728,128]{1,0:T(8,128)(2,1)S(1)}) custom-call(s32[3]{0:T(128)S(1)} %pad_add_fusion.side_ref, bf16[1664,1024]{1,0:T(8,128)(2,1)S(1)} %get-tuple-element.59.g_ref, bf16[1024,128]{1,0:T(8,128)(2,1)S(1)} %get-tuple-element.83.grad_ref, f32[1792,128]{1,0:T(8,128)S(1)} %weight_first.1.first_ref, ...), custom_call_target="tpu_custom_call" | custom-call | flops 4000000000 | bytes 5000000 | tf_op jit(solution)/shard_map/weight_second/pallas_call | solution.py:452
  37.0 1.2 %collective-permute-start.5 = (bf16[1728,128]{1,0:T(8,128)(2,1)S(1)}, bf16[1728,128]{1,0:T(8,128)(2,1)}, u32[]{:S(2)}, u32[]{:S(2)}) collective-permute-start(bf16[1728,128]{1,0:T(8,128)(2,1)S(1)} %get-tuple-element.63), channel_id=1, source_target_pairs={{0,4},{4,0},{8,12},{12,8},{16,20},{20,16},{24,28},{28,24},{32,36},... | collective-permute-start | bytes 1327112 | tf_op jit(solution)/shard_map/ppermute | solution.py:381
  38.2 1.6 %collective-permute-done.5 = bf16[1728,128]{1,0:T(8,128)(2,1)} collective-permute-done((bf16[1728,128]{1,0:T(8,128)(2,1)S(1)}, bf16[1728,128]{1,0:T(8,128)(2,1)}, u32[]{:S(2)}, u32[]{:S(2)}) %collective-permute-start.5) | collective-permute-done | bytes 442400 | tf_op jit(solution)/shard_map/ppermute | solution.py:381
  39.8 1.1 %convert_add_fusion = f32[1728,128]{1,0:T(8,128)S(1)} fusion(f32[1728,128]{1,0:T(8,128)S(1)} %get-tuple-element.62, bf16[1728,128]{1,0:T(8,128)(2,1)} %collective-permute-done.5), kind=kLoop, calls=%fused_computation | loop fusion | flops 442368 | bytes 2211840 | tf_op jit(solution)/shard_map/add | solution.py:479
  40.9 0.6 collective-permute-start.6
  41.5 2.4 %backward.4.refs_0_ = f32[256,128]{1,0:T(8,128)S(1)} custom-call(bf16[1024,128]{1,0:T(8,128)(2,1)S(1)} %get-tuple-element.83.grad_ref, s32[27,1024]{1,0:T(8,128)S(1)} %bitcast.46, bf16[27,128,128]{2,1,0:T(8,128)(2,1)S(1)} %bitcast.32), custom_call_target="tpu_custom_call" | custom-call | flops 3000000000 | bytes 2000000 | tf_op jit(solution)/shard_map/backward/pallas_call | solution.py:465
  43.9 2.4 %backward.5.refs_1_ = f32[256,128]{1,0:T(8,128)S(1)} custom-call(bf16[1024,128]{1,0:T(8,128)(2,1)S(1)} %get-tuple-element.83.grad_ref, s32[27,1024]{1,0:T(8,128)S(1)} %bitcast.47, bf16[27,128,128]{2,1,0:T(8,128)(2,1)S(1)} %bitcast.33), custom_call_target="tpu_custom_call" | custom-call | flops 3000000000 | bytes 2000000 | tf_op jit(solution)/shard_map/backward/pallas_call | solution.py:465
  46.4 1.5 %collective-permute-done.6 = bf16[2,432,128]{2,1,0:T(8,128)(2,1)S(1)} collective-permute-done((bf16[2,432,128]{2,1,0:T(8,128)(2,1)S(1)}, bf16[2,432,128]{2,1,0:T(8,128)(2,1)S(1)}, u32[]{:S(2)}, u32[]{:S(2)}) %collective-permute-start.6) | collective-permute-done | bytes 221216 | tf_op jit(solution)/shard_map/ppermute | solution.py:381
  47.9 0.1 collective-permute-start.7
  48.0 0.2 collective-permute-start.15
  48.3 1.5 %collective-permute-start.10 = (bf16[320,128]{1,0:T(8,128)(2,1)S(1)}, bf16[320,128]{1,0:T(8,128)(2,1)S(1)}, u32[]{:S(2)}, u32[]{:S(2)}) collective-permute-start(bf16[320,128]{1,0:T(8,128)(2,1)S(1)} %get-tuple-element.70), channel_id=1, source_target_pairs={{0,4},{4,0},{8,12},{12,8},{16,20},{20,16},{24,28},{28,24},{32,36},... | collective-permute-start | bytes 245768 | tf_op jit(solution)/shard_map/ppermute | solution.py:360
  49.8 0.1 collective-permute-start.11
  49.9 1.7 %collective-permute-done.7 = bf16[432,128]{1,0:T(8,128)(2,1)S(1)} collective-permute-done((bf16[432,128]{1,0:T(8,128)(2,1)S(1)}, bf16[432,128]{1,0:T(8,128)(2,1)S(1)}, u32[]{:S(2)}, u32[]{:S(2)}) %collective-permute-start.7) | collective-permute-done | bytes 110624 | tf_op jit(solution)/shard_map/ppermute | solution.py:381
  51.7 0.6 collective-permute-start.8
  52.2 1.9 %collective-permute-done.11.ixb_ref = bf16[320,128]{1,0:T(8,128)(2,1)S(1)} collective-permute-done((bf16[320,128]{1,0:T(8,128)(2,1)S(1)}, bf16[320,128]{1,0:T(8,128)(2,1)S(1)}, u32[]{:S(2)}, u32[]{:S(2)}) %collective-permute-start.11) | collective-permute-done | bytes 81952 | tf_op jit(solution)/shard_map/ppermute | solution.py:360
  54.1 0.0 collective-permute-done.10.ixa_ref
  54.2 2.2 %collective-permute-start.12 = (bf16[320,128]{1,0:T(8,128)(2,1)S(1)}, bf16[320,128]{1,0:T(8,128)(2,1)S(1)}, u32[]{:S(2)}, u32[]{:S(2)}) collective-permute-start(bf16[320,128]{1,0:T(8,128)(2,1)S(1)} %pad_maximum_fusion.4), channel_id=1, source_target_pairs={{0,16},{4,20},{8,24},{12,28},{16,0},{20,4},{24,8},{28,12},{32,48},... | collective-permute-start | bytes 245768 | tf_op jit(solution)/shard_map/ppermute | solution.py:373
  56.4 2.8 %collective-permute-start.13 = (bf16[320,128]{1,0:T(8,128)(2,1)S(1)}, bf16[320,128]{1,0:T(8,128)(2,1)S(1)}, u32[]{:S(2)}, u32[]{:S(2)}) collective-permute-start(bf16[320,128]{1,0:T(8,128)(2,1)S(1)} %pad_maximum_fusion.5), channel_id=1, source_target_pairs={{0,112},{4,116},{8,120},{12,124},{16,32},{20,36},{24,40},{28,44},{... | collective-permute-start | bytes 245768 | tf_op jit(solution)/shard_map/ppermute | solution.py:373
  59.2 2.4 %backward.6.refs_2_ = f32[256,128]{1,0:T(8,128)S(1)} custom-call(bf16[1024,128]{1,0:T(8,128)(2,1)S(1)} %get-tuple-element.83.grad_ref, s32[27,1024]{1,0:T(8,128)S(1)} %bitcast.48, bf16[27,128,128]{2,1,0:T(8,128)(2,1)S(1)} %bitcast.34), custom_call_target="tpu_custom_call" | custom-call | flops 3000000000 | bytes 2000000 | tf_op jit(solution)/shard_map/backward/pallas_call | solution.py:465
  61.6 0.0 collective-permute-done.8
  61.7 1.4 %collective-permute-start.9 = (bf16[432,128]{1,0:T(8,128)(2,1)S(1)}, bf16[432,128]{1,0:T(8,128)(2,1)S(1)}, u32[]{:S(2)}, u32[]{:S(2)}) collective-permute-start(bf16[432,128]{1,0:T(8,128)(2,1)S(1)} %add_convert_fusion.1), channel_id=1, source_target_pairs={{0,96},{4,100},{8,104},{12,108},{16,112},{20,116},{24,120},{28,124... | collective-permute-start | bytes 331784 | tf_op jit(solution)/shard_map/ppermute | solution.py:381
  63.1 0.0 collective-permute-done.12.iya_ref
  63.1 1.2 %collective-permute-done.13.iyb_ref = bf16[320,128]{1,0:T(8,128)(2,1)S(1)} collective-permute-done((bf16[320,128]{1,0:T(8,128)(2,1)S(1)}, bf16[320,128]{1,0:T(8,128)(2,1)S(1)}, u32[]{:S(2)}, u32[]{:S(2)}) %collective-permute-start.13) | collective-permute-done | bytes 81952 | tf_op jit(solution)/shard_map/ppermute | solution.py:373
  64.3 3.0 %returning.1.refs_4_ = f32[1152,128]{1,0:T(8,128)S(1)} custom-call(s32[3]{0:T(128)S(1)} %pad_add_fusion.side_ref, bf16[320,128]{1,0:T(8,128)(2,1)S(1)} %collective-permute-done.10.ixa_ref, bf16[320,128]{1,0:T(8,128)(2,1)S(1)} %collective-permute-done.11.ixb_ref, bf16[320,128]{1,0:T(8,128)(2,1)S(1)} %collective-permute-done.12.iya_ref, ...), custom_call_target="tpu_custom_call" | custom-call | flops 3000000000 | bytes 4000000 | tf_op jit(solution)/shard_map/returning/pallas_call | solution.py:497
  67.3 0.0 collective-permute-done.9
  67.4 0.3 collective-permute-start.14
  67.7 2.5 %backward.7.refs_3_ = f32[256,128]{1,0:T(8,128)S(1)} custom-call(bf16[1024,128]{1,0:T(8,128)(2,1)S(1)} %get-tuple-element.83.grad_ref, s32[27,1024]{1,0:T(8,128)S(1)} %bitcast.49, bf16[27,128,128]{2,1,0:T(8,128)(2,1)S(1)} %bitcast.36), custom_call_target="tpu_custom_call" | custom-call | flops 3000000000 | bytes 2000000 | tf_op jit(solution)/shard_map/backward/pallas_call | solution.py:465
  70.2 1.1 %collective-permute-done.14.one_ref = bf16[432,128]{1,0:T(8,128)(2,1)S(1)} collective-permute-done((bf16[432,128]{1,0:T(8,128)(2,1)S(1)}, bf16[432,128]{1,0:T(8,128)(2,1)S(1)}, u32[]{:S(2)}, u32[]{:S(2)}) %collective-permute-start.14) | collective-permute-done | bytes 110624 | tf_op jit(solution)/shard_map/ppermute | solution.py:381
  71.3 0.1 collective-permute-start.16
  71.4 0.0 collective-permute-done.15.refs_7_
  71.4 1.7 %final.1 = (bf16[1024,128]{1,0:T(8,128)(2,1)}, bf16[1024,128]{1,0:T(8,128)(2,1)}) custom-call(f32[256,128]{1,0:T(8,128)S(1)} %backward.4.refs_0_, f32[256,128]{1,0:T(8,128)S(1)} %backward.5.refs_1_, f32[256,128]{1,0:T(8,128)S(1)} %backward.6.refs_2_, f32[256,128]{1,0:T(8,128)S(1)} %backward.7.refs_3_, f32[1152,128]{1,0:T(8,128)S(1)} %returning.1.refs_4_, ...), custom_call_target="tpu_custom_call" | custom-call | flops 1000000000 | bytes 3000000 | tf_op jit(solution)/shard_map/final/pallas_call | solution.py:510
  73.1 3.1 %collective-permute-done.16.two_ref = bf16[2,432,128]{2,1,0:T(8,128)(2,1)S(1)} collective-permute-done((bf16[2,432,128]{2,1,0:T(8,128)(2,1)S(1)}, bf16[2,432,128]{2,1,0:T(8,128)(2,1)S(1)}, u32[]{:S(2)}, u32[]{:S(2)}) %collective-permute-start.16) | collective-permute-done | bytes 221216 | tf_op jit(solution)/shard_map/ppermute | solution.py:381
  76.2 4.7 %collective-permute-start.17 = (bf16[4,432,128]{2,1,0:T(8,128)(2,1)S(1)}, bf16[4,432,128]{2,1,0:T(8,128)(2,1)S(1)}, u32[]{:S(2)}, u32[]{:S(2)}) collective-permute-start(bf16[4,432,128]{2,1,0:T(8,128)(2,1)S(1)} %pad_maximum_fusion), channel_id=1, source_target_pairs={{0,4},{4,0},{8,12},{12,8},{16,20},{20,16},{24,28},{28,24},{32,36},... | collective-permute-start | bytes 1327112 | tf_op jit(solution)/shard_map/ppermute | solution.py:381
  80.9 0.1 pad_add_fusion.1.bits_ref
  81.0 1.3 %collective-permute-done.17.four_ref = bf16[4,432,128]{2,1,0:T(8,128)(2,1)S(1)} collective-permute-done((bf16[4,432,128]{2,1,0:T(8,128)(2,1)S(1)}, bf16[4,432,128]{2,1,0:T(8,128)(2,1)S(1)}, u32[]{:S(2)}, u32[]{:S(2)}) %collective-permute-start.17) | collective-permute-done | bytes 442400 | tf_op jit(solution)/shard_map/ppermute | solution.py:381
  82.3 1.9 %assemble.1 = f32[8,432,128]{2,1,0:T(8,128)} custom-call(s32[3]{0:T(128)S(1)} %pad_add_fusion.1.bits_ref, bf16[432,128]{1,0:T(8,128)(2,1)S(1)} %add_convert_fusion.own_ref, bf16[432,128]{1,0:T(8,128)(2,1)S(1)} %collective-permute-done.14.one_ref, bf16[2,432,128]{2,1,0:T(8,128)(2,1)S(1)} %collective-permute-done.16.two_ref, ...), custom_call_target="tpu_custom_call" | custom-call | flops 1000000 | bytes 3000000 | tf_op jit(solution)/shard_map/assemble/pallas_call | solution.py:519
  (20 shorter events, 0.3 us)
Async XLA Ops:
  0.6 26.7 %collective-permute-start.4 = (bf16[1024,128]{1,0:T(8,128)(2,1)}, bf16[1024,128]{1,0:T(8,128)(2,1)S(1)}, u32[]{:S(2)}, u32[]{:S(2)}) collective-permute-start(bf16[1024,128]{1,0:T(8,128)(2,1)} %bitcast.37), channel_id=1, source_target_pairs={{0,1},{1,0},{2,3},{3,2},{4,5},{5,4},{6,7},{7,6},{8,9},{9,8},{10,11... | collective-permute-start | bytes 786440 | tf_op jit(solution)/shard_map/ppermute | solution.py:377
  3.6 1.0 %copy-start.2 = (bf16[1,1024,128]{2,1,0:T(8,128)(2,1)S(1)}, bf16[1,1024,128]{2,1,0:T(8,128)(2,1)}, u32[]{:S(2)}) copy-start(bf16[1,1024,128]{2,1,0:T(8,128)(2,1)} %param.6) | copy-start | bytes 786436
  4.6 0.9 %copy-start.4 = (s32[1152,27]{0,1:T(8,128)S(1)}, s32[1152,27]{0,1:T(8,128)}, u32[]{:S(2)}) copy-start(s32[1152,27]{0,1:T(8,128)} %param.10) | copy-start | bytes 373252
  5.5 4.5 %copy-start = (bf16[1,27,128,128]{3,2,1,0:T(8,128)(2,1)S(1)}, bf16[1,27,128,128]{3,2,1,0:T(8,128)(2,1)}, u32[]{:S(2)}) copy-start(bf16[1,27,128,128]{3,2,1,0:T(8,128)(2,1)} %param.7) | copy-start | bytes 2654212
  5.5 4.5 %copy-start.5 = (s32[1024,27]{0,1:T(8,128)S(1)}, s32[1024,27]{0,1:T(8,128)}, u32[]{:S(2)}) copy-start(s32[1024,27]{0,1:T(8,128)} %param.9) | copy-start | bytes 331780
  7.8 8.3 %collective-permute-start = (bf16[384,128]{1,0:T(8,128)(2,1)S(1)}, bf16[384,128]{1,0:T(8,128)(2,1)S(1)}, u32[]{:S(2)}, u32[]{:S(2)}) collective-permute-start(bf16[384,128]{1,0:T(8,128)(2,1)S(1)} %get-tuple-element.48), channel_id=1, source_target_pairs={{0,4},{4,0},{8,12},{12,8},{16,20},{20,16},{24,28},{28,24},{32,36},... | collective-permute-start | bytes 294920 | tf_op jit(solution)/shard_map/ppermute | solution.py:360
  8.8 7.2 %collective-permute-start.1 = (bf16[384,128]{1,0:T(8,128)(2,1)S(1)}, bf16[384,128]{1,0:T(8,128)(2,1)S(1)}, u32[]{:S(2)}, u32[]{:S(2)}) collective-permute-start(bf16[384,128]{1,0:T(8,128)(2,1)S(1)} %get-tuple-element.51), channel_id=1, source_target_pairs={{0,12},{4,8},{8,4},{12,0},{16,28},{20,24},{24,20},{28,16},{32,44},... | collective-permute-start | bytes 294920 | tf_op jit(solution)/shard_map/ppermute | solution.py:360
  10.0 12.9 %copy-start.3 = (bf16[1,1024,128]{2,1,0:T(8,128)(2,1)S(1)}, bf16[1,1024,128]{2,1,0:T(8,128)(2,1)}, u32[]{:S(2)}) copy-start(bf16[1,1024,128]{2,1,0:T(8,128)(2,1)} %param.6) | copy-start | bytes 786436
  14.4 1.7 %copy-start.6 = (bf16[1664,1024]{1,0:T(8,128)(2,1)}, bf16[1664,1024]{1,0:T(8,128)(2,1)S(1)}, u32[]{:S(2)}) copy-start(bf16[1664,1024]{1,0:T(8,128)(2,1)S(1)} %get-tuple-element.60.g_ref) | copy-start | bytes 10223620
  16.1 11.2 %collective-permute-start.2 = (bf16[384,128]{1,0:T(8,128)(2,1)S(1)}, bf16[384,128]{1,0:T(8,128)(2,1)S(1)}, u32[]{:S(2)}, u32[]{:S(2)}) collective-permute-start(bf16[384,128]{1,0:T(8,128)(2,1)S(1)} %pad_maximum_fusion.2), channel_id=1, source_target_pairs={{0,16},{4,20},{8,24},{12,28},{16,0},{20,4},{24,8},{28,12},{32,48},... | collective-permute-start | bytes 294920 | tf_op jit(solution)/shard_map/ppermute | solution.py:373
  18.6 8.7 %copy-start.1 = (bf16[1,1024,128]{2,1,0:T(8,128)(2,1)S(1)}, bf16[1,1024,128]{2,1,0:T(8,128)(2,1)}, u32[]{:S(2)}) copy-start(bf16[1,1024,128]{2,1,0:T(8,128)(2,1)} %param.8) | copy-start | bytes 786436
  18.6 8.7 %collective-permute-start.3 = (bf16[384,128]{1,0:T(8,128)(2,1)S(1)}, bf16[384,128]{1,0:T(8,128)(2,1)S(1)}, u32[]{:S(2)}, u32[]{:S(2)}) collective-permute-start(bf16[384,128]{1,0:T(8,128)(2,1)S(1)} %pad_maximum_fusion.3), channel_id=1, source_target_pairs={{0,112},{4,116},{8,120},{12,124},{16,32},{20,36},{24,40},{28,44},{... | collective-permute-start | bytes 294920 | tf_op jit(solution)/shard_map/ppermute | solution.py:373
  27.3 6.8 %copy-start.7 = (bf16[1664,1024]{1,0:T(8,128)(2,1)S(1)}, bf16[1664,1024]{1,0:T(8,128)(2,1)}, u32[]{:S(2)}) copy-start(bf16[1664,1024]{1,0:T(8,128)(2,1)} %copy-done.6) | copy-start | bytes 10223620
  37.0 2.8 %collective-permute-start.5 = (bf16[1728,128]{1,0:T(8,128)(2,1)S(1)}, bf16[1728,128]{1,0:T(8,128)(2,1)}, u32[]{:S(2)}, u32[]{:S(2)}) collective-permute-start(bf16[1728,128]{1,0:T(8,128)(2,1)S(1)} %get-tuple-element.63), channel_id=1, source_target_pairs={{0,4},{4,0},{8,12},{12,8},{16,20},{20,16},{24,28},{28,24},{32,36},... | collective-permute-start | bytes 1327112 | tf_op jit(solution)/shard_map/ppermute | solution.py:381
  40.9 6.9 %collective-permute-start.6 = (bf16[2,432,128]{2,1,0:T(8,128)(2,1)S(1)}, bf16[2,432,128]{2,1,0:T(8,128)(2,1)S(1)}, u32[]{:S(2)}, u32[]{:S(2)}) collective-permute-start(bf16[2,432,128]{2,1,0:T(8,128)(2,1)S(1)} %fusion), channel_id=1, source_target_pairs={{0,8},{4,12},{8,0},{12,4},{16,24},{20,28},{24,16},{28,20},{32,40},... | collective-permute-start | bytes 663560 | tf_op jit(solution)/shard_map/ppermute | solution.py:381
  47.9 3.7 %collective-permute-start.7 = (bf16[432,128]{1,0:T(8,128)(2,1)S(1)}, bf16[432,128]{1,0:T(8,128)(2,1)S(1)}, u32[]{:S(2)}, u32[]{:S(2)}) collective-permute-start(bf16[432,128]{1,0:T(8,128)(2,1)S(1)} %fusion.2), channel_id=1, source_target_pairs={{0,32},{4,36},{8,40},{12,44},{16,48},{20,52},{24,56},{28,60},{32,0... | collective-permute-start | bytes 331784 | tf_op jit(solution)/shard_map/ppermute | solution.py:381
  48.0 23.4 %collective-permute-start.15 = (bf16[1024,128]{1,0:T(8,128)(2,1)S(1)}, bf16[1024,128]{1,0:T(8,128)(2,1)S(1)}, u32[]{:S(2)}, u32[]{:S(2)}) collective-permute-start(bf16[1024,128]{1,0:T(8,128)(2,1)S(1)} %get-tuple-element.87.refs_6_), channel_id=1, source_target_pairs={{0,1},{1,0},{2,3},{3,2},{4,5},{5,4},{6,7},{7,6},{8,9},{9,8},{10,11... | collective-permute-start | bytes 786440 | tf_op jit(solution)/shard_map/ppermute | solution.py:377
  48.3 5.8 %collective-permute-start.10 = (bf16[320,128]{1,0:T(8,128)(2,1)S(1)}, bf16[320,128]{1,0:T(8,128)(2,1)S(1)}, u32[]{:S(2)}, u32[]{:S(2)}) collective-permute-start(bf16[320,128]{1,0:T(8,128)(2,1)S(1)} %get-tuple-element.70), channel_id=1, source_target_pairs={{0,4},{4,0},{8,12},{12,8},{16,20},{20,16},{24,28},{28,24},{32,36},... | collective-permute-start | bytes 245768 | tf_op jit(solution)/shard_map/ppermute | solution.py:360
  49.8 4.4 %collective-permute-start.11 = (bf16[320,128]{1,0:T(8,128)(2,1)S(1)}, bf16[320,128]{1,0:T(8,128)(2,1)S(1)}, u32[]{:S(2)}, u32[]{:S(2)}) collective-permute-start(bf16[320,128]{1,0:T(8,128)(2,1)S(1)} %get-tuple-element.72), channel_id=1, source_target_pairs={{0,12},{4,8},{8,4},{12,0},{16,28},{20,24},{24,20},{28,16},{32,44},... | collective-permute-start | bytes 245768 | tf_op jit(solution)/shard_map/ppermute | solution.py:360
  51.7 10.0 %collective-permute-start.8 = (bf16[432,128]{1,0:T(8,128)(2,1)S(1)}, bf16[432,128]{1,0:T(8,128)(2,1)S(1)}, u32[]{:S(2)}, u32[]{:S(2)}) collective-permute-start(bf16[432,128]{1,0:T(8,128)(2,1)S(1)} %fusion.1), channel_id=1, source_target_pairs={{0,24},{4,28},{8,16},{12,20},{16,8},{20,12},{24,0},{28,4},{32,56},... | collective-permute-start | bytes 331784 | tf_op jit(solution)/shard_map/ppermute | solution.py:381
  54.2 8.9 %collective-permute-start.12 = (bf16[320,128]{1,0:T(8,128)(2,1)S(1)}, bf16[320,128]{1,0:T(8,128)(2,1)S(1)}, u32[]{:S(2)}, u32[]{:S(2)}) collective-permute-start(bf16[320,128]{1,0:T(8,128)(2,1)S(1)} %pad_maximum_fusion.4), channel_id=1, source_target_pairs={{0,16},{4,20},{8,24},{12,28},{16,0},{20,4},{24,8},{28,12},{32,48},... | collective-permute-start | bytes 245768 | tf_op jit(solution)/shard_map/ppermute | solution.py:373
  56.4 7.9 %collective-permute-start.13 = (bf16[320,128]{1,0:T(8,128)(2,1)S(1)}, bf16[320,128]{1,0:T(8,128)(2,1)S(1)}, u32[]{:S(2)}, u32[]{:S(2)}) collective-permute-start(bf16[320,128]{1,0:T(8,128)(2,1)S(1)} %pad_maximum_fusion.5), channel_id=1, source_target_pairs={{0,112},{4,116},{8,120},{12,124},{16,32},{20,36},{24,40},{28,44},{... | collective-permute-start | bytes 245768 | tf_op jit(solution)/shard_map/ppermute | solution.py:373
  61.7 5.6 %collective-permute-start.9 = (bf16[432,128]{1,0:T(8,128)(2,1)S(1)}, bf16[432,128]{1,0:T(8,128)(2,1)S(1)}, u32[]{:S(2)}, u32[]{:S(2)}) collective-permute-start(bf16[432,128]{1,0:T(8,128)(2,1)S(1)} %add_convert_fusion.1), channel_id=1, source_target_pairs={{0,96},{4,100},{8,104},{12,108},{16,112},{20,116},{24,120},{28,124... | collective-permute-start | bytes 331784 | tf_op jit(solution)/shard_map/ppermute | solution.py:381
  67.4 3.9 %collective-permute-start.14 = (bf16[432,128]{1,0:T(8,128)(2,1)S(1)}, bf16[432,128]{1,0:T(8,128)(2,1)S(1)}, u32[]{:S(2)}, u32[]{:S(2)}) collective-permute-start(bf16[432,128]{1,0:T(8,128)(2,1)S(1)} %add_convert_fusion.own_ref), channel_id=1, source_target_pairs={{0,32},{4,36},{8,40},{12,44},{16,48},{20,52},{24,56},{28,60},{32,0... | collective-permute-start | bytes 331784 | tf_op jit(solution)/shard_map/ppermute | solution.py:381
  71.3 4.9 %collective-permute-start.16 = (bf16[2,432,128]{2,1,0:T(8,128)(2,1)S(1)}, bf16[2,432,128]{2,1,0:T(8,128)(2,1)S(1)}, u32[]{:S(2)}, u32[]{:S(2)}) collective-permute-start(bf16[2,432,128]{2,1,0:T(8,128)(2,1)S(1)} %pad_maximum_fusion.1), channel_id=1, source_target_pairs={{0,8},{4,12},{8,0},{12,4},{16,24},{20,28},{24,16},{28,20},{32,40},... | collective-permute-start | bytes 663560 | tf_op jit(solution)/shard_map/ppermute | solution.py:381
  76.2 6.1 %collective-permute-start.17 = (bf16[4,432,128]{2,1,0:T(8,128)(2,1)S(1)}, bf16[4,432,128]{2,1,0:T(8,128)(2,1)S(1)}, u32[]{:S(2)}, u32[]{:S(2)}) collective-permute-start(bf16[4,432,128]{2,1,0:T(8,128)(2,1)S(1)} %pad_maximum_fusion), channel_id=1, source_target_pairs={{0,4},{4,0},{8,12},{12,8},{16,20},{20,16},{24,28},{28,24},{32,36},... | collective-permute-start | bytes 1327112 | tf_op jit(solution)/shard_map/ppermute | solution.py:381

commit v4 on v1

--- a/solution.py
+++ b/solution.py
@@ -473,20 +473,21 @@
 
     bits = [me % 2, (me // 2 + me // 4) % 2, (me // 8 + me // 16) % 2]
 
-    def halve(blocks, stage):
-        return pick(blocks, bits[stage]), pick(blocks, 1 - bits[stage]).astype(BF)
+    def halve(one, two, stage):
+        kept, sent = [plus(pick(one, at), pick(two, at)) for at in (bits[stage], 1 - bits[stage])]
+        return kept, sent.astype(BF)
 
     def plus(one, two):
         return one.astype(F32) + two.astype(F32)
 
     locals_ = []
     got = xor_send(sent, 1)
-    kept, sent = halve(plus(kept, got).reshape(2, 2, -1, C), 1)
+    kept, sent = halve(kept.reshape(2, 2, -1, C), got.reshape(2, 2, -1, C), 1)
     sent, in_x = lax.optimization_barrier((sent, in_x))
     got = xor_send(sent, 2)
     locals_.append(backward(0, tie(grad, sent)))
     locals_.append(backward(1, tie(grad, locals_[0])))
-    kept, sent = halve(plus(kept, tie(got, locals_[1])), 2)
+    kept, sent = halve(kept, tie(got, locals_[1]), 2)
     got = xor_send(sent, 8)
     in_y = exchange_y(second_phase(*[tie(v, sent) for v in (ya, yb, *in_x)], sides, CAP, TZ))
     own = plus(kept, got).astype(BF)

time: 83.5 us -> 83.5 us (level)
  no operation moved by 1% of the time
where the time goes in v4:
time: 83.5 us; the launch traced here: 83.2 us
  Pallas kernels  37 us (44%)
  starting transfers between devices  28 us (34%)
  waiting for transfers between devices  11.6 us (14%)
  local copies, waits for them, and re-layouts  4.27 us (5%)
  other arithmetic  1.54 us (2%)
  between operations  0.86 us (1%)
    ppermute x4, starting transfers between devices, exchange_y(): lax.ppermute(v, 'space', pairing('y', n))  11.6 us
    ppermute x8, starting transfers between devices, xor_send(): lax.ppermute(value, 'space', [(i, i ^ bits) for i in range(lax.axis_size(...  11.1 us
    pallas_call x4, Pallas kernels, backward(): pl.pallas_call(functools.partial(backward_kernel, begin=index * size), ou...  9.79 us
    ppermute x8, waiting for transfers between devices, xor_send(): lax.ppermute(value, 'space', [(i, i ^ bits) for i in range(lax.axis_size(...  9.63 us
    pallas_call x2, Pallas kernels, forward(): pl.pallas_call(functools.partial(forward_kernel, width=512, first=first),...  8.7 us
    pallas_call x1, Pallas kernels, on_device(): pl.pallas_call(activate_kernel, in_specs=[smem] + [vmem] * 9, out_shape=[...  6.77 us
    unnamed x16, local copies, waits for them, and re-layouts  3.57 us
    pallas_call x1, Pallas kernels, on_device(): pl.pallas_call(return_kernel, in_specs=[smem] + [vmem] * 7, out_shape=sha...  2.98 us
  transfers between devices with their start and end apart: 18, of which 7 were waited for; matrix products, arithmetic and copies ran while one was open for 3% of the time, Pallas kernels for 31%

profile of v4, /device:TPU:1, one launch (start us, length us, event | category | flops | bytes accessed | tf_op | source)
XLA Modules:
  0.0 83.2 jit_solution(5246547655319269766)
XLA Ops:
  0.6 2.2 %collective-permute-start.4 = (bf16[1024,128]{1,0:T(8,128)(2,1)}, bf16[1024,128]{1,0:T(8,128)(2,1)S(1)}, u32[]{:S(2)}, u32[]{:S(2)}) collective-permute-start(bf16[1024,128]{1,0:T(8,128)(2,1)} %bitcast.47), channel_id=1, source_target_pairs={{0,1},{1,0},{2,3},{3,2},{4,5},{5,4},{6,7},{7,6},{8,9},{9,8},{10,11... | collective-permute-start | bytes 786440 | tf_op jit(solution)/shard_map/ppermute | solution.py:377
  2.8 0.7 reshape.27.rr_ref.refs_5_
  3.5 0.1 pad_add_fusion.side_ref
  3.6 0.0 copy-start.2
  3.6 0.9 %copy-done.2 = bf16[1,1024,128]{2,1,0:T(8,128)(2,1)S(1)} copy-done((bf16[1,1024,128]{2,1,0:T(8,128)(2,1)S(1)}, bf16[1,1024,128]{2,1,0:T(8,128)(2,1)}, u32[]{:S(2)}) %copy-start.2) | copy-done | bytes 262168
  4.6 0.0 copy-start.4
  4.6 0.9 %copy-done.4 = s32[1152,27]{0,1:T(8,128)S(1)} copy-done((s32[1152,27]{0,1:T(8,128)S(1)}, s32[1152,27]{0,1:T(8,128)}, u32[]{:S(2)}) %copy-start.4) | copy-done | bytes 124440
  5.5 2.3 %start.1 = (bf16[384,128]{1,0:T(8,128)(2,1)S(1)}, bf16[384,128]{1,0:T(8,128)(2,1)S(1)}, bf16[288,128]{1,0:T(8,128)(2,1)S(1)}, bf16[288,128]{1,0:T(8,128)(2,1)S(1...) custom-call(s32[3]{0:T(128)S(1)} %pad_add_fusion.side_ref, bf16[1024,128]{1,0:T(8,128)(2,1)S(1)} %bitcast.49, ...), custom_call_target="tpu_custom_call" | custom-call | flops 2000000000 | bytes 4000000 | tf_op jit(solution)/shard_map/start/pallas_call | solution.py:410
  7.8 1.0 %collective-permute-start = (bf16[384,128]{1,0:T(8,128)(2,1)S(1)}, bf16[384,128]{1,0:T(8,128)(2,1)S(1)}, u32[]{:S(2)}, u32[]{:S(2)}) collective-permute-start(bf16[384,128]{1,0:T(8,128)(2,1)S(1)} %get-tuple-element.49), channel_id=1, source_target_pairs={{0,4},{4,0},{8,12},{12,8},{16,20},{20,16},{24,28},{28,24},{32,36},... | collective-permute-start | bytes 294920 | tf_op jit(solution)/shard_map/ppermute | solution.py:360
  8.8 1.2 %collective-permute-start.1 = (bf16[384,128]{1,0:T(8,128)(2,1)S(1)}, bf16[384,128]{1,0:T(8,128)(2,1)S(1)}, u32[]{:S(2)}, u32[]{:S(2)}) collective-permute-start(bf16[384,128]{1,0:T(8,128)(2,1)S(1)} %get-tuple-element.52), channel_id=1, source_target_pairs={{0,12},{4,8},{8,4},{12,0},{16,28},{20,24},{24,20},{28,16},{32,44},... | collective-permute-start | bytes 294920 | tf_op jit(solution)/shard_map/ppermute | solution.py:360
  10.0 0.0 copy-done
  10.0 0.0 copy-done.5
  10.0 4.3 %forward.2 = (bf16[1664,1024]{1,0:T(8,128)(2,1)S(1)}, f32[128,1024]{1,0:T(8,128)S(1)}) custom-call(bf16[1024,128]{1,0:T(8,128)(2,1)S(1)} %bitcast.50, s32[27,1024]{1,0:T(8,128)S(1)} %bitcast.54, bf16[27,128,128]{2,1,0:T(8,128)(2,1)S(1)} %bitcast.39), custom_call_target="tpu_custom_call" | custom-call | flops 7000000000 | bytes 5000000 | tf_op jit(solution)/shard_map/forward/pallas_call | solution.py:422
  14.4 0.0 copy-start.6
  14.4 1.7 %copy-done.6 = bf16[1664,1024]{1,0:T(8,128)(2,1)} copy-done((bf16[1664,1024]{1,0:T(8,128)(2,1)}, bf16[1664,1024]{1,0:T(8,128)(2,1)S(1)}, u32[]{:S(2)}) %copy-start.6) | copy-done | bytes 3407896
  16.1 0.0 collective-permute-done.1.ixb_ref
  16.1 0.0 collective-permute-done.ixa_ref
  16.1 2.5 %collective-permute-start.2 = (bf16[384,128]{1,0:T(8,128)(2,1)S(1)}, bf16[384,128]{1,0:T(8,128)(2,1)S(1)}, u32[]{:S(2)}, u32[]{:S(2)}) collective-permute-start(bf16[384,128]{1,0:T(8,128)(2,1)S(1)} %pad_maximum_fusion.2), channel_id=1, source_target_pairs={{0,16},{4,20},{8,24},{12,28},{16,0},{20,4},{24,8},{28,12},{32,48},... | collective-permute-start | bytes 294920 | tf_op jit(solution)/shard_map/ppermute | solution.py:373
  18.6 4.3 %collective-permute-start.3 = (bf16[384,128]{1,0:T(8,128)(2,1)S(1)}, bf16[384,128]{1,0:T(8,128)(2,1)S(1)}, u32[]{:S(2)}, u32[]{:S(2)}) collective-permute-start(bf16[384,128]{1,0:T(8,128)(2,1)S(1)} %pad_maximum_fusion.3), channel_id=1, source_target_pairs={{0,112},{4,116},{8,120},{12,124},{16,32},{20,36},{24,40},{28,44},{... | collective-permute-start | bytes 294920 | tf_op jit(solution)/shard_map/ppermute | solution.py:373
  22.9 0.0 copy-done.3
  22.9 4.4 %forward.3 = (bf16[1664,1024]{1,0:T(8,128)(2,1)S(1)}, f32[1024,128]{1,0:T(8,128)S(1)}) custom-call(bf16[1024,128]{1,0:T(8,128)(2,1)S(1)} %bitcast.51, s32[27,1024]{1,0:T(8,128)S(1)} %bitcast.55, bf16[27,128,128]{2,1,0:T(8,128)(2,1)S(1)} %bitcast.40, f32[128,1024]{1,0:T(8,128)S(1)} %get-tuple-element.50.refs_0_), custom_call_target="tpu_custom_call" | custom-call | flops 7000000000 | bytes 5000000 | tf_op jit(solution)/shard_map/forward/pallas_call | solution.py:422
  27.3 0.0 collective-permute-done.3.iyb_ref
  27.3 0.0 collective-permute-done.2.iya_ref
  27.3 0.0 collective-permute-done.4.pair_ref
  27.3 0.0 copy-done.1
  27.3 6.8 %activate.1 = (bf16[1024,128]{1,0:T(8,128)(2,1)S(1)}, bf16[1024,128]{1,0:T(8,128)(2,1)S(1)}, bf16[320,128]{1,0:T(8,128)(2,1)S(1)}, bf16[320,128]{1,0:T(8,128)(2,...) custom-call(s32[3]{0:T(128)S(1)} %pad_add_fusion.side_ref, ...), custom_call_target="tpu_custom_call" | custom-call | flops 4000000000 | bytes 3000000 | tf_op jit(solution)/shard_map/activate/pallas_call | solution.py:436
  34.1 0.0 copy-done.7
  34.1 1.1 %weight_first.1.first_ref = f32[1792,128]{1,0:T(8,128)S(1)} custom-call(bf16[1664,1024]{1,0:T(8,128)(2,1)S(1)} %copy-done.7, bf16[1024,128]{1,0:T(8,128)(2,1)S(1)} %get-tuple-element.85.grad_ref, bf16[1024,128]{1,0:T(8,128)(2,1)S(1)} %bitcast.52, f32[27,128,128]{2,1,0:T(8,128)S(1)} %get-tuple-element.62.halo_ref), custom_call_target="tpu_custom_call" | custom-call | flops 4000000000 | bytes 5000000 | tf_op jit(solution)/shard_map/weight_first/pallas_call | solution.py:446
  35.3 1.7 %weight_second.1 = (f32[1728,128]{1,0:T(8,128)S(1)}, bf16[1728,128]{1,0:T(8,128)(2,1)S(1)}) custom-call(s32[3]{0:T(128)S(1)} %pad_add_fusion.side_ref, bf16[1664,1024]{1,0:T(8,128)(2,1)S(1)} %get-tuple-element.60.g_ref, bf16[1024,128]{1,0:T(8,128)(2,1)S(1)} %get-tuple-element.85.grad_ref, f32[1792,128]{1,0:T(8,128)S(1)} %weight_first.1.first_ref, ...), custom_call_target="tpu_custom_call" | custom-call | flops 4000000000 | bytes 5000000 | tf_op jit(solution)/shard_map/weight_second/pallas_call | solution.py:453
  37.0 1.2 %collective-permute-start.5 = (bf16[1728,128]{1,0:T(8,128)(2,1)S(1)}, bf16[1728,128]{1,0:T(8,128)(2,1)}, u32[]{:S(2)}, u32[]{:S(2)}) collective-permute-start(bf16[1728,128]{1,0:T(8,128)(2,1)S(1)} %get-tuple-element.64), channel_id=1, source_target_pairs={{0,4},{4,0},{8,12},{12,8},{16,20},{20,16},{24,28},{28,24},{32,36},... | collective-permute-start | bytes 1327112 | tf_op jit(solution)/shard_map/ppermute | solution.py:381
  38.2 0.2 collective-permute-start.6
  38.4 0.5 collective-permute-start.7
  38.9 0.9 %collective-permute-done.5 = bf16[1728,128]{1,0:T(8,128)(2,1)} collective-permute-done((bf16[1728,128]{1,0:T(8,128)(2,1)S(1)}, bf16[1728,128]{1,0:T(8,128)(2,1)}, u32[]{:S(2)}, u32[]{:S(2)}) %collective-permute-start.5) | collective-permute-done | bytes 442400 | tf_op jit(solution)/shard_map/ppermute | solution.py:381
  39.8 1.1 %convert_add_fusion = (f32[1,2,432,128]{3,2,1,0:T(8,128)S(1)}, bf16[2,432,128]{2,1,0:T(8,128)(2,1)S(1)}) fusion(f32[2,2,432,128]{3,2,1,0:T(8,128)S(1)} %bitcast.38, s32[]{:T(128)S(6)} %select_n.113, bf16[2,2,432,128]{3,2,1,0:T(8,128)(2,1)} %bitcast.8, s32[]{:T(128)S(6)} %select_n.112), kind=kLoop, calls=%fused_computation.1 | loop fusion | flops 552960 | bytes 1990664 | tf_op jit(solution)/shard_map/add | solution.py:481
  40.9 0.0 collective-permute-done.6.ixa_ref
  40.9 1.9 %collective-permute-done.7.ixb_ref = bf16[320,128]{1,0:T(8,128)(2,1)S(1)} collective-permute-done((bf16[320,128]{1,0:T(8,128)(2,1)S(1)}, bf16[320,128]{1,0:T(8,128)(2,1)S(1)}, u32[]{:S(2)}, u32[]{:S(2)}) %collective-permute-start.7) | collective-permute-done | bytes 81952 | tf_op jit(solution)/shard_map/ppermute | solution.py:360
  42.8 0.3 collective-permute-start.8
  43.1 2.4 %backward.4.refs_0_ = f32[256,128]{1,0:T(8,128)S(1)} custom-call(bf16[1024,128]{1,0:T(8,128)(2,1)S(1)} %get-tuple-element.85.grad_ref, s32[27,1024]{1,0:T(8,128)S(1)} %bitcast.56, bf16[27,128,128]{2,1,0:T(8,128)(2,1)S(1)} %bitcast.42), custom_call_target="tpu_custom_call" | custom-call | flops 3000000000 | bytes 2000000 | tf_op jit(solution)/shard_map/backward/pallas_call | solution.py:466
  45.5 2.5 %backward.5.refs_1_ = f32[256,128]{1,0:T(8,128)S(1)} custom-call(bf16[1024,128]{1,0:T(8,128)(2,1)S(1)} %get-tuple-element.85.grad_ref, s32[27,1024]{1,0:T(8,128)S(1)} %bitcast.57, bf16[27,128,128]{2,1,0:T(8,128)(2,1)S(1)} %bitcast.43), custom_call_target="tpu_custom_call" | custom-call | flops 3000000000 | bytes 2000000 | tf_op jit(solution)/shard_map/backward/pallas_call | solution.py:466
  48.0 1.4 %collective-permute-done.8 = bf16[2,432,128]{2,1,0:T(8,128)(2,1)S(1)} collective-permute-done((bf16[2,432,128]{2,1,0:T(8,128)(2,1)S(1)}, bf16[2,432,128]{2,1,0:T(8,128)(2,1)S(1)}, u32[]{:S(2)}, u32[]{:S(2)}) %collective-permute-start.8) | collective-permute-done | bytes 221216 | tf_op jit(solution)/shard_map/ppermute | solution.py:381
  49.5 0.1 collective-permute-start.9
  49.6 2.0 %collective-permute-start.12 = (bf16[320,128]{1,0:T(8,128)(2,1)S(1)}, bf16[320,128]{1,0:T(8,128)(2,1)S(1)}, u32[]{:S(2)}, u32[]{:S(2)}) collective-permute-start(bf16[320,128]{1,0:T(8,128)(2,1)S(1)} %pad_maximum_fusion.4), channel_id=1, source_target_pairs={{0,16},{4,20},{8,24},{12,28},{16,0},{20,4},{24,8},{28,12},{32,48},... | collective-permute-start | bytes 245768 | tf_op jit(solution)/shard_map/ppermute | solution.py:373
  51.7 2.8 %collective-permute-start.13 = (bf16[320,128]{1,0:T(8,128)(2,1)S(1)}, bf16[320,128]{1,0:T(8,128)(2,1)S(1)}, u32[]{:S(2)}, u32[]{:S(2)}) collective-permute-start(bf16[320,128]{1,0:T(8,128)(2,1)S(1)} %pad_maximum_fusion.5), channel_id=1, source_target_pairs={{0,112},{4,116},{8,120},{12,124},{16,32},{20,36},{24,40},{28,44},{... | collective-permute-start | bytes 245768 | tf_op jit(solution)/shard_map/ppermute | solution.py:373
  54.4 0.0 collective-permute-done.9
  54.5 0.1 collective-permute-start.10
  54.6 2.4 %backward.6.refs_2_ = f32[256,128]{1,0:T(8,128)S(1)} custom-call(bf16[1024,128]{1,0:T(8,128)(2,1)S(1)} %get-tuple-element.85.grad_ref, s32[27,1024]{1,0:T(8,128)S(1)} %bitcast.58, bf16[27,128,128]{2,1,0:T(8,128)(2,1)S(1)} %bitcast.44), custom_call_target="tpu_custom_call" | custom-call | flops 3000000000 | bytes 2000000 | tf_op jit(solution)/shard_map/backward/pallas_call | solution.py:466
  57.0 0.2 collective-permute-start.15
  57.3 2.5 %collective-permute-done.10 = bf16[432,128]{1,0:T(8,128)(2,1)S(1)} collective-permute-done((bf16[432,128]{1,0:T(8,128)(2,1)S(1)}, bf16[432,128]{1,0:T(8,128)(2,1)S(1)}, u32[]{:S(2)}, u32[]{:S(2)}) %collective-permute-start.10) | collective-permute-done | bytes 110624 | tf_op jit(solution)/shard_map/ppermute | solution.py:381
  59.8 2.2 %collective-permute-start.11 = (bf16[432,128]{1,0:T(8,128)(2,1)S(1)}, bf16[432,128]{1,0:T(8,128)(2,1)S(1)}, u32[]{:S(2)}, u32[]{:S(2)}) collective-permute-start(bf16[432,128]{1,0:T(8,128)(2,1)S(1)} %add_convert_fusion.2), channel_id=1, source_target_pairs={{0,96},{4,100},{8,104},{12,108},{16,112},{20,116},{24,120},{28,124... | collective-permute-start | bytes 331784 | tf_op jit(solution)/shard_map/ppermute | solution.py:381
  61.9 0.0 collective-permute-done.12.iya_ref
  62.0 0.0 collective-permute-done.13.iyb_ref
  62.0 3.0 %returning.1.refs_4_ = f32[1152,128]{1,0:T(8,128)S(1)} custom-call(s32[3]{0:T(128)S(1)} %pad_add_fusion.side_ref, bf16[320,128]{1,0:T(8,128)(2,1)S(1)} %collective-permute-done.6.ixa_ref, bf16[320,128]{1,0:T(8,128)(2,1)S(1)} %collective-permute-done.7.ixb_ref, bf16[320,128]{1,0:T(8,128)(2,1)S(1)} %collective-permute-done.12.iya_ref, ...), custom_call_target="tpu_custom_call" | custom-call | flops 3000000000 | bytes 4000000 | tf_op jit(solution)/shard_map/returning/pallas_call | solution.py:499
  64.9 0.0 collective-permute-done.11
  65.0 1.0 %collective-permute-start.14 = (bf16[432,128]{1,0:T(8,128)(2,1)S(1)}, bf16[432,128]{1,0:T(8,128)(2,1)S(1)}, u32[]{:S(2)}, u32[]{:S(2)}) collective-permute-start(bf16[432,128]{1,0:T(8,128)(2,1)S(1)} %add_convert_fusion.1.own_ref), channel_id=1, source_target_pairs={{0,32},{4,36},{8,40},{12,44},{16,48},{20,52},{24,56},{28,60},{32,0... | collective-permute-start | bytes 331784 | tf_op jit(solution)/shard_map/ppermute | solution.py:381
  66.0 2.5 %backward.7.refs_3_ = f32[256,128]{1,0:T(8,128)S(1)} custom-call(bf16[1024,128]{1,0:T(8,128)(2,1)S(1)} %get-tuple-element.85.grad_ref, s32[27,1024]{1,0:T(8,128)S(1)} %bitcast.59, bf16[27,128,128]{2,1,0:T(8,128)(2,1)S(1)} %bitcast.46), custom_call_target="tpu_custom_call" | custom-call | flops 3000000000 | bytes 2000000 | tf_op jit(solution)/shard_map/backward/pallas_call | solution.py:466
  68.4 0.5 collective-permute-done.14.one_ref
  69.0 0.2 collective-permute-start.16
  69.2 0.0 collective-permute-done.15.refs_7_
  69.2 1.7 %final.1 = (bf16[1024,128]{1,0:T(8,128)(2,1)}, bf16[1024,128]{1,0:T(8,128)(2,1)}) custom-call(f32[256,128]{1,0:T(8,128)S(1)} %backward.4.refs_0_, f32[256,128]{1,0:T(8,128)S(1)} %backward.5.refs_1_, f32[256,128]{1,0:T(8,128)S(1)} %backward.6.refs_2_, f32[256,128]{1,0:T(8,128)S(1)} %backward.7.refs_3_, f32[1152,128]{1,0:T(8,128)S(1)} %returning.1.refs_4_, ...), custom_call_target="tpu_custom_call" | custom-call | flops 1000000000 | bytes 3000000 | tf_op jit(solution)/shard_map/final/pallas_call | solution.py:512
  70.8 3.0 %collective-permute-done.16.two_ref = bf16[2,432,128]{2,1,0:T(8,128)(2,1)S(1)} collective-permute-done((bf16[2,432,128]{2,1,0:T(8,128)(2,1)S(1)}, bf16[2,432,128]{2,1,0:T(8,128)(2,1)S(1)}, u32[]{:S(2)}, u32[]{:S(2)}) %collective-permute-start.16) | collective-permute-done | bytes 221216 | tf_op jit(solution)/shard_map/ppermute | solution.py:381
  73.9 6.1 %collective-permute-start.17 = (bf16[4,432,128]{2,1,0:T(8,128)(2,1)S(1)}, bf16[4,432,128]{2,1,0:T(8,128)(2,1)S(1)}, u32[]{:S(2)}, u32[]{:S(2)}) collective-permute-start(bf16[4,432,128]{2,1,0:T(8,128)(2,1)S(1)} %pad_maximum_fusion), channel_id=1, source_target_pairs={{0,4},{4,0},{8,12},{12,8},{16,20},{20,16},{24,28},{28,24},{32,36},... | collective-permute-start | bytes 1327112 | tf_op jit(solution)/shard_map/ppermute | solution.py:381
  79.9 0.1 pad_add_fusion.1.bits_ref
  80.0 1.3 %collective-permute-done.17.four_ref = bf16[4,432,128]{2,1,0:T(8,128)(2,1)S(1)} collective-permute-done((bf16[4,432,128]{2,1,0:T(8,128)(2,1)S(1)}, bf16[4,432,128]{2,1,0:T(8,128)(2,1)S(1)}, u32[]{:S(2)}, u32[]{:S(2)}) %collective-permute-start.17) | collective-permute-done | bytes 442400 | tf_op jit(solution)/shard_map/ppermute | solution.py:381
  81.4 1.9 %assemble.1 = f32[8,432,128]{2,1,0:T(8,128)} custom-call(s32[3]{0:T(128)S(1)} %pad_add_fusion.1.bits_ref, bf16[432,128]{1,0:T(8,128)(2,1)S(1)} %add_convert_fusion.1.own_ref, bf16[432,128]{1,0:T(8,128)(2,1)S(1)} %collective-permute-done.14.one_ref, bf16[2,432,128]{2,1,0:T(8,128)(2,1)S(1)} %collective-permute-done.16.two_ref, ...), custom_call_target="tpu_custom_call" | custom-call | flops 1000000 | bytes 3000000 | tf_op jit(solution)/shard_map/assemble/pallas_call | solution.py:521
  (18 shorter events, 0.3 us)
Async XLA Ops:
  0.6 26.7 %collective-permute-start.4 = (bf16[1024,128]{1,0:T(8,128)(2,1)}, bf16[1024,128]{1,0:T(8,128)(2,1)S(1)}, u32[]{:S(2)}, u32[]{:S(2)}) collective-permute-start(bf16[1024,128]{1,0:T(8,128)(2,1)} %bitcast.47), channel_id=1, source_target_pairs={{0,1},{1,0},{2,3},{3,2},{4,5},{5,4},{6,7},{7,6},{8,9},{9,8},{10,11... | collective-permute-start | bytes 786440 | tf_op jit(solution)/shard_map/ppermute | solution.py:377
  3.6 1.0 %copy-start.2 = (bf16[1,1024,128]{2,1,0:T(8,128)(2,1)S(1)}, bf16[1,1024,128]{2,1,0:T(8,128)(2,1)}, u32[]{:S(2)}) copy-start(bf16[1,1024,128]{2,1,0:T(8,128)(2,1)} %param.6) | copy-start | bytes 786436
  4.6 0.9 %copy-start.4 = (s32[1152,27]{0,1:T(8,128)S(1)}, s32[1152,27]{0,1:T(8,128)}, u32[]{:S(2)}) copy-start(s32[1152,27]{0,1:T(8,128)} %param.10) | copy-start | bytes 373252
  5.5 4.5 %copy-start = (bf16[1,27,128,128]{3,2,1,0:T(8,128)(2,1)S(1)}, bf16[1,27,128,128]{3,2,1,0:T(8,128)(2,1)}, u32[]{:S(2)}) copy-start(bf16[1,27,128,128]{3,2,1,0:T(8,128)(2,1)} %param.7) | copy-start | bytes 2654212
  5.5 4.5 %copy-start.5 = (s32[1024,27]{0,1:T(8,128)S(1)}, s32[1024,27]{0,1:T(8,128)}, u32[]{:S(2)}) copy-start(s32[1024,27]{0,1:T(8,128)} %param.9) | copy-start | bytes 331780
  7.8 8.3 %collective-permute-start = (bf16[384,128]{1,0:T(8,128)(2,1)S(1)}, bf16[384,128]{1,0:T(8,128)(2,1)S(1)}, u32[]{:S(2)}, u32[]{:S(2)}) collective-permute-start(bf16[384,128]{1,0:T(8,128)(2,1)S(1)} %get-tuple-element.49), channel_id=1, source_target_pairs={{0,4},{4,0},{8,12},{12,8},{16,20},{20,16},{24,28},{28,24},{32,36},... | collective-permute-start | bytes 294920 | tf_op jit(solution)/shard_map/ppermute | solution.py:360
  8.8 7.2 %collective-permute-start.1 = (bf16[384,128]{1,0:T(8,128)(2,1)S(1)}, bf16[384,128]{1,0:T(8,128)(2,1)S(1)}, u32[]{:S(2)}, u32[]{:S(2)}) collective-permute-start(bf16[384,128]{1,0:T(8,128)(2,1)S(1)} %get-tuple-element.52), channel_id=1, source_target_pairs={{0,12},{4,8},{8,4},{12,0},{16,28},{20,24},{24,20},{28,16},{32,44},... | collective-permute-start | bytes 294920 | tf_op jit(solution)/shard_map/ppermute | solution.py:360
  10.0 12.9 %copy-start.3 = (bf16[1,1024,128]{2,1,0:T(8,128)(2,1)S(1)}, bf16[1,1024,128]{2,1,0:T(8,128)(2,1)}, u32[]{:S(2)}) copy-start(bf16[1,1024,128]{2,1,0:T(8,128)(2,1)} %param.6) | copy-start | bytes 786436
  14.4 1.7 %copy-start.6 = (bf16[1664,1024]{1,0:T(8,128)(2,1)}, bf16[1664,1024]{1,0:T(8,128)(2,1)S(1)}, u32[]{:S(2)}) copy-start(bf16[1664,1024]{1,0:T(8,128)(2,1)S(1)} %get-tuple-element.61.g_ref) | copy-start | bytes 10223620
  16.1 11.2 %collective-permute-start.2 = (bf16[384,128]{1,0:T(8,128)(2,1)S(1)}, bf16[384,128]{1,0:T(8,128)(2,1)S(1)}, u32[]{:S(2)}, u32[]{:S(2)}) collective-permute-start(bf16[384,128]{1,0:T(8,128)(2,1)S(1)} %pad_maximum_fusion.2), channel_id=1, source_target_pairs={{0,16},{4,20},{8,24},{12,28},{16,0},{20,4},{24,8},{28,12},{32,48},... | collective-permute-start | bytes 294920 | tf_op jit(solution)/shard_map/ppermute | solution.py:373
  18.6 8.7 %copy-start.1 = (bf16[1,1024,128]{2,1,0:T(8,128)(2,1)S(1)}, bf16[1,1024,128]{2,1,0:T(8,128)(2,1)}, u32[]{:S(2)}) copy-start(bf16[1,1024,128]{2,1,0:T(8,128)(2,1)} %param.8) | copy-start | bytes 786436
  18.6 8.7 %collective-permute-start.3 = (bf16[384,128]{1,0:T(8,128)(2,1)S(1)}, bf16[384,128]{1,0:T(8,128)(2,1)S(1)}, u32[]{:S(2)}, u32[]{:S(2)}) collective-permute-start(bf16[384,128]{1,0:T(8,128)(2,1)S(1)} %pad_maximum_fusion.3), channel_id=1, source_target_pairs={{0,112},{4,116},{8,120},{12,124},{16,32},{20,36},{24,40},{28,44},{... | collective-permute-start | bytes 294920 | tf_op jit(solution)/shard_map/ppermute | solution.py:373
  27.3 6.8 %copy-start.7 = (bf16[1664,1024]{1,0:T(8,128)(2,1)S(1)}, bf16[1664,1024]{1,0:T(8,128)(2,1)}, u32[]{:S(2)}) copy-start(bf16[1664,1024]{1,0:T(8,128)(2,1)} %copy-done.6) | copy-start | bytes 10223620
  37.0 2.8 %collective-permute-start.5 = (bf16[1728,128]{1,0:T(8,128)(2,1)S(1)}, bf16[1728,128]{1,0:T(8,128)(2,1)}, u32[]{:S(2)}, u32[]{:S(2)}) collective-permute-start(bf16[1728,128]{1,0:T(8,128)(2,1)S(1)} %get-tuple-element.64), channel_id=1, source_target_pairs={{0,4},{4,0},{8,12},{12,8},{16,20},{20,16},{24,28},{28,24},{32,36},... | collective-permute-start | bytes 1327112 | tf_op jit(solution)/shard_map/ppermute | solution.py:381
  38.2 2.7 %collective-permute-start.6 = (bf16[320,128]{1,0:T(8,128)(2,1)S(1)}, bf16[320,128]{1,0:T(8,128)(2,1)S(1)}, u32[]{:S(2)}, u32[]{:S(2)}) collective-permute-start(bf16[320,128]{1,0:T(8,128)(2,1)S(1)} %get-tuple-element.65), channel_id=1, source_target_pairs={{0,4},{4,0},{8,12},{12,8},{16,20},{20,16},{24,28},{28,24},{32,36},... | collective-permute-start | bytes 245768 | tf_op jit(solution)/shard_map/ppermute | solution.py:360
  38.4 4.4 %collective-permute-start.7 = (bf16[320,128]{1,0:T(8,128)(2,1)S(1)}, bf16[320,128]{1,0:T(8,128)(2,1)S(1)}, u32[]{:S(2)}, u32[]{:S(2)}) collective-permute-start(bf16[320,128]{1,0:T(8,128)(2,1)S(1)} %get-tuple-element.66), channel_id=1, source_target_pairs={{0,12},{4,8},{8,4},{12,0},{16,28},{20,24},{24,20},{28,16},{32,44},... | collective-permute-start | bytes 245768 | tf_op jit(solution)/shard_map/ppermute | solution.py:360
  42.8 6.6 %collective-permute-start.8 = (bf16[2,432,128]{2,1,0:T(8,128)(2,1)S(1)}, bf16[2,432,128]{2,1,0:T(8,128)(2,1)S(1)}, u32[]{:S(2)}, u32[]{:S(2)}) collective-permute-start(bf16[2,432,128]{2,1,0:T(8,128)(2,1)S(1)} %get-tuple-element.67), channel_id=1, source_target_pairs={{0,8},{4,12},{8,0},{12,4},{16,24},{20,28},{24,16},{28,20},{32,40},... | collective-permute-start | bytes 663560 | tf_op jit(solution)/shard_map/ppermute | solution.py:381
  49.5 4.9 %collective-permute-start.9 = (bf16[432,128]{1,0:T(8,128)(2,1)S(1)}, bf16[432,128]{1,0:T(8,128)(2,1)S(1)}, u32[]{:S(2)}, u32[]{:S(2)}) collective-permute-start(bf16[432,128]{1,0:T(8,128)(2,1)S(1)} %fusion.3), channel_id=1, source_target_pairs={{0,32},{4,36},{8,40},{12,44},{16,48},{20,52},{24,56},{28,60},{32,0... | collective-permute-start | bytes 331784 | tf_op jit(solution)/shard_map/ppermute | solution.py:381
  49.6 12.3 %collective-permute-start.12 = (bf16[320,128]{1,0:T(8,128)(2,1)S(1)}, bf16[320,128]{1,0:T(8,128)(2,1)S(1)}, u32[]{:S(2)}, u32[]{:S(2)}) collective-permute-start(bf16[320,128]{1,0:T(8,128)(2,1)S(1)} %pad_maximum_fusion.4), channel_id=1, source_target_pairs={{0,16},{4,20},{8,24},{12,28},{16,0},{20,4},{24,8},{28,12},{32,48},... | collective-permute-start | bytes 245768 | tf_op jit(solution)/shard_map/ppermute | solution.py:373
  51.7 10.3 %collective-permute-start.13 = (bf16[320,128]{1,0:T(8,128)(2,1)S(1)}, bf16[320,128]{1,0:T(8,128)(2,1)S(1)}, u32[]{:S(2)}, u32[]{:S(2)}) collective-permute-start(bf16[320,128]{1,0:T(8,128)(2,1)S(1)} %pad_maximum_fusion.5), channel_id=1, source_target_pairs={{0,112},{4,116},{8,120},{12,124},{16,32},{20,36},{24,40},{28,44},{... | collective-permute-start | bytes 245768 | tf_op jit(solution)/shard_map/ppermute | solution.py:373
  54.5 5.2 %collective-permute-start.10 = (bf16[432,128]{1,0:T(8,128)(2,1)S(1)}, bf16[432,128]{1,0:T(8,128)(2,1)S(1)}, u32[]{:S(2)}, u32[]{:S(2)}) collective-permute-start(bf16[432,128]{1,0:T(8,128)(2,1)S(1)} %fusion.2), channel_id=1, source_target_pairs={{0,24},{4,28},{8,16},{12,20},{16,8},{20,12},{24,0},{28,4},{32,56},... | collective-permute-start | bytes 331784 | tf_op jit(solution)/shard_map/ppermute | solution.py:381
  57.0 12.1 %collective-permute-start.15 = (bf16[1024,128]{1,0:T(8,128)(2,1)S(1)}, bf16[1024,128]{1,0:T(8,128)(2,1)S(1)}, u32[]{:S(2)}, u32[]{:S(2)}) collective-permute-start(bf16[1024,128]{1,0:T(8,128)(2,1)S(1)} %get-tuple-element.89.refs_6_), channel_id=1, source_target_pairs={{0,1},{1,0},{2,3},{3,2},{4,5},{5,4},{6,7},{7,6},{8,9},{9,8},{10,11... | collective-permute-start | bytes 786440 | tf_op jit(solution)/shard_map/ppermute | solution.py:377
  59.8 5.2 %collective-permute-start.11 = (bf16[432,128]{1,0:T(8,128)(2,1)S(1)}, bf16[432,128]{1,0:T(8,128)(2,1)S(1)}, u32[]{:S(2)}, u32[]{:S(2)}) collective-permute-start(bf16[432,128]{1,0:T(8,128)(2,1)S(1)} %add_convert_fusion.2), channel_id=1, source_target_pairs={{0,96},{4,100},{8,104},{12,108},{16,112},{20,116},{24,120},{28,124... | collective-permute-start | bytes 331784 | tf_op jit(solution)/shard_map/ppermute | solution.py:381
  65.0 3.9 %collective-permute-start.14 = (bf16[432,128]{1,0:T(8,128)(2,1)S(1)}, bf16[432,128]{1,0:T(8,128)(2,1)S(1)}, u32[]{:S(2)}, u32[]{:S(2)}) collective-permute-start(bf16[432,128]{1,0:T(8,128)(2,1)S(1)} %add_convert_fusion.1.own_ref), channel_id=1, source_target_pairs={{0,32},{4,36},{8,40},{12,44},{16,48},{20,52},{24,56},{28,60},{32,0... | collective-permute-start | bytes 331784 | tf_op jit(solution)/shard_map/ppermute | solution.py:381
  69.0 4.9 %collective-permute-start.16 = (bf16[2,432,128]{2,1,0:T(8,128)(2,1)S(1)}, bf16[2,432,128]{2,1,0:T(8,128)(2,1)S(1)}, u32[]{:S(2)}, u32[]{:S(2)}) collective-permute-start(bf16[2,432,128]{2,1,0:T(8,128)(2,1)S(1)} %pad_maximum_fusion.1), channel_id=1, source_target_pairs={{0,8},{4,12},{8,0},{12,4},{16,24},{20,28},{24,16},{28,20},{32,40},... | collective-permute-start | bytes 663560 | tf_op jit(solution)/shard_map/ppermute | solution.py:381
  73.9 7.5 %collective-permute-start.17 = (bf16[4,432,128]{2,1,0:T(8,128)(2,1)S(1)}, bf16[4,432,128]{2,1,0:T(8,128)(2,1)S(1)}, u32[]{:S(2)}, u32[]{:S(2)}) collective-permute-start(bf16[4,432,128]{2,1,0:T(8,128)(2,1)S(1)} %pad_maximum_fusion), channel_id=1, source_target_pairs={{0,4},{4,0},{8,12},{12,8},{16,20},{20,16},{24,28},{28,24},{32,36},... | collective-permute-start | bytes 1327112 | tf_op jit(solution)/shard_map/ppermute | solution.py:381

commit v5 on v4

--- a/solution.py
+++ b/solution.py
@@ -420,7 +420,7 @@
 
     def forward(first, dims, x, *before):
         return pl.pallas_call(
-            functools.partial(forward_kernel, width=512, first=first),
+            functools.partial(forward_kernel, width=1024, first=first),
             out_shape=[shape((13 * C, ROWS), BF), shape(dims, F32)],
             compiler_params=PARAMS,
             cost_estimate=cost(7e9, 5e6),

time: 83.5 us -> 83.5 us (level)
  no operation moved by 1% of the time
where the time goes in v5:
time: 83.5 us; the launch traced here: 83.2 us
  Pallas kernels  37 us (44%)
  starting transfers between devices  28 us (34%)
  waiting for transfers between devices  11.6 us (14%)
  local copies, waits for them, and re-layouts  4.27 us (5%)
  other arithmetic  1.54 us (2%)
  between operations  0.86 us (1%)
    ppermute x4, starting transfers between devices, exchange_y(): lax.ppermute(v, 'space', pairing('y', n))  11.6 us
    ppermute x8, starting transfers between devices, xor_send(): lax.ppermute(value, 'space', [(i, i ^ bits) for i in range(lax.axis_size(...  11.1 us
    pallas_call x4, Pallas kernels, backward(): pl.pallas_call(functools.partial(backward_kernel, begin=index * size), ou...  9.79 us
    ppermute x8, waiting for transfers between devices, xor_send(): lax.ppermute(value, 'space', [(i, i ^ bits) for i in range(lax.axis_size(...  9.64 us
    pallas_call x2, Pallas kernels, forward(): pl.pallas_call(functools.partial(forward_kernel, width=1024, first=first)...  8.71 us
    pallas_call x1, Pallas kernels, on_device(): pl.pallas_call(activate_kernel, in_specs=[smem] + [vmem] * 9, out_shape=[...  6.77 us
    unnamed x16, local copies, waits for them, and re-layouts  3.57 us
    pallas_call x1, Pallas kernels, on_device(): pl.pallas_call(return_kernel, in_specs=[smem] + [vmem] * 7, out_shape=sha...  2.98 us
  transfers between devices with their start and end apart: 18, of which 7 were waited for; matrix products, arithmetic and copies ran while one was open for 3% of the time, Pallas kernels for 31%

profile of v5, /device:TPU:1, one launch (start us, length us, event | category | flops | bytes accessed | tf_op | source)
XLA Modules:
  0.0 83.2 jit_solution(10116931840902054235)
XLA Ops:
  0.6 2.2 %collective-permute-start.4 = (bf16[1024,128]{1,0:T(8,128)(2,1)}, bf16[1024,128]{1,0:T(8,128)(2,1)S(1)}, u32[]{:S(2)}, u32[]{:S(2)}) collective-permute-start(bf16[1024,128]{1,0:T(8,128)(2,1)} %bitcast.47), channel_id=1, source_target_pairs={{0,1},{1,0},{2,3},{3,2},{4,5},{5,4},{6,7},{7,6},{8,9},{9,8},{10,11... | collective-permute-start | bytes 786440 | tf_op jit(solution)/shard_map/ppermute | solution.py:377
  2.8 0.7 reshape.27.rr_ref.refs_5_
  3.5 0.1 pad_add_fusion.side_ref
  3.6 0.0 copy-start.2
  3.6 0.9 %copy-done.2 = bf16[1,1024,128]{2,1,0:T(8,128)(2,1)S(1)} copy-done((bf16[1,1024,128]{2,1,0:T(8,128)(2,1)S(1)}, bf16[1,1024,128]{2,1,0:T(8,128)(2,1)}, u32[]{:S(2)}) %copy-start.2) | copy-done | bytes 262168
  4.6 0.0 copy-start.4
  4.6 0.9 %copy-done.4 = s32[1152,27]{0,1:T(8,128)S(1)} copy-done((s32[1152,27]{0,1:T(8,128)S(1)}, s32[1152,27]{0,1:T(8,128)}, u32[]{:S(2)}) %copy-start.4) | copy-done | bytes 124440
  5.5 2.3 %start.1 = (bf16[384,128]{1,0:T(8,128)(2,1)S(1)}, bf16[384,128]{1,0:T(8,128)(2,1)S(1)}, bf16[288,128]{1,0:T(8,128)(2,1)S(1)}, bf16[288,128]{1,0:T(8,128)(2,1)S(1...) custom-call(s32[3]{0:T(128)S(1)} %pad_add_fusion.side_ref, bf16[1024,128]{1,0:T(8,128)(2,1)S(1)} %bitcast.49, ...), custom_call_target="tpu_custom_call" | custom-call | flops 2000000000 | bytes 4000000 | tf_op jit(solution)/shard_map/start/pallas_call | solution.py:410
  7.8 1.0 %collective-permute-start = (bf16[384,128]{1,0:T(8,128)(2,1)S(1)}, bf16[384,128]{1,0:T(8,128)(2,1)S(1)}, u32[]{:S(2)}, u32[]{:S(2)}) collective-permute-start(bf16[384,128]{1,0:T(8,128)(2,1)S(1)} %get-tuple-element.49), channel_id=1, source_target_pairs={{0,4},{4,0},{8,12},{12,8},{16,20},{20,16},{24,28},{28,24},{32,36},... | collective-permute-start | bytes 294920 | tf_op jit(solution)/shard_map/ppermute | solution.py:360
  8.8 1.2 %collective-permute-start.1 = (bf16[384,128]{1,0:T(8,128)(2,1)S(1)}, bf16[384,128]{1,0:T(8,128)(2,1)S(1)}, u32[]{:S(2)}, u32[]{:S(2)}) collective-permute-start(bf16[384,128]{1,0:T(8,128)(2,1)S(1)} %get-tuple-element.52), channel_id=1, source_target_pairs={{0,12},{4,8},{8,4},{12,0},{16,28},{20,24},{24,20},{28,16},{32,44},... | collective-permute-start | bytes 294920 | tf_op jit(solution)/shard_map/ppermute | solution.py:360
  10.0 0.0 copy-done
  10.0 0.0 copy-done.5
  10.0 4.3 %forward.2 = (bf16[1664,1024]{1,0:T(8,128)(2,1)S(1)}, f32[128,1024]{1,0:T(8,128)S(1)}) custom-call(bf16[1024,128]{1,0:T(8,128)(2,1)S(1)} %bitcast.50, s32[27,1024]{1,0:T(8,128)S(1)} %bitcast.54, bf16[27,128,128]{2,1,0:T(8,128)(2,1)S(1)} %bitcast.39), custom_call_target="tpu_custom_call" | custom-call | flops 7000000000 | bytes 5000000 | tf_op jit(solution)/shard_map/forward/pallas_call | solution.py:422
  14.4 0.0 copy-start.6
  14.4 1.7 %copy-done.6 = bf16[1664,1024]{1,0:T(8,128)(2,1)} copy-done((bf16[1664,1024]{1,0:T(8,128)(2,1)}, bf16[1664,1024]{1,0:T(8,128)(2,1)S(1)}, u32[]{:S(2)}) %copy-start.6) | copy-done | bytes 3407896
  16.1 0.0 collective-permute-done.1.ixb_ref
  16.1 0.0 collective-permute-done.ixa_ref
  16.1 2.5 %collective-permute-start.2 = (bf16[384,128]{1,0:T(8,128)(2,1)S(1)}, bf16[384,128]{1,0:T(8,128)(2,1)S(1)}, u32[]{:S(2)}, u32[]{:S(2)}) collective-permute-start(bf16[384,128]{1,0:T(8,128)(2,1)S(1)} %pad_maximum_fusion.2), channel_id=1, source_target_pairs={{0,16},{4,20},{8,24},{12,28},{16,0},{20,4},{24,8},{28,12},{32,48},... | collective-permute-start | bytes 294920 | tf_op jit(solution)/shard_map/ppermute | solution.py:373
  18.6 4.3 %collective-permute-start.3 = (bf16[384,128]{1,0:T(8,128)(2,1)S(1)}, bf16[384,128]{1,0:T(8,128)(2,1)S(1)}, u32[]{:S(2)}, u32[]{:S(2)}) collective-permute-start(bf16[384,128]{1,0:T(8,128)(2,1)S(1)} %pad_maximum_fusion.3), channel_id=1, source_target_pairs={{0,112},{4,116},{8,120},{12,124},{16,32},{20,36},{24,40},{28,44},{... | collective-permute-start | bytes 294920 | tf_op jit(solution)/shard_map/ppermute | solution.py:373
  22.9 0.0 copy-done.3
  22.9 4.4 %forward.3 = (bf16[1664,1024]{1,0:T(8,128)(2,1)S(1)}, f32[1024,128]{1,0:T(8,128)S(1)}) custom-call(bf16[1024,128]{1,0:T(8,128)(2,1)S(1)} %bitcast.51, s32[27,1024]{1,0:T(8,128)S(1)} %bitcast.55, bf16[27,128,128]{2,1,0:T(8,128)(2,1)S(1)} %bitcast.40, f32[128,1024]{1,0:T(8,128)S(1)} %get-tuple-element.50.refs_0_), custom_call_target="tpu_custom_call" | custom-call | flops 7000000000 | bytes 5000000 | tf_op jit(solution)/shard_map/forward/pallas_call | solution.py:422
  27.3 0.0 collective-permute-done.3.iyb_ref
  27.3 0.0 collective-permute-done.2.iya_ref
  27.3 0.0 collective-permute-done.4.pair_ref
  27.3 0.0 copy-done.1
  27.3 6.8 %activate.1 = (bf16[1024,128]{1,0:T(8,128)(2,1)S(1)}, bf16[1024,128]{1,0:T(8,128)(2,1)S(1)}, bf16[320,128]{1,0:T(8,128)(2,1)S(1)}, bf16[320,128]{1,0:T(8,128)(2,...) custom-call(s32[3]{0:T(128)S(1)} %pad_add_fusion.side_ref, ...), custom_call_target="tpu_custom_call" | custom-call | flops 4000000000 | bytes 3000000 | tf_op jit(solution)/shard_map/activate/pallas_call | solution.py:436
  34.1 0.0 copy-done.7
  34.1 1.1 %weight_first.1.first_ref = f32[1792,128]{1,0:T(8,128)S(1)} custom-call(bf16[1664,1024]{1,0:T(8,128)(2,1)S(1)} %copy-done.7, bf16[1024,128]{1,0:T(8,128)(2,1)S(1)} %get-tuple-element.85.grad_ref, bf16[1024,128]{1,0:T(8,128)(2,1)S(1)} %bitcast.52, f32[27,128,128]{2,1,0:T(8,128)S(1)} %get-tuple-element.62.halo_ref), custom_call_target="tpu_custom_call" | custom-call | flops 4000000000 | bytes 5000000 | tf_op jit(solution)/shard_map/weight_first/pallas_call | solution.py:446
  35.3 1.7 %weight_second.1 = (f32[1728,128]{1,0:T(8,128)S(1)}, bf16[1728,128]{1,0:T(8,128)(2,1)S(1)}) custom-call(s32[3]{0:T(128)S(1)} %pad_add_fusion.side_ref, bf16[1664,1024]{1,0:T(8,128)(2,1)S(1)} %get-tuple-element.60.g_ref, bf16[1024,128]{1,0:T(8,128)(2,1)S(1)} %get-tuple-element.85.grad_ref, f32[1792,128]{1,0:T(8,128)S(1)} %weight_first.1.first_ref, ...), custom_call_target="tpu_custom_call" | custom-call | flops 4000000000 | bytes 5000000 | tf_op jit(solution)/shard_map/weight_second/pallas_call | solution.py:453
  37.0 1.2 %collective-permute-start.5 = (bf16[1728,128]{1,0:T(8,128)(2,1)S(1)}, bf16[1728,128]{1,0:T(8,128)(2,1)}, u32[]{:S(2)}, u32[]{:S(2)}) collective-permute-start(bf16[1728,128]{1,0:T(8,128)(2,1)S(1)} %get-tuple-element.64), channel_id=1, source_target_pairs={{0,4},{4,0},{8,12},{12,8},{16,20},{20,16},{24,28},{28,24},{32,36},... | collective-permute-start | bytes 1327112 | tf_op jit(solution)/shard_map/ppermute | solution.py:381
  38.2 0.2 collective-permute-start.6
  38.4 0.5 collective-permute-start.7
  38.9 0.9 %collective-permute-done.5 = bf16[1728,128]{1,0:T(8,128)(2,1)} collective-permute-done((bf16[1728,128]{1,0:T(8,128)(2,1)S(1)}, bf16[1728,128]{1,0:T(8,128)(2,1)}, u32[]{:S(2)}, u32[]{:S(2)}) %collective-permute-start.5) | collective-permute-done | bytes 442400 | tf_op jit(solution)/shard_map/ppermute | solution.py:381
  39.8 1.1 %convert_add_fusion = (f32[1,2,432,128]{3,2,1,0:T(8,128)S(1)}, bf16[2,432,128]{2,1,0:T(8,128)(2,1)S(1)}) fusion(f32[2,2,432,128]{3,2,1,0:T(8,128)S(1)} %bitcast.38, s32[]{:T(128)S(6)} %select_n.113, bf16[2,2,432,128]{3,2,1,0:T(8,128)(2,1)} %bitcast.8, s32[]{:T(128)S(6)} %select_n.112), kind=kLoop, calls=%fused_computation.1 | loop fusion | flops 552960 | bytes 1990664 | tf_op jit(solution)/shard_map/add | solution.py:481
  40.9 0.0 collective-permute-done.6.ixa_ref
  40.9 1.9 %collective-permute-done.7.ixb_ref = bf16[320,128]{1,0:T(8,128)(2,1)S(1)} collective-permute-done((bf16[320,128]{1,0:T(8,128)(2,1)S(1)}, bf16[320,128]{1,0:T(8,128)(2,1)S(1)}, u32[]{:S(2)}, u32[]{:S(2)}) %collective-permute-start.7) | collective-permute-done | bytes 81952 | tf_op jit(solution)/shard_map/ppermute | solution.py:360
  42.8 0.3 collective-permute-start.8
  43.1 2.4 %backward.4.refs_0_ = f32[256,128]{1,0:T(8,128)S(1)} custom-call(bf16[1024,128]{1,0:T(8,128)(2,1)S(1)} %get-tuple-element.85.grad_ref, s32[27,1024]{1,0:T(8,128)S(1)} %bitcast.56, bf16[27,128,128]{2,1,0:T(8,128)(2,1)S(1)} %bitcast.42), custom_call_target="tpu_custom_call" | custom-call | flops 3000000000 | bytes 2000000 | tf_op jit(solution)/shard_map/backward/pallas_call | solution.py:466
  45.5 2.4 %backward.5.refs_1_ = f32[256,128]{1,0:T(8,128)S(1)} custom-call(bf16[1024,128]{1,0:T(8,128)(2,1)S(1)} %get-tuple-element.85.grad_ref, s32[27,1024]{1,0:T(8,128)S(1)} %bitcast.57, bf16[27,128,128]{2,1,0:T(8,128)(2,1)S(1)} %bitcast.43), custom_call_target="tpu_custom_call" | custom-call | flops 3000000000 | bytes 2000000 | tf_op jit(solution)/shard_map/backward/pallas_call | solution.py:466
  48.0 1.4 %collective-permute-done.8 = bf16[2,432,128]{2,1,0:T(8,128)(2,1)S(1)} collective-permute-done((bf16[2,432,128]{2,1,0:T(8,128)(2,1)S(1)}, bf16[2,432,128]{2,1,0:T(8,128)(2,1)S(1)}, u32[]{:S(2)}, u32[]{:S(2)}) %collective-permute-start.8) | collective-permute-done | bytes 221216 | tf_op jit(solution)/shard_map/ppermute | solution.py:381
  49.5 0.1 collective-permute-start.9
  49.6 2.0 %collective-permute-start.12 = (bf16[320,128]{1,0:T(8,128)(2,1)S(1)}, bf16[320,128]{1,0:T(8,128)(2,1)S(1)}, u32[]{:S(2)}, u32[]{:S(2)}) collective-permute-start(bf16[320,128]{1,0:T(8,128)(2,1)S(1)} %pad_maximum_fusion.4), channel_id=1, source_target_pairs={{0,16},{4,20},{8,24},{12,28},{16,0},{20,4},{24,8},{28,12},{32,48},... | collective-permute-start | bytes 245768 | tf_op jit(solution)/shard_map/ppermute | solution.py:373
  51.6 2.8 %collective-permute-start.13 = (bf16[320,128]{1,0:T(8,128)(2,1)S(1)}, bf16[320,128]{1,0:T(8,128)(2,1)S(1)}, u32[]{:S(2)}, u32[]{:S(2)}) collective-permute-start(bf16[320,128]{1,0:T(8,128)(2,1)S(1)} %pad_maximum_fusion.5), channel_id=1, source_target_pairs={{0,112},{4,116},{8,120},{12,124},{16,32},{20,36},{24,40},{28,44},{... | collective-permute-start | bytes 245768 | tf_op jit(solution)/shard_map/ppermute | solution.py:373
  54.4 0.0 collective-permute-done.9
  54.5 0.1 collective-permute-start.10
  54.6 2.4 %backward.6.refs_2_ = f32[256,128]{1,0:T(8,128)S(1)} custom-call(bf16[1024,128]{1,0:T(8,128)(2,1)S(1)} %get-tuple-element.85.grad_ref, s32[27,1024]{1,0:T(8,128)S(1)} %bitcast.58, bf16[27,128,128]{2,1,0:T(8,128)(2,1)S(1)} %bitcast.44), custom_call_target="tpu_custom_call" | custom-call | flops 3000000000 | bytes 2000000 | tf_op jit(solution)/shard_map/backward/pallas_call | solution.py:466
  57.0 0.2 collective-permute-start.15
  57.3 2.5 %collective-permute-done.10 = bf16[432,128]{1,0:T(8,128)(2,1)S(1)} collective-permute-done((bf16[432,128]{1,0:T(8,128)(2,1)S(1)}, bf16[432,128]{1,0:T(8,128)(2,1)S(1)}, u32[]{:S(2)}, u32[]{:S(2)}) %collective-permute-start.10) | collective-permute-done | bytes 110624 | tf_op jit(solution)/shard_map/ppermute | solution.py:381
  59.8 2.2 %collective-permute-start.11 = (bf16[432,128]{1,0:T(8,128)(2,1)S(1)}, bf16[432,128]{1,0:T(8,128)(2,1)S(1)}, u32[]{:S(2)}, u32[]{:S(2)}) collective-permute-start(bf16[432,128]{1,0:T(8,128)(2,1)S(1)} %add_convert_fusion.2), channel_id=1, source_target_pairs={{0,96},{4,100},{8,104},{12,108},{16,112},{20,116},{24,120},{28,124... | collective-permute-start | bytes 331784 | tf_op jit(solution)/shard_map/ppermute | solution.py:381
  61.9 0.0 collective-permute-done.12.iya_ref
  61.9 0.0 collective-permute-done.13.iyb_ref
  61.9 3.0 %returning.1.refs_4_ = f32[1152,128]{1,0:T(8,128)S(1)} custom-call(s32[3]{0:T(128)S(1)} %pad_add_fusion.side_ref, bf16[320,128]{1,0:T(8,128)(2,1)S(1)} %collective-permute-done.6.ixa_ref, bf16[320,128]{1,0:T(8,128)(2,1)S(1)} %collective-permute-done.7.ixb_ref, bf16[320,128]{1,0:T(8,128)(2,1)S(1)} %collective-permute-done.12.iya_ref, ...), custom_call_target="tpu_custom_call" | custom-call | flops 3000000000 | bytes 4000000 | tf_op jit(solution)/shard_map/returning/pallas_call | solution.py:499
  64.9 0.0 collective-permute-done.11
  65.0 1.0 %collective-permute-start.14 = (bf16[432,128]{1,0:T(8,128)(2,1)S(1)}, bf16[432,128]{1,0:T(8,128)(2,1)S(1)}, u32[]{:S(2)}, u32[]{:S(2)}) collective-permute-start(bf16[432,128]{1,0:T(8,128)(2,1)S(1)} %add_convert_fusion.1.own_ref), channel_id=1, source_target_pairs={{0,32},{4,36},{8,40},{12,44},{16,48},{20,52},{24,56},{28,60},{32,0... | collective-permute-start | bytes 331784 | tf_op jit(solution)/shard_map/ppermute | solution.py:381
  66.0 2.5 %backward.7.refs_3_ = f32[256,128]{1,0:T(8,128)S(1)} custom-call(bf16[1024,128]{1,0:T(8,128)(2,1)S(1)} %get-tuple-element.85.grad_ref, s32[27,1024]{1,0:T(8,128)S(1)} %bitcast.59, bf16[27,128,128]{2,1,0:T(8,128)(2,1)S(1)} %bitcast.46), custom_call_target="tpu_custom_call" | custom-call | flops 3000000000 | bytes 2000000 | tf_op jit(solution)/shard_map/backward/pallas_call | solution.py:466
  68.4 0.5 collective-permute-done.14.one_ref
  69.0 0.2 collective-permute-start.16
  69.2 0.0 collective-permute-done.15.refs_7_
  69.2 1.7 %final.1 = (bf16[1024,128]{1,0:T(8,128)(2,1)}, bf16[1024,128]{1,0:T(8,128)(2,1)}) custom-call(f32[256,128]{1,0:T(8,128)S(1)} %backward.4.refs_0_, f32[256,128]{1,0:T(8,128)S(1)} %backward.5.refs_1_, f32[256,128]{1,0:T(8,128)S(1)} %backward.6.refs_2_, f32[256,128]{1,0:T(8,128)S(1)} %backward.7.refs_3_, f32[1152,128]{1,0:T(8,128)S(1)} %returning.1.refs_4_, ...), custom_call_target="tpu_custom_call" | custom-call | flops 1000000000 | bytes 3000000 | tf_op jit(solution)/shard_map/final/pallas_call | solution.py:512
  70.8 3.0 %collective-permute-done.16.two_ref = bf16[2,432,128]{2,1,0:T(8,128)(2,1)S(1)} collective-permute-done((bf16[2,432,128]{2,1,0:T(8,128)(2,1)S(1)}, bf16[2,432,128]{2,1,0:T(8,128)(2,1)S(1)}, u32[]{:S(2)}, u32[]{:S(2)}) %collective-permute-start.16) | collective-permute-done | bytes 221216 | tf_op jit(solution)/shard_map/ppermute | solution.py:381
  73.9 6.1 %collective-permute-start.17 = (bf16[4,432,128]{2,1,0:T(8,128)(2,1)S(1)}, bf16[4,432,128]{2,1,0:T(8,128)(2,1)S(1)}, u32[]{:S(2)}, u32[]{:S(2)}) collective-permute-start(bf16[4,432,128]{2,1,0:T(8,128)(2,1)S(1)} %pad_maximum_fusion), channel_id=1, source_target_pairs={{0,4},{4,0},{8,12},{12,8},{16,20},{20,16},{24,28},{28,24},{32,36},... | collective-permute-start | bytes 1327112 | tf_op jit(solution)/shard_map/ppermute | solution.py:381
  79.9 0.1 pad_add_fusion.1.bits_ref
  80.0 1.3 %collective-permute-done.17.four_ref = bf16[4,432,128]{2,1,0:T(8,128)(2,1)S(1)} collective-permute-done((bf16[4,432,128]{2,1,0:T(8,128)(2,1)S(1)}, bf16[4,432,128]{2,1,0:T(8,128)(2,1)S(1)}, u32[]{:S(2)}, u32[]{:S(2)}) %collective-permute-start.17) | collective-permute-done | bytes 442400 | tf_op jit(solution)/shard_map/ppermute | solution.py:381
  81.4 1.9 %assemble.1 = f32[8,432,128]{2,1,0:T(8,128)} custom-call(s32[3]{0:T(128)S(1)} %pad_add_fusion.1.bits_ref, bf16[432,128]{1,0:T(8,128)(2,1)S(1)} %add_convert_fusion.1.own_ref, bf16[432,128]{1,0:T(8,128)(2,1)S(1)} %collective-permute-done.14.one_ref, bf16[2,432,128]{2,1,0:T(8,128)(2,1)S(1)} %collective-permute-done.16.two_ref, ...), custom_call_target="tpu_custom_call" | custom-call | flops 1000000 | bytes 3000000 | tf_op jit(solution)/shard_map/assemble/pallas_call | solution.py:521
  (18 shorter events, 0.3 us)
Async XLA Ops:
  0.6 26.7 %collective-permute-start.4 = (bf16[1024,128]{1,0:T(8,128)(2,1)}, bf16[1024,128]{1,0:T(8,128)(2,1)S(1)}, u32[]{:S(2)}, u32[]{:S(2)}) collective-permute-start(bf16[1024,128]{1,0:T(8,128)(2,1)} %bitcast.47), channel_id=1, source_target_pairs={{0,1},{1,0},{2,3},{3,2},{4,5},{5,4},{6,7},{7,6},{8,9},{9,8},{10,11... | collective-permute-start | bytes 786440 | tf_op jit(solution)/shard_map/ppermute | solution.py:377
  3.6 1.0 %copy-start.2 = (bf16[1,1024,128]{2,1,0:T(8,128)(2,1)S(1)}, bf16[1,1024,128]{2,1,0:T(8,128)(2,1)}, u32[]{:S(2)}) copy-start(bf16[1,1024,128]{2,1,0:T(8,128)(2,1)} %param.6) | copy-start | bytes 786436
  4.6 0.9 %copy-start.4 = (s32[1152,27]{0,1:T(8,128)S(1)}, s32[1152,27]{0,1:T(8,128)}, u32[]{:S(2)}) copy-start(s32[1152,27]{0,1:T(8,128)} %param.10) | copy-start | bytes 373252
  5.5 4.5 %copy-start = (bf16[1,27,128,128]{3,2,1,0:T(8,128)(2,1)S(1)}, bf16[1,27,128,128]{3,2,1,0:T(8,128)(2,1)}, u32[]{:S(2)}) copy-start(bf16[1,27,128,128]{3,2,1,0:T(8,128)(2,1)} %param.7) | copy-start | bytes 2654212
  5.5 4.5 %copy-start.5 = (s32[1024,27]{0,1:T(8,128)S(1)}, s32[1024,27]{0,1:T(8,128)}, u32[]{:S(2)}) copy-start(s32[1024,27]{0,1:T(8,128)} %param.9) | copy-start | bytes 331780
  7.8 8.3 %collective-permute-start = (bf16[384,128]{1,0:T(8,128)(2,1)S(1)}, bf16[384,128]{1,0:T(8,128)(2,1)S(1)}, u32[]{:S(2)}, u32[]{:S(2)}) collective-permute-start(bf16[384,128]{1,0:T(8,128)(2,1)S(1)} %get-tuple-element.49), channel_id=1, source_target_pairs={{0,4},{4,0},{8,12},{12,8},{16,20},{20,16},{24,28},{28,24},{32,36},... | collective-permute-start | bytes 294920 | tf_op jit(solution)/shard_map/ppermute | solution.py:360
  8.8 7.2 %collective-permute-start.1 = (bf16[384,128]{1,0:T(8,128)(2,1)S(1)}, bf16[384,128]{1,0:T(8,128)(2,1)S(1)}, u32[]{:S(2)}, u32[]{:S(2)}) collective-permute-start(bf16[384,128]{1,0:T(8,128)(2,1)S(1)} %get-tuple-element.52), channel_id=1, source_target_pairs={{0,12},{4,8},{8,4},{12,0},{16,28},{20,24},{24,20},{28,16},{32,44},... | collective-permute-start | bytes 294920 | tf_op jit(solution)/shard_map/ppermute | solution.py:360
  10.0 12.9 %copy-start.3 = (bf16[1,1024,128]{2,1,0:T(8,128)(2,1)S(1)}, bf16[1,1024,128]{2,1,0:T(8,128)(2,1)}, u32[]{:S(2)}) copy-start(bf16[1,1024,128]{2,1,0:T(8,128)(2,1)} %param.6) | copy-start | bytes 786436
  14.4 1.7 %copy-start.6 = (bf16[1664,1024]{1,0:T(8,128)(2,1)}, bf16[1664,1024]{1,0:T(8,128)(2,1)S(1)}, u32[]{:S(2)}) copy-start(bf16[1664,1024]{1,0:T(8,128)(2,1)S(1)} %get-tuple-element.61.g_ref) | copy-start | bytes 10223620
  16.1 11.2 %collective-permute-start.2 = (bf16[384,128]{1,0:T(8,128)(2,1)S(1)}, bf16[384,128]{1,0:T(8,128)(2,1)S(1)}, u32[]{:S(2)}, u32[]{:S(2)}) collective-permute-start(bf16[384,128]{1,0:T(8,128)(2,1)S(1)} %pad_maximum_fusion.2), channel_id=1, source_target_pairs={{0,16},{4,20},{8,24},{12,28},{16,0},{20,4},{24,8},{28,12},{32,48},... | collective-permute-start | bytes 294920 | tf_op jit(solution)/shard_map/ppermute | solution.py:373
  18.6 8.7 %copy-start.1 = (bf16[1,1024,128]{2,1,0:T(8,128)(2,1)S(1)}, bf16[1,1024,128]{2,1,0:T(8,128)(2,1)}, u32[]{:S(2)}) copy-start(bf16[1,1024,128]{2,1,0:T(8,128)(2,1)} %param.8) | copy-start | bytes 786436
  18.6 8.7 %collective-permute-start.3 = (bf16[384,128]{1,0:T(8,128)(2,1)S(1)}, bf16[384,128]{1,0:T(8,128)(2,1)S(1)}, u32[]{:S(2)}, u32[]{:S(2)}) collective-permute-start(bf16[384,128]{1,0:T(8,128)(2,1)S(1)} %pad_maximum_fusion.3), channel_id=1, source_target_pairs={{0,112},{4,116},{8,120},{12,124},{16,32},{20,36},{24,40},{28,44},{... | collective-permute-start | bytes 294920 | tf_op jit(solution)/shard_map/ppermute | solution.py:373
  27.3 6.8 %copy-start.7 = (bf16[1664,1024]{1,0:T(8,128)(2,1)S(1)}, bf16[1664,1024]{1,0:T(8,128)(2,1)}, u32[]{:S(2)}) copy-start(bf16[1664,1024]{1,0:T(8,128)(2,1)} %copy-done.6) | copy-start | bytes 10223620
  37.0 2.8 %collective-permute-start.5 = (bf16[1728,128]{1,0:T(8,128)(2,1)S(1)}, bf16[1728,128]{1,0:T(8,128)(2,1)}, u32[]{:S(2)}, u32[]{:S(2)}) collective-permute-start(bf16[1728,128]{1,0:T(8,128)(2,1)S(1)} %get-tuple-element.64), channel_id=1, source_target_pairs={{0,4},{4,0},{8,12},{12,8},{16,20},{20,16},{24,28},{28,24},{32,36},... | collective-permute-start | bytes 1327112 | tf_op jit(solution)/shard_map/ppermute | solution.py:381
  38.2 2.7 %collective-permute-start.6 = (bf16[320,128]{1,0:T(8,128)(2,1)S(1)}, bf16[320,128]{1,0:T(8,128)(2,1)S(1)}, u32[]{:S(2)}, u32[]{:S(2)}) collective-permute-start(bf16[320,128]{1,0:T(8,128)(2,1)S(1)} %get-tuple-element.65), channel_id=1, source_target_pairs={{0,4},{4,0},{8,12},{12,8},{16,20},{20,16},{24,28},{28,24},{32,36},... | collective-permute-start | bytes 245768 | tf_op jit(solution)/shard_map/ppermute | solution.py:360
  38.4 4.4 %collective-permute-start.7 = (bf16[320,128]{1,0:T(8,128)(2,1)S(1)}, bf16[320,128]{1,0:T(8,128)(2,1)S(1)}, u32[]{:S(2)}, u32[]{:S(2)}) collective-permute-start(bf16[320,128]{1,0:T(8,128)(2,1)S(1)} %get-tuple-element.66), channel_id=1, source_target_pairs={{0,12},{4,8},{8,4},{12,0},{16,28},{20,24},{24,20},{28,16},{32,44},... | collective-permute-start | bytes 245768 | tf_op jit(solution)/shard_map/ppermute | solution.py:360
  42.8 6.6 %collective-permute-start.8 = (bf16[2,432,128]{2,1,0:T(8,128)(2,1)S(1)}, bf16[2,432,128]{2,1,0:T(8,128)(2,1)S(1)}, u32[]{:S(2)}, u32[]{:S(2)}) collective-permute-start(bf16[2,432,128]{2,1,0:T(8,128)(2,1)S(1)} %get-tuple-element.67), channel_id=1, source_target_pairs={{0,8},{4,12},{8,0},{12,4},{16,24},{20,28},{24,16},{28,20},{32,40},... | collective-permute-start | bytes 663560 | tf_op jit(solution)/shard_map/ppermute | solution.py:381
  49.5 4.9 %collective-permute-start.9 = (bf16[432,128]{1,0:T(8,128)(2,1)S(1)}, bf16[432,128]{1,0:T(8,128)(2,1)S(1)}, u32[]{:S(2)}, u32[]{:S(2)}) collective-permute-start(bf16[432,128]{1,0:T(8,128)(2,1)S(1)} %fusion.3), channel_id=1, source_target_pairs={{0,32},{4,36},{8,40},{12,44},{16,48},{20,52},{24,56},{28,60},{32,0... | collective-permute-start | bytes 331784 | tf_op jit(solution)/shard_map/ppermute | solution.py:381
  49.6 12.3 %collective-permute-start.12 = (bf16[320,128]{1,0:T(8,128)(2,1)S(1)}, bf16[320,128]{1,0:T(8,128)(2,1)S(1)}, u32[]{:S(2)}, u32[]{:S(2)}) collective-permute-start(bf16[320,128]{1,0:T(8,128)(2,1)S(1)} %pad_maximum_fusion.4), channel_id=1, source_target_pairs={{0,16},{4,20},{8,24},{12,28},{16,0},{20,4},{24,8},{28,12},{32,48},... | collective-permute-start | bytes 245768 | tf_op jit(solution)/shard_map/ppermute | solution.py:373
  51.6 10.3 %collective-permute-start.13 = (bf16[320,128]{1,0:T(8,128)(2,1)S(1)}, bf16[320,128]{1,0:T(8,128)(2,1)S(1)}, u32[]{:S(2)}, u32[]{:S(2)}) collective-permute-start(bf16[320,128]{1,0:T(8,128)(2,1)S(1)} %pad_maximum_fusion.5), channel_id=1, source_target_pairs={{0,112},{4,116},{8,120},{12,124},{16,32},{20,36},{24,40},{28,44},{... | collective-permute-start | bytes 245768 | tf_op jit(solution)/shard_map/ppermute | solution.py:373
  54.5 5.2 %collective-permute-start.10 = (bf16[432,128]{1,0:T(8,128)(2,1)S(1)}, bf16[432,128]{1,0:T(8,128)(2,1)S(1)}, u32[]{:S(2)}, u32[]{:S(2)}) collective-permute-start(bf16[432,128]{1,0:T(8,128)(2,1)S(1)} %fusion.2), channel_id=1, source_target_pairs={{0,24},{4,28},{8,16},{12,20},{16,8},{20,12},{24,0},{28,4},{32,56},... | collective-permute-start | bytes 331784 | tf_op jit(solution)/shard_map/ppermute | solution.py:381
  57.0 12.1 %collective-permute-start.15 = (bf16[1024,128]{1,0:T(8,128)(2,1)S(1)}, bf16[1024,128]{1,0:T(8,128)(2,1)S(1)}, u32[]{:S(2)}, u32[]{:S(2)}) collective-permute-start(bf16[1024,128]{1,0:T(8,128)(2,1)S(1)} %get-tuple-element.89.refs_6_), channel_id=1, source_target_pairs={{0,1},{1,0},{2,3},{3,2},{4,5},{5,4},{6,7},{7,6},{8,9},{9,8},{10,11... | collective-permute-start | bytes 786440 | tf_op jit(solution)/shard_map/ppermute | solution.py:377
  59.8 5.2 %collective-permute-start.11 = (bf16[432,128]{1,0:T(8,128)(2,1)S(1)}, bf16[432,128]{1,0:T(8,128)(2,1)S(1)}, u32[]{:S(2)}, u32[]{:S(2)}) collective-permute-start(bf16[432,128]{1,0:T(8,128)(2,1)S(1)} %add_convert_fusion.2), channel_id=1, source_target_pairs={{0,96},{4,100},{8,104},{12,108},{16,112},{20,116},{24,120},{28,124... | collective-permute-start | bytes 331784 | tf_op jit(solution)/shard_map/ppermute | solution.py:381
  65.0 3.9 %collective-permute-start.14 = (bf16[432,128]{1,0:T(8,128)(2,1)S(1)}, bf16[432,128]{1,0:T(8,128)(2,1)S(1)}, u32[]{:S(2)}, u32[]{:S(2)}) collective-permute-start(bf16[432,128]{1,0:T(8,128)(2,1)S(1)} %add_convert_fusion.1.own_ref), channel_id=1, source_target_pairs={{0,32},{4,36},{8,40},{12,44},{16,48},{20,52},{24,56},{28,60},{32,0... | collective-permute-start | bytes 331784 | tf_op jit(solution)/shard_map/ppermute | solution.py:381
  69.0 4.9 %collective-permute-start.16 = (bf16[2,432,128]{2,1,0:T(8,128)(2,1)S(1)}, bf16[2,432,128]{2,1,0:T(8,128)(2,1)S(1)}, u32[]{:S(2)}, u32[]{:S(2)}) collective-permute-start(bf16[2,432,128]{2,1,0:T(8,128)(2,1)S(1)} %pad_maximum_fusion.1), channel_id=1, source_target_pairs={{0,8},{4,12},{8,0},{12,4},{16,24},{20,28},{24,16},{28,20},{32,40},... | collective-permute-start | bytes 663560 | tf_op jit(solution)/shard_map/ppermute | solution.py:381
  73.9 7.5 %collective-permute-start.17 = (bf16[4,432,128]{2,1,0:T(8,128)(2,1)S(1)}, bf16[4,432,128]{2,1,0:T(8,128)(2,1)S(1)}, u32[]{:S(2)}, u32[]{:S(2)}) collective-permute-start(bf16[4,432,128]{2,1,0:T(8,128)(2,1)S(1)} %pad_maximum_fusion), channel_id=1, source_target_pairs={{0,4},{4,0},{8,12},{12,8},{16,20},{20,16},{24,28},{28,24},{32,36},... | collective-permute-start | bytes 1327112 | tf_op jit(solution)/shard_map/ppermute | solution.py:381
